TPU v7x, 32 devices: a whole 2x2x4 slice. The times are simulated.
32 devices in a mesh: dp: 8 (over y, x, core), seq: 4 (over z).
Axes of the slice: x: 2, y: 2, z: 4, core: 2. Of those that a mesh axis runs over, the one named last changes fastest.
Arguments:
- inputs: bfloat16 [512, 32, 1024], P('seq', 'dp'), may hold values from -6 to 6
- memory: bfloat16 [512, 32, 1024], P('seq', 'dp'), may hold values from -6 to 6
- compressed: bfloat16 [512, 32, 1024], P('seq', 'dp'), may hold values from -6 to 6
- seg_len: int32 [32], P('dp'), may hold values from 128 to 512, as said below
- gain_first: float32 [1024], replicated, may hold values from 0.5 to 1.5
- shift_first: float32 [1024], replicated, may hold values from -1.75 to 1.75
- w_query: bfloat16 [1024, 1024], replicated, may hold values from -0.1875 to 0.1875
- w_key: bfloat16 [1024, 1024], replicated, may hold values from -0.1875 to 0.1875
- w_value: bfloat16 [1024, 1024], replicated, may hold values from -0.1875 to 0.1875
- w_rel: bfloat16 [1024, 1024], replicated, may hold values from -0.1875 to 0.1875
- bias_content: float32 [1024], replicated, may hold values from -3 to 3
- bias_position: float32 [1024], replicated, may hold values from -3 to 3
- w_out: bfloat16 [1024, 1024], replicated, may hold values from -0.75 to 0.75
- gain_second: float32 [1024], replicated, may hold values from 0.5 to 1.5
- shift_second: float32 [1024], replicated, may hold values from -1.75 to 1.75
- w_up: bfloat16 [1024, 4096], P(None, 'seq'), may hold values from -0.1875 to 0.1875
- bias_up: bfloat16 [4096], P('seq'), may hold values from -3 to 3
- w_down: bfloat16 [4096, 1024], P('seq'), may hold values from -0.09375 to 0.09375
- bias_down: float32 [1024], replicated, may hold values from -1.75 to 1.75
- w_comp: bfloat16 [3, 1024, 1024], P(None, None, 'seq'), may hold values from -0.109375 to 0.109375
- comp_bias: float32 [1024], P('seq'), may hold values from -1.75 to 1.75
- grad_out: bfloat16 [512, 32, 1024], P('seq', 'dp'), may hold values from -6 to 6
- grad_comp: bfloat16 [170, 32, 1024], P(None, 'dp', 'seq'), may hold values from -6 to 6
Outputs:
- output: bfloat16 [512, 32, 1024], P('seq', 'dp')
- grad_inputs: bfloat16 [512, 32, 1024], P('seq', 'dp')
- new_compressed: bfloat16 [170, 32, 1024], P(None, 'dp', 'seq')
- grad_gain_first: float32 [1024], replicated
- grad_shift_first: float32 [1024], replicated
- grad_w_query: float32 [1024, 1024], replicated
- grad_w_key: float32 [1024, 1024], replicated
- grad_w_value: float32 [1024, 1024], replicated
- grad_w_rel: float32 [1024, 1024], replicated
- grad_bias_content: float32 [1024], replicated
- grad_bias_position: float32 [1024], replicated
- grad_w_out: float32 [1024, 1024], replicated
- grad_gain_second: float32 [1024], replicated
- grad_shift_second: float32 [1024], replicated
- grad_w_up: float32 [1024, 4096], P(None, 'seq')
- grad_bias_up: float32 [4096], P('seq')
- grad_w_down: float32 [4096, 1024], P('seq')
- grad_bias_down: float32 [1024], replicated
- grad_w_comp: float32 [3, 1024, 1024], P(None, None, 'seq')
- grad_comp_bias: float32 [1024], P('seq')
Inputs may be any that keep to these rules, and one draw needn't show every extreme that they name: `seg_len`: each stream's true length is a quarter of 512, half of 512 or 512; among the 4 streams of each index of dp at least one has length 512.
All inputs are finite; a program needn't handle non-finite values.
Results may differ from a plain program's by a relative error of at most 0.017.
Values may be sent and summed in bfloat16 or wider, within the bound.
No kernel may reach another device: no remote copies, remote signals or barrier semaphores. Data moves between devices by JAX's collectives and lax.ppermute only.
A program may use at most 320 MiB of HBM per device.

v0:
```python
import math

import jax
import jax.numpy as jnp
from jax import lax
from jax.sharding import PartitionSpec as P

D = 1024
H = 8
DH = 128
MEM = 512
CMEM = 512
RATE = 3


def layer_norm(values, gain, shift):
    center = values - jnp.mean(values, -1, keepdims=True)
    spread = jnp.mean(center * center, -1, keepdims=True)
    return center * lax.rsqrt(spread + 1e-05) * gain + shift


def gelu_tanh(values):
    return jax.nn.gelu(values, approximate=True)


def sinusoids(positions):
    half_width = D // 2
    frequency = jnp.exp(jnp.arange(half_width, dtype=jnp.float32) * (-2.0 * math.log(10000.0) / D))
    angles = positions.astype(jnp.float32)[:, None] * frequency[None, :]
    return (jnp.cos(angles), jnp.sin(angles))


def key_positions(seq_parts, cmem_dev, mem_dev, seg_dev):
    ctx_dev = cmem_dev + mem_dev + seg_dev
    row_ids = jnp.arange(ctx_dev * seq_parts, dtype=jnp.int32)
    device_ids = row_ids // ctx_dev
    local_ids = row_ids % ctx_dev
    in_cmem = device_ids * cmem_dev + local_ids
    in_mem = CMEM + device_ids * mem_dev + (local_ids - cmem_dev)
    in_seg = CMEM + MEM + device_ids * seg_dev + (local_ids - cmem_dev - mem_dev)
    return jnp.where(
        local_ids < cmem_dev, in_cmem, jnp.where(local_ids < cmem_dev + mem_dev, in_mem, in_seg)
    )


def rotate_rows(position_rows, rel_heads, row_sin, row_cos, half_width):
    mixed = jnp.einsum(
        "qshd,fhd->qshf", position_rows, rel_heads, preferred_element_type=jnp.float32
    )
    first_half = mixed[..., :half_width]
    second_half = mixed[..., half_width:]
    return jnp.concatenate(
        [
            first_half * row_sin + second_half * row_cos,
            second_half * row_sin - first_half * row_cos,
        ],
        -1,
    ).astype(jnp.bfloat16)


def on_device(
    inputs,
    memory,
    compressed,
    seg_len,
    gain_first,
    shift_first,
    w_query,
    w_key,
    w_value,
    w_rel,
    bias_content,
    bias_position,
    w_out,
    gain_second,
    shift_second,
    w_up,
    bias_up,
    w_down,
    bias_down,
    w_comp,
    comp_bias,
    grad_out,
    grad_comp,
):
    seq_parts = lax.axis_size("seq")
    my_index = lax.axis_index("seq")
    seg_dev, streams, model_width = inputs.shape
    mem_dev = memory.shape[0]
    cmem_dev = compressed.shape[0]
    split_at = cmem_dev + mem_dev
    ctx_dev = split_at + seg_dev
    total_keys = ctx_dev * seq_parts
    half_width = model_width // 2
    score_scale = 1.0 / math.sqrt(DH)
    key_pos = key_positions(seq_parts, cmem_dev, mem_dev, seg_dev)
    key_cos, key_sin = sinusoids(key_pos)
    pos_table = jnp.concatenate([key_cos, key_sin], -1).astype(jnp.bfloat16)
    query_rows = my_index * seg_dev + jnp.arange(seg_dev, dtype=jnp.int32)
    query_cos, query_sin = sinusoids(CMEM + MEM + query_rows)
    query_cos = query_cos[:, None, None, :]
    query_sin = query_sin[:, None, None, :]
    key_seg = key_pos - (CMEM + MEM)
    visible = (key_seg[None, None, :] < 0) | (
        key_seg[None, None, :] <= query_rows[None, :, None]
    ) & (key_seg[None, None, :] < seg_len[:, None, None])
    x_in = inputs.astype(jnp.float32)
    context = jnp.concatenate([compressed, memory, inputs], 0).astype(jnp.float32)
    normed = layer_norm(context, gain_first, shift_first)
    normed_low = normed.astype(jnp.bfloat16)
    seg_normed = normed_low[split_at:]
    queries = jnp.dot(seg_normed, w_query, preferred_element_type=jnp.float32)
    keys_low = jnp.dot(normed_low, w_key, preferred_element_type=jnp.float32).astype(jnp.bfloat16)
    values_low = jnp.dot(normed_low, w_value, preferred_element_type=jnp.float32).astype(
        jnp.bfloat16
    )
    query_content = (queries + bias_content).astype(jnp.bfloat16).reshape(seg_dev, streams, H, DH)
    query_position = (queries + bias_position).astype(jnp.bfloat16).reshape(seg_dev, streams, H, DH)
    rel_heads = w_rel.reshape(model_width, H, DH)
    rotated = rotate_rows(query_position, rel_heads, query_sin, query_cos, half_width)
    keys_all, values_all, memory_all = (
        lax.all_gather(keys_low, "seq", axis=0, tiled=True),
        lax.all_gather(values_low, "seq", axis=0, tiled=True),
        lax.all_gather(memory, "seq", axis=0, tiled=True),
    )

    def scores_of(keys_gathered):
        content = jnp.einsum(
            "qshd,kshd->shqk",
            query_content,
            keys_gathered.reshape(total_keys, streams, H, DH),
            preferred_element_type=jnp.float32,
        )
        placed = jnp.einsum("qshf,kf->shqk", rotated, pos_table, preferred_element_type=jnp.float32)
        return jnp.where(visible[:, None], (content + placed) * score_scale, -1e30)

    scores = scores_of(keys_all)
    row_max = jnp.max(scores, -1, keepdims=True)
    exp_scores = jnp.exp(scores - row_max)
    row_total = jnp.sum(exp_scores, -1, keepdims=True)
    attn_prob = (exp_scores / row_total).astype(jnp.bfloat16)
    log_total = row_max + jnp.log(row_total)
    attended = jnp.einsum(
        "shqk,kshd->qshd",
        attn_prob,
        values_all.reshape(total_keys, streams, H, DH),
        preferred_element_type=jnp.float32,
    )
    attn_out = attended.reshape(seg_dev, streams, model_width).astype(jnp.bfloat16)
    hidden = x_in + jnp.dot(attn_out, w_out, preferred_element_type=jnp.float32)
    normed_two = layer_norm(hidden, gain_second, shift_second).astype(jnp.bfloat16)
    normed_all = lax.all_gather(normed_two, "seq", axis=0, tiled=True)
    pre_act = jnp.dot(normed_all, w_up, preferred_element_type=jnp.float32) + bias_up.astype(
        jnp.float32
    )
    activated = gelu_tanh(pre_act).astype(jnp.bfloat16)
    row_piece = activated
    ffn_result = lax.psum_scatter(
        jnp.dot(row_piece, w_down, preferred_element_type=jnp.float32).astype(jnp.bfloat16),
        "seq",
        scatter_dimension=0,
        tiled=True,
    ).astype(jnp.float32)
    output = (hidden + ffn_result + bias_down).astype(jnp.bfloat16)
    grad_all = lax.all_gather(grad_out, "seq", axis=0, tiled=True)
    d_activated = jnp.einsum("rsd,fd->rsf", grad_all, w_down, preferred_element_type=jnp.float32)
    _, gelu_back = jax.vjp(gelu_tanh, pre_act)
    d_pre = gelu_back(d_activated)[0].astype(jnp.bfloat16)
    grad_w_down = jnp.einsum("rsf,rsd->fd", activated, grad_all, preferred_element_type=jnp.float32)
    grad_w_up = jnp.einsum("rsd,rsf->df", normed_all, d_pre, preferred_element_type=jnp.float32)
    grad_bias_up = jnp.sum(d_pre.astype(jnp.float32), (0, 1))
    row_piece = d_pre
    d_normed_two = lax.psum_scatter(
        jnp.einsum("rsf,df->rsd", row_piece, w_up, preferred_element_type=jnp.float32).astype(
            jnp.bfloat16
        ),
        "seq",
        scatter_dimension=0,
        tiled=True,
    ).astype(jnp.float32)
    _, norm_two_back = jax.vjp(layer_norm, hidden, gain_second, shift_second)
    d_hidden_ffn, grad_gain_second, grad_shift_second = norm_two_back(d_normed_two)
    grad_rows_f = grad_out.astype(jnp.float32)
    d_hidden = grad_rows_f + d_hidden_ffn
    grad_bias_down = jnp.sum(grad_rows_f, (0, 1))
    d_branch = d_hidden.astype(jnp.bfloat16)
    grad_w_out = jnp.einsum("rsd,rse->de", attn_out, d_branch, preferred_element_type=jnp.float32)
    d_attn = (
        jnp.einsum("rse,de->rsd", d_branch, w_out, preferred_element_type=jnp.float32)
        .astype(jnp.bfloat16)
        .reshape(seg_dev, streams, H, DH)
    )
    keys_back, values_back = (
        lax.all_gather(keys_low, "seq", axis=0, tiled=True),
        lax.all_gather(values_low, "seq", axis=0, tiled=True),
    )
    keys_heads = keys_back.reshape(total_keys, streams, H, DH)
    values_heads = values_back.reshape(total_keys, streams, H, DH)
    prob_full = jnp.exp(scores_of(keys_back) - log_total)
    prob_low = prob_full.astype(jnp.bfloat16)
    d_prob = jnp.einsum("qshd,kshd->shqk", d_attn, values_heads, preferred_element_type=jnp.float32)
    inner_sum = jnp.sum(d_prob * prob_full, -1, keepdims=True)
    d_scores = (prob_full * (d_prob - inner_sum)).astype(jnp.bfloat16)
    key_part = (
        jnp.einsum("shqk,qshd->kshd", d_scores, query_content, preferred_element_type=jnp.float32)
        * score_scale
    )
    value_part = jnp.einsum("shqk,qshd->kshd", prob_low, d_attn, preferred_element_type=jnp.float32)
    key_sums = lax.psum_scatter(
        jnp.concatenate(
            [
                key_part.reshape(ctx_dev * lax.axis_size("seq"), streams, model_width),
                value_part.reshape(ctx_dev * lax.axis_size("seq"), streams, model_width),
            ],
            -1,
        ).astype(jnp.bfloat16),
        "seq",
        scatter_dimension=0,
        tiled=True,
    ).astype(jnp.float32)
    d_keys = key_sums[..., :model_width].astype(jnp.bfloat16)
    d_values = key_sums[..., model_width:].astype(jnp.bfloat16)
    d_content = (
        jnp.einsum("shqk,kshd->qshd", d_scores, keys_heads, preferred_element_type=jnp.float32)
        * score_scale
    )
    d_rotated = (
        jnp.einsum("shqk,kf->qshf", d_scores, pos_table, preferred_element_type=jnp.float32)
        * score_scale
    )
    lead_part = d_rotated[..., :half_width]
    tail_part = d_rotated[..., half_width:]
    d_mixed = jnp.concatenate(
        [
            lead_part * query_sin - tail_part * query_cos,
            lead_part * query_cos + tail_part * query_sin,
        ],
        -1,
    ).astype(jnp.bfloat16)
    d_query_pos = jnp.einsum(
        "qshf,fhd->qshd", d_mixed, rel_heads, preferred_element_type=jnp.float32
    )
    grad_w_rel = jnp.einsum(
        "qshf,qshd->fhd", d_mixed, query_position, preferred_element_type=jnp.float32
    ).reshape(model_width, model_width)
    grad_bias_content = jnp.sum(d_content, (0, 1)).reshape(model_width)
    grad_bias_position = jnp.sum(d_query_pos, (0, 1)).reshape(model_width)
    d_queries = (
        (d_content + d_query_pos).reshape(seg_dev, streams, model_width).astype(jnp.bfloat16)
    )
    grad_w_query = jnp.einsum(
        "rsd,rse->de", seg_normed, d_queries, preferred_element_type=jnp.float32
    )
    grad_w_key = jnp.einsum("rsd,rse->de", normed_low, d_keys, preferred_element_type=jnp.float32)
    grad_w_value = jnp.einsum(
        "rsd,rse->de", normed_low, d_values, preferred_element_type=jnp.float32
    )
    d_from_kv = jnp.einsum(
        "rse,de->rsd", d_keys, w_key, preferred_element_type=jnp.float32
    ) + jnp.einsum("rse,de->rsd", d_values, w_value, preferred_element_type=jnp.float32)
    d_from_query = jnp.einsum("rse,de->rsd", d_queries, w_query, preferred_element_type=jnp.float32)
    d_normed = jnp.concatenate([d_from_kv[:split_at], d_from_kv[split_at:] + d_from_query], 0)
    _, norm_one_back = jax.vjp(layer_norm, context, gain_first, shift_first)
    d_context, grad_gain_first, grad_shift_first = norm_one_back(d_normed)
    grad_inputs = (d_hidden + d_context[split_at:]).astype(jnp.bfloat16)
    new_rows = memory_all.shape[0] // RATE
    windows = memory_all[: new_rows * RATE].reshape(new_rows, RATE, streams, model_width)
    new_compressed = (
        jnp.einsum("rtsd,tde->rse", windows, w_comp, preferred_element_type=jnp.float32) + comp_bias
    ).astype(jnp.bfloat16)
    grad_w_comp = jnp.einsum(
        "rtsd,rse->tde", windows, grad_comp, preferred_element_type=jnp.float32
    )
    grad_comp_bias = jnp.sum(grad_comp.astype(jnp.float32), (0, 1))
    (
        grad_w_query,
        grad_w_key,
        grad_w_value,
        grad_w_rel,
        grad_w_out,
        grad_bias_content,
        grad_bias_position,
        grad_gain_first,
        grad_shift_first,
        grad_gain_second,
        grad_shift_second,
        grad_bias_down,
    ) = lax.psum(
        (
            grad_w_query,
            grad_w_key,
            grad_w_value,
            grad_w_rel,
            grad_w_out,
            grad_bias_content,
            grad_bias_position,
            grad_gain_first,
            grad_shift_first,
            grad_gain_second,
            grad_shift_second,
            grad_bias_down,
        ),
        ("dp", "seq"),
    )
    grad_w_up, grad_bias_up, grad_w_down, grad_w_comp, grad_comp_bias = (
        lax.psum(grad_w_up.astype(jnp.bfloat16), "dp").astype(jnp.float32),
        lax.psum(grad_bias_up.astype(jnp.bfloat16), "dp").astype(jnp.float32),
        lax.psum(grad_w_down.astype(jnp.bfloat16), "dp").astype(jnp.float32),
        lax.psum(grad_w_comp.astype(jnp.bfloat16), "dp").astype(jnp.float32),
        lax.psum(grad_comp_bias.astype(jnp.bfloat16), "dp").astype(jnp.float32),
    )
    return (
        output,
        grad_inputs,
        new_compressed,
        grad_gain_first,
        grad_shift_first,
        grad_w_query,
        grad_w_key,
        grad_w_value,
        grad_w_rel,
        grad_bias_content,
        grad_bias_position,
        grad_w_out,
        grad_gain_second,
        grad_shift_second,
        grad_w_up,
        grad_bias_up,
        grad_w_down,
        grad_bias_down,
        grad_w_comp,
        grad_comp_bias,
    )


def solution(mesh):
    in_specs = (
        P("seq", "dp", None),
        P("seq", "dp", None),
        P("seq", "dp", None),
        P("dp"),
        P(),
        P(),
        P(),
        P(),
        P(),
        P(),
        P(),
        P(),
        P(),
        P(),
        P(),
        P(None, "seq"),
        P("seq"),
        P("seq", None),
        P(),
        P(None, None, "seq"),
        P("seq"),
        P("seq", "dp", None),
        P(None, "dp", "seq"),
    )
    out_specs = (
        P("seq", "dp", None),
        P("seq", "dp", None),
        P(None, "dp", "seq"),
        P(),
        P(),
        P(),
        P(),
        P(),
        P(),
        P(),
        P(),
        P(),
        P(),
        P(),
        P(None, "seq"),
        P("seq"),
        P("seq", None),
        P(),
        P(None, None, "seq"),
        P("seq"),
    )
    return jax.shard_map(
        on_device, mesh=mesh, in_specs=in_specs, out_specs=out_specs, check_vma=False
    )
```

profile of v0, /device:TPU:0, one launch (start us, length us, event | category | flops | bytes accessed | tf_op | source)
XLA Modules:
  0.0 1845.3 jit_solution(12783544380849261424)
XLA Ops:
  17.3 4.7 convolution_convert_fusion.3
  22.1 7.6 convolution_convert_fusion.4
  30.0 4.5 add_convert_fusion.5
  44.4 13.0 fusion.42
  59.8 4.7 add_convert_fusion.1
  64.6 21.7 %fusion.25 = f32[1536,128,4,8]{0,1,3,2:T(8,128)} fusion(bf16[1536,512]{1,0:T(8,128)(2,1)} %get-tuple-element.121, bf16[1536,512]{1,0:T(8,128)(2,1)} %get-tuple-element.120, bf16[128,4,8,512]{3,0,1,2:T(8,128)(2,1)} %get-tuple-element.108, bf16[128,4,8,512]{3,0,1,2:T(8,128)(2,1)} %get-tuple-element.107), kind=kOutput, calls=%fused_computation.38 | convolution fusion | flops 12907970560 | bytes 36700160 | tf_op jit(solution)/shard_map/qshf,kf->shqk/dot_general | solution.py:134
  86.3 156.8 %all-gather.8.cloned.1.call-done = bf16[1536,4,1024]{2,0,1:T(8,128)(2,1)} async-done(((bf16[384,4,1024]{2,0,1:T(8,128)(2,1)}), bf16[1536,4,1024]{2,0,1:T(8,128)(2,1)}) %all-gather.8.cloned.1.call-update) | async-done | bytes 12582928 | tf_op jit(solution)/shard_map/all_gather | solution.py:122
  243.1 17.0 copy.186
  260.0 23.8 %fusion.147 = (f32[4,8,128]{2,1,0:T(8,128)S(1)}, f32[4,8,128,1536]{3,2,1,0:T(8,128)}) fusion(f32[1536,128,4,8]{0,1,3,2:T(8,128)} %fusion.25, bf16[128,4,8,128]{0,3,2,1:T(8,128)(2,1)S(1)} %bitcast.191, bf16[1536,4,8,128]{0,3,2,1:T(8,128)(2,1)} %bitcast.185, pred[4,128,1536]{2,1,0:T(8,128)(4,1)} %and_or_fusion), kind=kOutput, calls=%fused_computation.194 | convolution fusion | flops 1635774464 | bytes 64765952 | tf_op jit(solution)/shard_map/qshd,kshd->shqk/dot_general | solution.py:128
  283.8 11.2 fusion.2
  295.0 166.6 %all-gather.6.cloned.1.call-done = bf16[1536,4,1024]{2,0,1:T(8,128)(2,1)} async-done(((bf16[384,4,1024]{2,0,1:T(8,128)(2,1)}), bf16[1536,4,1024]{2,0,1:T(8,128)(2,1)}) %all-gather.6.cloned.1.call-update) | async-done | bytes 12582928 | tf_op jit(solution)/shard_map/all_gather | solution.py:123
  461.7 15.2 fusion.99
  484.0 76.5 %all-gather.10.cloned.1.call-done = bf16[512,4,1024]{2,0,1:T(8,128)(2,1)} async-done(((bf16[128,4,1024]{2,0,1:T(8,128)(2,1)}), bf16[512,4,1024]{2,0,1:T(8,128)(2,1)}) %all-gather.10.cloned.1.call-update) | async-done | bytes 4194320 | tf_op jit(solution)/shard_map/all_gather | solution.py:152
  560.5 10.9 fusion.74
  571.4 70.4 %all-gather.12.cloned.1.call-done = bf16[512,4,1024]{2,0,1:T(8,128)(2,1)} async-done(((bf16[128,4,1024]{2,0,1:T(8,128)(2,1)}), bf16[512,4,1024]{2,0,1:T(8,128)(2,1)}) %all-gather.12.cloned.1.call-update) | async-done | bytes 4194320 | tf_op jit(solution)/shard_map/all_gather | solution.py:165
  641.8 13.4 fusion.150
  657.2 6.2 convolution_convert_fusion.1
  664.5 74.4 %reduce-scatter.6.cloned.1.call-done = bf16[128,4,1024]{2,0,1:T(8,128)(2,1)} async-done(((bf16[512,4,1024]{2,0,1:T(8,128)(2,1)}), bf16[128,4,1024]{2,0,1:T(8,128)(2,1)}) %reduce-scatter.6.cloned.1.call-update) | async-done | bytes 1048592 | tf_op jit(solution)/shard_map/reduce_scatter | solution.py:173
  752.5 14.6 convolution_convert_fusion
  767.1 16.7 copy.141
  783.8 24.3 %multiply_reduce_fusion = (f32[4,8,128]{2,1,0:T(8,128)S(1)}, f32[4,8,128,1536]{3,2,1,0:T(8,128)}) fusion(f32[4,8,128,1536]{3,2,1,0:T(8,128)} %get-tuple-element.125, f32[4,8,128]{2,1,0:T(8,128)S(1)} %log_add_fusion, bf16[128,4,8,128]{0,3,2,1:T(8,128)(2,1)} %bitcast.194, bf16[1536,4,1024]{2,0,1:T(8,128)(2,1)} %all-gather.6.cloned.1.call-done), kind=kOutput, calls=%fused_computation.6 | convolution fusion | flops 1629483008 | bytes 63995904 | tf_op jit(solution)/shard_map/qshd,kshd->shqk/dot_general | solution.py:201
  808.1 21.7 %multiply_convert_fusion.1 = bf16[4,8,128,1536]{3,2,1,0:T(8,128)(2,1)} fusion(f32[4,8,128,1536]{3,2,1,0:T(8,128)} %get-tuple-element.129, f32[4,8,128,1536]{3,2,1,0:T(8,128)} %get-tuple-element.125, f32[4,8,128]{2,1,0:T(8,128)S(1)} %get-tuple-element.128, f32[4,8,128]{2,1,0:T(8,128)S(1)} %log_add_fusion), kind=kLoop, calls=%fused_computation.5 | loop fusion | flops 25165824 | bytes 62947328 | tf_op jit(solution)/shard_map/convert_element_type | solution.py:203
  829.8 12.5 multiply_convert_fusion
  842.3 16.6 copy.140
  859.0 20.6 %pad_maximum_fusion = bf16[1536,4,2048]{2,0,1:T(8,128)(2,1)} fusion(bf16[1536,4,1024]{2,0,1:T(8,128)(2,1)} %copy.141, bf16[1536,4,1024]{2,0,1:T(8,128)(2,1)} %copy.140), kind=kLoop, calls=%fused_computation | loop fusion | flops 50331648 | bytes 50331648 | tf_op jit(solution)/shard_map/concatenate | solution.py:210
  883.6 4.2 bitcast_convert_fusion.2
  889.7 5.8 bitcast_convert_fusion.1
  895.5 6.2 bitcast_convert_fusion
  901.8 4.1 copy.145
  906.0 11.3 convolution_convert_fusion.2
  917.6 20.3 %multiply_bitcast_fusion = f32[128,4,8,1024]{3,0,1,2:T(8,128)} fusion(bf16[4,8,128,1536]{3,2,1,0:T(8,128)(2,1)} %multiply_convert_fusion.1, bf16[1536,512]{1,0:T(8,128)(2,1)} %get-tuple-element.121, bf16[1536,512]{1,0:T(8,128)(2,1)} %get-tuple-element.120), kind=kOutput, calls=%fused_computation.12 | convolution fusion | flops 12895387648 | bytes 32505856 | tf_op jit(solution)/shard_map/shqk,kf->qshf/dot_general | solution.py:228
  937.9 7.5 subtract_convert_fusion
  950.0 5.4 copy.154
  955.5 4.6 convolution_bitcast_fusion.1
  960.0 11.8 fusion.151
  971.9 5.5 bitcast_reduce_fusion
  981.7 312.9 %reduce-scatter.8.cloned.1.call-done = bf16[384,4,2048]{2,0,1:T(8,128)(2,1)} async-done(((bf16[1536,4,2048]{2,0,1:T(8,128)(2,1)}), bf16[384,4,2048]{2,0,1:T(8,128)(2,1)}) %reduce-scatter.8.cloned.1.call-update) | async-done | bytes 6291472 | tf_op jit(solution)/shard_map/reduce_scatter | solution.py:209
  1294.6 8.5 fusion.59
  1303.1 5.0 fusion.62
  1308.8 5.1 fusion.113
  1314.8 14.8 all-reduce.2
  1330.8 68.3 %all-reduce.9.cloned.1.call-done = (bf16[1024,1024]{1,0:T(8,128)(2,1)}, bf16[1024,1024]{1,0:T(8,128)(2,1)}, bf16[3,1024,256]{2,1,0:T(8,128)(2,1)}) async-done(((bf16[1024,1024]{1,0:T(8,128)(2,1)}, bf16[1024,1024]{1,0:T(8,128)(2,1)}, bf16[3,1024,256]{2,1,0:T(8,128)(2,1)}), (bf16[1024,1024]{1,0:T(8,128)(2,1)}, bf16[1024,1024]{1,0:T(8,128)(2,1)}, bf16[3,1024,256]{2,1,0:T(8,128)(2,1)})) %all-reduce.9.cloned.1.call-update) | async-done | bytes 5767184 | tf_op jit(solution)/shard_map/psum | solution.py:306
  1399.1 4.2 convert_element_type.170
  1421.8 4.0 fusion.146
  1425.8 53.1 %reduce-scatter.4.cloned.1.call-done = bf16[128,4,1024]{2,0,1:T(8,128)(2,1)} async-done(((bf16[512,4,1024]{2,0,1:T(8,128)(2,1)}), bf16[128,4,1024]{2,0,1:T(8,128)(2,1)}) %reduce-scatter.4.cloned.1.call-update) | async-done | bytes 1048592 | tf_op jit(solution)/shard_map/reduce_scatter | solution.py:158
  1486.3 43.7 %all-reduce = (f32[1024]{0:T(1024)}, f32[1024]{0:T(1024)}, f32[1024]{0:T(1024)}, f32[1024]{0:T(1024)}, f32[1024]{0:T(1024)}, /*index=5*/f32[1024]{0:T(1024)}, f32[1024]{0:T(1024)}) all-reduce(f32[1024]{0:T(1024)S(1)} %get-tuple-element.80, f32[1024]{0:T(1024)S(1)} %reduce_sum.212, ...), channel_id=1, replica_groups=mesh['dp'=8,'seq'=4] {'dp','seq'}, use_global_device_ids=true, to_apply=%region_15.16 | all-reduce | flops 7168 | bytes 57344 | tf_op jit(solution)/shard_map/psum | solution.py:288
  1530.0 290.1 %all-reduce.7.cloned.1.call-done = (f32[1024,1024]{1,0:T(8,128)}, f32[1024,1024]{1,0:T(8,128)}, f32[1024,1024]{1,0:T(8,128)}, f32[1024,1024]{1,0:T(8,128)}, f32[1024,1024]{1,0:T(8,128)}) async-done(((f32[1024,1024]{1,0:T(8,128)}, f32[1024,1024]{1,0:T(8,128)}, f32[1024,1024]{1,0:T(8,128)}, f32[1024,1024]{1,0:T(8,128)}, f32[1024,1024]{1,0:T(8,128)}), (f32[1024,1024]{1,0:T(8,128)}, f32[1024,1024]{1,0:T(8,128)}, ...) | async-done | bytes 20971536 | tf_op jit(solution)/shard_map/psum | solution.py:288
  1820.1 4.9 copy.243
  (261 shorter events, 102.6 us)
Async XLA Ops:
  7.2 634.6 %copy-start = (bf16[1024,1024]{1,0:T(8,128)(2,1)S(1)}, bf16[1024,1024]{1,0:T(8,128)(2,1)}, u32[]{:S(2)}) copy-start(bf16[1024,1024]{1,0:T(8,128)(2,1)} %param.40) | copy-start | bytes 6291460
  7.2 235.9 %all-gather.8.cloned.1.call-start = ((), (), s32[]{:S(2)}) async-start(), calls=%async_computation.4 | async-start | bytes 15728640 | tf_op jit(solution)/shard_map/all_gather | solution.py:122
  22.0 8.0 copy-start.77
  22.0 8.0 copy-start.78
  22.0 439.6 %all-gather.6.cloned.1.call-start = ((), (), s32[]{:S(2)}) async-start(), calls=%async_computation.3 | async-start | bytes 15728640 | tf_op jit(solution)/shard_map/all_gather | solution.py:123
  29.8 530.7 %all-gather.10.cloned.1.call-start = ((), (), s32[]{:S(2)}) async-start(), calls=%async_computation.5 | async-start | bytes 5242880 | tf_op jit(solution)/shard_map/all_gather | solution.py:152
  34.9 7.9 copy-start.68
  41.7 15.7 copy-start.9
  41.7 15.7 copy-start.17
  42.8 17.0 copy-start.28
  42.8 17.0 copy-start.30
  461.6 15.2 copy-start.23
  461.7 15.2 copy-start.33
  478.6 266.7 %copy-start.46 = (f32[128,4]{0,1:T(4,128)}, f32[128,4]{0,1:T(4,128)S(1)}, u32[]{:S(2)}) copy-start(f32[128,4]{0,1:T(4,128)S(1)} %broadcast_multiply_fusion.1) | copy-start | bytes 6148
  480.0 265.4 %copy-start.52 = (f32[128,4]{0,1:T(4,128)}, f32[128,4]{0,1:T(4,128)S(1)}, u32[]{:S(2)}) copy-start(f32[128,4]{0,1:T(4,128)S(1)} %fusion.141) | copy-start | bytes 6148
  481.4 160.4 %all-gather.12.cloned.1.call-start = ((), (), s32[]{:S(2)}) async-start(), calls=%async_computation.7 | async-start | bytes 5242880 | tf_op jit(solution)/shard_map/all_gather | solution.py:165
  483.9 254.9 %reduce-scatter.6.cloned.1.call-start = ((), (), s32[]{:S(2)}) async-start(), calls=%async_computation.8 | async-start | bytes 5242880 | tf_op jit(solution)/shard_map/reduce_scatter | solution.py:173
  641.8 15.4 copy-start.72
  663.4 216.5 %all-gather.14.cloned.1.call-start = ((), (), s32[]{:S(2)}) async-start(), calls=%async_computation.10 | async-start | bytes 5242880 | tf_op jit(solution)/shard_map/all_gather | solution.py:124
  664.0 630.6 %reduce-scatter.8.cloned.1.call-start = ((), (), s32[]{:S(2)}) async-start(), calls=%async_computation.9 | async-start | bytes 31457280 | tf_op jit(solution)/shard_map/reduce_scatter | solution.py:209
  738.9 6.5 copy-start.10
  738.9 6.5 copy-start.12
  742.2 5.7 copy-start.34
  879.6 519.5 %all-reduce.9.cloned.1.call-start = ((), (), s32[]{:S(2)}) async-start(), calls=%async_computation.12 | async-start | bytes 11534336 | tf_op jit(solution)/shard_map/psum | solution.py:306
  883.5 6.1 copy-start.83
  883.6 11.9 slice-start.2
  889.7 5.8 copy-start.71
  889.7 5.8 slice-start.3
  901.8 577.2 %reduce-scatter.4.cloned.1.call-start = ((), (), s32[]{:S(2)}) async-start(), calls=%async_computation.6 | async-start | bytes 5242880 | tf_op jit(solution)/shard_map/reduce_scatter | solution.py:158
  917.3 20.6 %copy-start.29 = (f32[128,512]{1,0:T(8,128)S(1)}, f32[128,512]{1,0:T(8,128)}, u32[]{:S(2)}) copy-start(f32[128,512]{1,0:T(8,128)} %copy-done.28) | copy-start | bytes 786436
  917.3 20.6 %copy-start.31 = (f32[128,512]{1,0:T(8,128)S(1)}, f32[128,512]{1,0:T(8,128)}, u32[]{:S(2)}) copy-start(f32[128,512]{1,0:T(8,128)} %copy-done.30) | copy-start | bytes 786436
  917.3 902.8 %all-reduce.7.cloned.1.call-start = ((), (), s32[]{:S(2)}) async-start(), calls=%async_computation.11 | async-start | bytes 41943040 | tf_op jit(solution)/shard_map/psum | solution.py:288
  937.9 7.5 copy-start.18
  960.0 11.9 copy-start.14
  960.0 11.9 copy-start.16
  960.0 11.9 copy-start.35
  971.9 6.5 copy-start.26
  1294.6 8.5 copy-start.27
  1294.6 8.5 copy-start.69
  1308.8 6.0 copy-start.67
  1399.1 8.9 slice-start
  1421.7 57.3 %copy-start.11 = (bf16[128,4,1024]{2,0,1:T(8,128)(2,1)S(1)}, bf16[128,4,1024]{2,0,1:T(8,128)(2,1)}, u32[]{:S(2)}) copy-start(bf16[128,4,1024]{2,0,1:T(8,128)(2,1)} %reduce-scatter.6.cloned.1.call-done) | copy-start | bytes 3145732
  1421.7 57.3 %copy-start.45 = (f32[1024]{0:T(1024)S(1)}, f32[1024]{0:T(1024)}, u32[]{:S(2)}) copy-start(f32[1024]{0:T(1024)} %param.36) | copy-start | bytes 12292
  1421.7 57.2 %copy-start.47 = (f32[128,4]{0,1:T(4,128)S(1)}, f32[128,4]{0,1:T(4,128)}, u32[]{:S(2)}) copy-start(f32[128,4]{0,1:T(4,128)} %copy-done.46) | copy-start | bytes 6148
  1421.7 57.2 %copy-start.53 = (f32[128,4]{0,1:T(4,128)S(1)}, f32[128,4]{0,1:T(4,128)}, u32[]{:S(2)}) copy-start(f32[128,4]{0,1:T(4,128)} %copy-done.52) | copy-start | bytes 6148
  1421.7 57.2 %copy-start.57 = (f32[128,4]{0,1:T(4,128)S(1)}, f32[128,4]{0,1:T(4,128)}, u32[]{:S(2)}) copy-start(f32[128,4]{0,1:T(4,128)} %copy-done.56) | copy-start | bytes 6148
  1421.8 57.2 %copy-start.59 = (f32[128,4]{0,1:T(4,128)S(1)}, f32[128,4]{0,1:T(4,128)}, u32[]{:S(2)}) copy-start(f32[128,4]{0,1:T(4,128)} %copy-done.58) | copy-start | bytes 6148
  1421.8 57.2 %copy-start.64 = (f32[1024]{0:T(1024)S(1)}, f32[1024]{0:T(1024)}, u32[]{:S(2)}) copy-start(f32[1024]{0:T(1024)} %param.41) | copy-start | bytes 12292
  (50 other events, 151.9 us)
Sparse Core Ops, SparseCore 0:
  22.1 220.8 all-gather.7
  245.2 216.3 all-gather.5
  481.5 78.9 all-gather.9
  562.5 79.2 all-gather.11
  663.5 75.2 reduce-scatter.5
  740.4 81.2 all-gather.13
  879.8 414.8 reduce-scatter.7
  1298.3 100.8 all-reduce.8
  1402.1 76.8 reduce-scatter.3
  1486.4 333.7 all-reduce.6
where the time goes:
time: 1850 us
  waiting for transfers between devices  1270 us (69%)
  matrix products  269 us (15%)
  local copies, waits for them, and re-layouts  116 us (6%)
  other arithmetic  115 us (6%)
  blocking collectives  58.5 us (3%)
    reduce_scatter x1, waiting for transfers between devices, on_device(): lax.psum_scatter(jnp.concatenate([key_part.reshape(ctx_dev * lax.axis_siz...  313 us
    psum x1, waiting for transfers between devices, on_device(): lax.psum((grad_w_query, grad_w_key, grad_w_value, grad_w_rel, grad_w_out,...  290 us
    all_gather x1, waiting for transfers between devices, on_device(): lax.all_gather(values_low, 'seq', axis=0, tiled=True)  167 us
    all_gather x1, waiting for transfers between devices, on_device(): lax.all_gather(keys_low, 'seq', axis=0, tiled=True)  157 us
    all_gather x1, waiting for transfers between devices, on_device(): normed_all = lax.all_gather(normed_two, 'seq', axis=0, tiled=True)  76.5 us
    reduce_scatter x1, waiting for transfers between devices, on_device(): lax.psum_scatter(jnp.einsum('rsf,df->rsd', row_piece, w_up, preferred_ele...  74.4 us
    all_gather x1, waiting for transfers between devices, on_device(): grad_all = lax.all_gather(grad_out, 'seq', axis=0, tiled=True)  70.4 us
    psum x1, waiting for transfers between devices, on_device(): lax.psum(grad_w_up.astype(jnp.bfloat16), 'dp').astype(jnp.float32)  68.3 us
  transfers between devices with their start and end apart: 10, of which 9 were waited for; matrix products, arithmetic and copies ran while one was open for 23% of the time, Pallas kernels for 0%

commit v1 on v0

--- a/solution.py
+++ b/solution.py
@@ -1,8 +1,11 @@
+import functools
 import math
 
 import jax
 import jax.numpy as jnp
 from jax import lax
+from jax.experimental import pallas as pl
+from jax.experimental.pallas import tpu as pltpu
 from jax.sharding import PartitionSpec as P
 
 D = 1024
@@ -58,7 +61,7 @@
     ).astype(jnp.bfloat16)
 
 
-def on_device(
+def split_rows_plan(
     inputs,
     memory,
     compressed,
@@ -333,6 +336,990 @@
     )
 
 
+BF16 = jnp.bfloat16
+F32 = jnp.float32
+QUERY_BLOCK = 256
+HEADS_A_CALL = 2
+VMEM_LIMIT = 48 * 1024 * 1024
+SHORT = pl.CostEstimate(flops=1024, bytes_accessed=1024, transcendentals=0)
+
+
+def contract(left, right, left_dim, right_dim):
+    return lax.dot_general(
+        left, right, (((left_dim,), (right_dim,)), ((), ())), preferred_element_type=F32
+    )
+
+
+def bit_of(axis, distance):
+    return (lax.axis_index(axis) // distance) % 2
+
+
+def swap(rows, axis, distance):
+    count = lax.axis_size(axis)
+    return lax.ppermute(rows, axis, [(i, i ^ distance) for i in range(count)])
+
+
+def after(value, *others):
+    return lax.optimization_barrier((value, *others))[0]
+
+
+def pick(rows, which, dim):
+    return lax.dynamic_index_in_dim(rows, which, dim, keepdims=False)
+
+
+def halve(rows, step, dim=0):
+    bit = bit_of(*step)
+    got = swap(pick(rows, 1 - bit, dim).astype(BF16), *step)
+    return pick(rows, bit, dim).astype(F32) + got.astype(F32)
+
+
+def double(rows, step, dim=0):
+    got = swap(rows, *step)
+    second = bit_of(*step) == 1
+    return jnp.stack([jnp.where(second, got, rows), jnp.where(second, rows, got)], dim)
+
+
+def bits_below(count):
+    return [1 << i for i in range(count.bit_length() - 1)]
+
+
+def token(value):
+    return (value[(0,) * value.ndim].astype(F32) * 0.0).astype(jnp.int32)
+
+
+def to_streams(rows, count, order=0):
+    me = lax.axis_index("seq")
+    block = rows.shape[1]
+    whole = jnp.zeros((count * block, rows.shape[2]), rows.dtype)
+    for shift in range(count):
+        part = pick(rows, (me + shift) % count + order, 0)
+        if shift:
+            part = lax.ppermute(part, "seq", [(i, (i + shift) % count) for i in range(count)])
+        whole = lax.dynamic_update_slice_in_dim(whole, part, (me - shift) % count * block, 0)
+    return whole
+
+
+def by_stream(rows):
+    return jnp.swapaxes(rows, 0, 1)
+
+
+def attend_kernel(
+    len_ref, qc_ref, qp_ref, k_ref, v_ref, rel_ref, table_ref, cos_ref, sin_ref, *rest
+):
+    p_ref, o_ref = rest[-2:]
+    rows = qc_ref.shape[0]
+    keys = k_ref.shape[0]
+    half = cos_ref.shape[1]
+    split = CMEM + MEM
+    mixed = contract(qp_ref[...], rel_ref[...], 1, 1)
+    lead, tail = mixed[:, :half], mixed[:, half:]
+    cos, sin = cos_ref[...], sin_ref[...]
+    rotated = jnp.concatenate(
+        [(lead * sin + tail * cos).astype(BF16), (tail * sin - lead * cos).astype(BF16)], 1
+    )
+    scores = contract(qc_ref[...], k_ref[...], 1, 1) + contract(rotated, table_ref[...], 1, 1)
+    scores = scores * (1.0 / math.sqrt(DH))
+    row_ids = pl.program_id(1) * rows + lax.broadcasted_iota(jnp.int32, (rows, keys - split), 0)
+    col_ids = lax.broadcasted_iota(jnp.int32, (rows, keys - split), 1)
+    visible = (col_ids <= row_ids) & (col_ids < len_ref[0])
+    past = scores[:, :split]
+    own = jnp.where(visible, scores[:, split:], -1e30)
+    top = jnp.maximum(jnp.max(past, 1, keepdims=True), jnp.max(own, 1, keepdims=True))
+    past = jnp.exp(past - top)
+    own = jnp.exp(own - top)
+    total = jnp.sum(past, 1, keepdims=True) + jnp.sum(own, 1, keepdims=True)
+    scale = 1.0 / total
+    prob = jnp.concatenate([(past * scale).astype(BF16), (own * scale).astype(BF16)], 1)
+    p_ref[0] = prob
+    o_ref[...] = jnp.dot(prob, v_ref[...], preferred_element_type=F32).astype(BF16)
+
+
+def attend(heads, length, content, position, keys, values, w_rel, table, cos, sin, first=(), into=()):
+    seg, width = content.shape
+    total = keys.shape[0]
+    block = QUERY_BLOCK
+    start, count = heads.start, len(heads)
+    head = lambda h, q: (0, start + h)
+    rows = lambda h, q: (q, start + h)
+    whole = pl.BlockSpec(memory_space=pl.ANY)
+    operands = [length, content, position, keys, values, w_rel, table, cos, sin]
+    aliases = {len(operands) + i: i for i in range(len(into))}
+    operands += [*into, *first]
+    return pl.pallas_call(
+        attend_kernel,
+        grid=(count, seg // block),
+        in_specs=[
+            pl.BlockSpec(memory_space=pltpu.SMEM),
+            pl.BlockSpec((block, DH), rows),
+            pl.BlockSpec((block, DH), rows),
+            pl.BlockSpec((total, DH), head),
+            pl.BlockSpec((total, DH), head),
+            pl.BlockSpec((width, DH), head),
+            pl.BlockSpec((total, width), lambda h, q: (0, 0)),
+            pl.BlockSpec((block, width // 2), lambda h, q: (q, 0)),
+            pl.BlockSpec((block, width // 2), lambda h, q: (q, 0)),
+        ]
+        + [whole] * (len(into) + len(first)),
+        out_specs=[
+            pl.BlockSpec((1, block, total), lambda h, q: (start + h, q, 0)),
+            pl.BlockSpec((block, DH), rows),
+        ],
+        out_shape=[
+            jax.ShapeDtypeStruct((H, seg, total), BF16),
+            jax.ShapeDtypeStruct((seg, width), BF16),
+        ],
+        input_output_aliases=aliases,
+        compiler_params=pltpu.CompilerParams(vmem_limit_bytes=VMEM_LIMIT),
+        cost_estimate=SHORT,
+        name="attend",
+    )(*operands)
+
+
+def attend_back_kernel(
+    with_sums,
+    bits_ref,
+    p_ref,
+    da_ref,
+    qc_ref,
+    qp_ref,
+    k_ref,
+    v_ref,
+    rel_ref,
+    wq_ref,
+    wk_ref,
+    wv_ref,
+    normed_ref,
+    table_ref,
+    cos_ref,
+    sin_ref,
+    *rest,
+):
+    keep_ref, give_ref, rows_ref, along_ref, shift_ref, bias_ref = rest[-10:-4]
+    dk_sum, dv_sum, drel_sum, dq_all = rest[-4:]
+    head, step = pl.program_id(0), pl.program_id(1)
+    scale = 1.0 / math.sqrt(DH)
+    half = cos_ref.shape[1]
+    block = da_ref.shape[0]
+    seg = dq_all.shape[0]
+
+    @pl.when(step == 0)
+    def _():
+        dk_sum[...] = jnp.zeros_like(dk_sum)
+        dv_sum[...] = jnp.zeros_like(dv_sum)
+        drel_sum[...] = jnp.zeros_like(drel_sum)
+        bias_ref[...] = jnp.zeros_like(bias_ref)
+
+    prob = p_ref[0]
+    d_attn = da_ref[...]
+    dv_sum[...] += contract(prob, d_attn, 0, 0)
+    d_prob = contract(d_attn, v_ref[...], 1, 1)
+    prob_f = prob.astype(F32)
+    weighted = prob_f * d_prob
+    inner = jnp.sum(weighted, 1, keepdims=True)
+    d_scores = (weighted - prob_f * inner).astype(BF16)
+    dk_sum[...] += contract(d_scores, qc_ref[...], 0, 0)
+    d_content = jnp.dot(d_scores, k_ref[...], preferred_element_type=F32) * scale
+    d_rotated = jnp.dot(d_scores, table_ref[...], preferred_element_type=F32) * scale
+    lead, tail = d_rotated[:, :half], d_rotated[:, half:]
+    cos, sin = cos_ref[...], sin_ref[...]
+    d_mixed = jnp.concatenate(
+        [(lead * sin - tail * cos).astype(BF16), (lead * cos + tail * sin).astype(BF16)], 1
+    )
+    d_position = jnp.dot(d_mixed, rel_ref[...], preferred_element_type=F32)
+    drel_sum[...] += contract(d_mixed, qp_ref[...], 0, 0)
+    dq_all[pl.ds(pl.multiple_of(step * block, block), block), :] = (d_content + d_position).astype(
+        BF16
+    )
+    bias_ref[...] += jnp.concatenate(
+        [jnp.sum(d_content, 0, keepdims=True), jnp.sum(d_position, 0, keepdims=True)], 0
+    )
+
+    @pl.when(step == pl.num_programs(1) - 1)
+    def _():
+        d_key = (dk_sum[...] * scale).astype(BF16)
+        d_value = dv_sum[...].astype(BF16)
+        d_query = dq_all[...]
+        past = d_key.shape[0] - seg
+        of_kv = jnp.dot(
+            normed_ref[...], jnp.concatenate([d_key, d_value], 1), preferred_element_type=F32
+        )
+        of_query = jnp.dot(normed_ref[:, past:], d_query, preferred_element_type=F32)
+        mine = bits_ref[0] == 1
+        for i, grad in enumerate((of_query, drel_sum[...], of_kv[:, :DH], of_kv[:, DH:])):
+            middle = grad.shape[0] // 2
+            low, high = grad[:middle].astype(BF16), grad[middle:].astype(BF16)
+            keep_ref[i] = jnp.where(mine, high, low)
+            give_ref[i] = jnp.where(mine, low, high)
+        own_rows = (
+            contract(d_query, wq_ref[...], 1, 1)
+            + contract(d_key[past:], wk_ref[...], 1, 1)
+            + contract(d_value[past:], wv_ref[...], 1, 1)
+        )
+        wq = wq_ref[...].astype(F32)
+        wk = wk_ref[...].astype(F32)
+        wv = wv_ref[...].astype(F32)
+        own_along = of_query * wq + of_kv[:, :DH] * wk + of_kv[:, DH:] * wv
+        own_shift = (
+            jnp.sum(d_query.astype(F32), 0, keepdims=True) * wq
+            + jnp.sum(d_key.astype(F32), 0, keepdims=True) * wk
+            + jnp.sum(d_value.astype(F32), 0, keepdims=True) * wv
+        )
+
+        @pl.when(head == 0)
+        def _():
+            before = rest[:3] if with_sums else None
+            rows_ref[...] = own_rows + before[0][...] if with_sums else own_rows
+            along_ref[...] = own_along + before[1][...] if with_sums else own_along
+            shift_ref[...] = own_shift + before[2][...] if with_sums else own_shift
+
+        @pl.when(head > 0)
+        def _():
+            rows_ref[...] += own_rows
+            along_ref[...] += own_along
+            shift_ref[...] += own_shift
+
+
+def attend_back(
+    start,
+    count,
+    heads,
+    bits,
+    prob,
+    d_attn,
+    content,
+    position,
+    keys,
+    values,
+    w_rel,
+    w_query,
+    w_key,
+    w_value,
+    normed_t,
+    table,
+    cos,
+    sin,
+    sums=(),
+    into=(),
+    first=(),
+):
+    seg, width = content.shape
+    total = keys.shape[0]
+    block = QUERY_BLOCK
+    column = lambda h, q: (0, start + h)
+    rows = lambda h, q: (q, start + h)
+    fixed = lambda h, q: (0, 0)
+    whole = pl.BlockSpec(memory_space=pl.ANY)
+    operands = [bits, prob, d_attn, content, position, keys, values, w_rel]
+    operands += [w_query, w_key, w_value, normed_t, table, cos, sin]
+    aliases = {}
+    sum_specs = [
+        pl.BlockSpec((seg, width), fixed),
+        pl.BlockSpec((width, DH), fixed),
+        pl.BlockSpec((width, DH), fixed),
+    ]
+    for i in range(len(sums)):
+        aliases[len(operands) + i] = 2 + i
+    operands += [*sums]
+    for i in range(len(into)):
+        aliases[len(operands) + i] = i
+    operands += [*into, *first]
+    half = jax.ShapeDtypeStruct(into[0].shape if into else (4, width // 2, len(heads) * DH), BF16)
+    half_spec = pl.BlockSpec((4, width // 2, DH), lambda h, q: (0, 0, start - heads.start + h))
+    return pl.pallas_call(
+        functools.partial(attend_back_kernel, bool(sums)),
+        grid=(count, seg // block),
+        in_specs=[
+            pl.BlockSpec(memory_space=pltpu.SMEM),
+            pl.BlockSpec((1, block, total), lambda h, q: (start + h, q, 0)),
+            pl.BlockSpec((block, DH), rows),
+            pl.BlockSpec((block, DH), rows),
+            pl.BlockSpec((block, DH), rows),
+            pl.BlockSpec((total, DH), column),
+            pl.BlockSpec((total, DH), column),
+            pl.BlockSpec((width, DH), column),
+            pl.BlockSpec((width, DH), column),
+            pl.BlockSpec((width, DH), column),
+            pl.BlockSpec((width, DH), column),
+            pl.BlockSpec((width, total), fixed),
+            pl.BlockSpec((total, width), fixed),
+            pl.BlockSpec((block, width // 2), rows_of_block),
+            pl.BlockSpec((block, width // 2), rows_of_block),
+        ]
+        + sum_specs[: len(sums)]
+        + [whole] * (len(into) + len(first)),
+        out_specs=[half_spec, half_spec] + sum_specs + [pl.BlockSpec((2, DH), lambda h, q: (0, h))],
+        out_shape=[
+            half,
+            half,
+            jax.ShapeDtypeStruct((seg, width), F32),
+            jax.ShapeDtypeStruct((width, DH), F32),
+            jax.ShapeDtypeStruct((width, DH), F32),
+            jax.ShapeDtypeStruct((2, count * DH), F32),
+        ],
+        scratch_shapes=[
+            pltpu.VMEM((total, DH), F32),
+            pltpu.VMEM((total, DH), F32),
+            pltpu.VMEM((width, DH), F32),
+            pltpu.VMEM((seg, DH), BF16),
+        ],
+        input_output_aliases=aliases,
+        compiler_params=pltpu.CompilerParams(vmem_limit_bytes=VMEM_LIMIT),
+        cost_estimate=SHORT,
+        name="attend_back",
+    )(*operands)
+
+
+def rows_of_block(h, q):
+    return (q, 0)
+
+
+def in_vmem():
+    return pl.BlockSpec(memory_space=pltpu.VMEM)
+
+
+def norm_kernel(count, owners_ref, *refs):
+    parts, (gain_ref, shift_ref), (normed_ref, rows_ref) = refs[:count], refs[count : count + 2], refs[-2:]
+    block = rows_ref.shape[1]
+    for i, part in enumerate(parts):
+        owner = owners_ref[i]
+        for kind in range(3):
+            low = part[kind * block : (kind + 1) * block]
+            values = low.astype(F32)
+            center = values - jnp.mean(values, -1, keepdims=True)
+            spread = jnp.mean(center * center, -1, keepdims=True)
+            normed = center * lax.rsqrt(spread + 1e-05) * gain_ref[...] + shift_ref[...]
+            normed_ref[kind, owner] = normed.astype(BF16)
+            if kind == 2:
+                rows_ref[owner] = low
+
+
+def norm_context(parts, owners, gain, shift, after=()):
+    rows, width = parts[0].shape
+    block = rows // 3
+    normed, inputs = pl.pallas_call(
+        functools.partial(norm_kernel, len(parts)),
+        in_specs=[pl.BlockSpec(memory_space=pltpu.SMEM)] + [in_vmem()] * (len(parts) + 2)
+        + [pl.BlockSpec(memory_space=pl.ANY)] * len(after),
+        out_specs=[in_vmem(), in_vmem()],
+        out_shape=[
+            jax.ShapeDtypeStruct((3, len(parts), block, width), BF16),
+            jax.ShapeDtypeStruct((len(parts), block, width), BF16),
+        ],
+        compiler_params=pltpu.CompilerParams(vmem_limit_bytes=VMEM_LIMIT),
+        cost_estimate=SHORT,
+        name="norm_context",
+    )(owners, *parts, gain.reshape(1, -1), shift.reshape(1, -1), *after)
+    return normed.reshape(-1, width), inputs.reshape(-1, width)
+
+
+def place_kernel(count, owners_ref, *refs):
+    for i, part in enumerate(refs[:count]):
+        refs[-1][owners_ref[i]] = part[...]
+
+
+def place_rows(parts, owners, after=()):
+    rows, width = parts[0].shape
+    return pl.pallas_call(
+        functools.partial(place_kernel, len(parts)),
+        in_specs=[pl.BlockSpec(memory_space=pltpu.SMEM)]
+        + [in_vmem()] * len(parts)
+        + [pl.BlockSpec(memory_space=pl.ANY)] * len(after),
+        out_specs=in_vmem(),
+        out_shape=jax.ShapeDtypeStruct((len(parts), rows, width), parts[0].dtype),
+        cost_estimate=SHORT,
+        name="place_rows",
+    )(owners, *parts, *after)
+
+
+def copy_kernel(rows_ref, *refs):
+    refs[-1][...] = rows_ref[...]
+
+
+def copy_after(rows, *others):
+    return pl.pallas_call(
+        copy_kernel,
+        in_specs=[in_vmem()] + [pl.BlockSpec(memory_space=pl.ANY)] * len(others),
+        out_specs=in_vmem(),
+        out_shape=jax.ShapeDtypeStruct(rows.shape, rows.dtype),
+        cost_estimate=SHORT,
+        name="copy_after",
+    )(rows, *others)
+
+
+def flip_kernel(rows_ref, *refs):
+    refs[-1][...] = rows_ref[...].T
+
+
+def flip_after(rows, *others):
+    count, width = rows.shape
+    block = width // 2
+    return pl.pallas_call(
+        flip_kernel,
+        grid=(count // block,),
+        in_specs=[pl.BlockSpec((block, width), lambda i: (i, 0))]
+        + [pl.BlockSpec(memory_space=pl.ANY)] * len(others),
+        out_specs=pl.BlockSpec((width, block), lambda i: (0, i)),
+        out_shape=jax.ShapeDtypeStruct((width, count), rows.dtype),
+        cost_estimate=SHORT,
+        name="flip_after",
+    )(rows, *others)
+
+
+def half_grad_kernel(bits_ref, left_ref, right_ref, out_ref):
+    out_ref[...] = contract(left_ref[...], right_ref[...], 0, 0).astype(BF16)
+
+
+def half_grad(bits, which, pre, left, right, give):
+    rows, units = left.shape
+    width = right.shape[1]
+    cells = 1 << max(pre.bit_length(), 2)
+    run = cells // (2 * pre)
+
+    def column(i, bits):
+        side = 1 - bits[which] if give else bits[which]
+        return (0, (i // run * 2 + side) * run + i % run)
+
+    return pl.pallas_call(
+        half_grad_kernel,
+        grid_spec=pltpu.PrefetchScalarGridSpec(
+            num_scalar_prefetch=1,
+            grid=(cells // 2,),
+            in_specs=[
+                pl.BlockSpec((rows, units // cells), column),
+                pl.BlockSpec((rows, width), lambda i, bits: (0, 0)),
+            ],
+            out_specs=pl.BlockSpec((units // cells, width), lambda i, bits: (i, 0)),
+        ),
+        out_shape=jax.ShapeDtypeStruct((units // 2, width), BF16),
+        compiler_params=pltpu.CompilerParams(vmem_limit_bytes=VMEM_LIMIT),
+        cost_estimate=SHORT,
+        name="half_grad",
+    )(bits, left, right)[None]
+
+
+def out_grad_kernel(bits_ref, left_ref, right_ref, keep_ref, give_ref):
+    mine = bits_ref[0] == 1
+    grad = contract(left_ref[...], right_ref[...], 0, 0)
+    middle, columns = keep_ref.shape[1:]
+    for i in range(2):
+        part = grad[:, i * columns : (i + 1) * columns]
+        low, high = part[:middle].astype(BF16), part[middle:].astype(BF16)
+        keep_ref[i] = jnp.where(mine, high, low)
+        give_ref[i] = jnp.where(mine, low, high)
+
+
+def out_grad(bits, left, right):
+    width = right.shape[1]
+    half = jax.ShapeDtypeStruct((6, width // 2, width // 2), BF16)
+    spec = pl.BlockSpec((2, width // 2, width // 2), lambda i: (2, 0, 0))
+    whole = pl.BlockSpec(left.shape, lambda i: (0, 0))
+    return pl.pallas_call(
+        out_grad_kernel,
+        grid=(1,),
+        in_specs=[pl.BlockSpec(memory_space=pltpu.SMEM), whole, whole],
+        out_specs=[spec, spec],
+        out_shape=[half, half],
+        compiler_params=pltpu.CompilerParams(vmem_limit_bytes=VMEM_LIMIT),
+        cost_estimate=SHORT,
+        name="out_grad",
+    )(bits, left, right)
+
+
+def finish_kernel(bits_ref, own_ref, got_ref, *refs):
+    outs = refs[-5:]
+    own = pl.program_id(0) == bits_ref[0]
+
+    def write(ref):
+        for i in range(4):
+            outs[i][...] = ref[i].astype(F32)
+        if ref.shape[0] > 4:
+            half = ref.shape[2]
+            outs[4][:, :half] = ref[4].astype(F32)
+            outs[4][:, half:] = ref[5].astype(F32)
+
+    pl.when(own)(lambda: write(own_ref))
+    pl.when(jnp.logical_not(own))(lambda: write(got_ref))
+
+
+def finish(bits, column, columns, own, got, results):
+    count, rows, width = own.shape
+    fixed = pl.BlockSpec(own.shape, lambda i: (0, 0, 0))
+    block = pl.BlockSpec((rows, width), lambda i: (i, column))
+    last = pl.BlockSpec((rows, columns * width), lambda i: (i, 0))
+    out = jax.ShapeDtypeStruct((2 * rows, columns * width), F32)
+    if count == 4:
+        out_specs, before = [block] * 4, results[:4]
+    else:
+        out_specs, before = [block] * 4 + [last], results
+    sums = pl.pallas_call(
+        finish_kernel if count > 4 else lambda *refs: finish_kernel(*refs, None),
+        grid=(2,),
+        in_specs=[pl.BlockSpec(memory_space=pltpu.SMEM), fixed, fixed]
+        + [pl.BlockSpec(memory_space=pl.ANY)] * len(before),
+        out_specs=out_specs,
+        out_shape=[out] * len(out_specs),
+        input_output_aliases={3 + i: i for i in range(len(before))},
+        compiler_params=pltpu.CompilerParams(vmem_limit_bytes=VMEM_LIMIT),
+        cost_estimate=SHORT,
+        name="finish",
+    )(bits, own, got, *before)
+    return list(sums) + list(results[len(sums) :])
+
+
+class Chain:
+    def __init__(self, moves, keeps, gives):
+        self.moves, self.keeps, self.gives = list(moves), keeps, gives
+        self.join = False
+
+
+def parts_of(move):
+    return len(move[1])
+
+
+def split_rows(rows, pre):
+    lead, count, columns = rows.shape
+    return rows.reshape(lead, pre, 2, count // (2 * pre), columns)
+
+
+def first_halves(rows, move):
+    keeps, gives = [], []
+    size = rows.shape[0] // parts_of(move)
+    for i, (step, pre) in enumerate(move[1]):
+        cells = split_rows(rows[i * size : (i + 1) * size], pre)
+        bit = bit_of(*step)
+        flat = (size, -1, rows.shape[2])
+        keeps.append(pick(cells, bit, 2).reshape(flat))
+        gives.append(pick(cells, 1 - bit, 2).reshape(flat))
+    return keeps, gives
+
+
+def round_of(chains, bits, bit_names, after=()):
+    operands, plans, out_shape = [], [], []
+    for chain in chains:
+        kind, cuts = chain.moves.pop(0)
+        nexts = chain.moves[0] if chain.moves else None
+        got = [swap(give, *step) for give, (step, _) in zip(chain.gives, cuts)]
+        held = chain.keeps if kind == "halve" else chain.gives
+        leads, columns = [h.shape[0] for h in held], held[0].shape[2]
+        total = sum(leads)
+        next_kind, next_cuts = nexts if nexts else ("end", [None])
+        size = total // len(next_cuts)
+        ins, views = [], []
+        for i, (h, g) in enumerate(zip(held, got)):
+            base = sum(leads[:i])
+            if kind == "double":
+                cells = max(pre for _, pre in cuts)
+                view = (h.shape[0], cells, h.shape[1] // cells, columns)
+                bit = (bit_names.index(cuts[i][0]), cuts[i][1])
+            elif next_kind == "halve":
+                cells = max(2 * pre for _, pre in next_cuts)
+                view = (h.shape[0], cells, h.shape[1] // cells, columns)
+                bit = None
+            else:
+                view = h.shape
+                bit = None
+            ins.append((len(operands), base, bit, view))
+            operands += [h.reshape(view), g.reshape(view)]
+        rows = held[0].shape[1]
+        outs = []
+        for j, cut in enumerate(next_cuts):
+            if next_kind == "halve":
+                cells = ins[0][3][1]
+                shape = (size, cells // 2, rows // cells, columns)
+                outs.append((len(out_shape), bit_names.index(cut[0]), cut[1]))
+                out_shape += [jax.ShapeDtypeStruct(shape, BF16)] * 2
+            else:
+                if kind == "double":
+                    cells = ins[0][3][1]
+                    shape = (size, cells * 2, rows // cells, columns)
+                    if chain.join and next_kind == "end":
+                        shape = (1, cells * 2, rows // cells, size * columns)
+                else:
+                    shape = (size, rows, columns)
+                outs.append((len(out_shape), None, None))
+                out_shape += [jax.ShapeDtypeStruct(shape, held[0].dtype)]
+        plans.append((kind, next_kind, size, ins, outs))
+
+    def kernel(bits_ref, *refs):
+        inputs, results = refs[: len(operands)], refs[-len(out_shape) :]
+        for kind, next_kind, size, ins, outs in plans:
+            for at, base, bit, view in ins:
+                held_ref, got_ref = inputs[at], inputs[at + 1]
+                for i in range(view[0]):
+                    where, which = divmod(base + i, size)
+                    out, out_bit, out_pre = outs[where]
+                    if kind == "double":
+                        mine = bits_ref[bit[0]]
+                        run = view[1] // bit[1]
+                        for cell in range(view[1]):
+                            for side, ref in ((mine, held_ref), (1 - mine, got_ref)):
+                                place = (cell // run * 2 + side) * run + cell % run
+                                if results[out].shape[3] == ref.shape[3]:
+                                    results[out][which, place] = ref[i, cell]
+                                else:
+                                    wide = slice(which * ref.shape[3], (which + 1) * ref.shape[3])
+                                    results[out][0, place, :, wide] = ref[i, cell]
+                    elif next_kind == "halve":
+                        mine = bits_ref[out_bit]
+                        run = view[1] // (2 * out_pre)
+                        for cell in range(view[1] // 2):
+                            for side, slot in ((mine, out), (1 - mine, out + 1)):
+                                place = (cell // run * 2 + side) * run + cell % run
+                                results[slot][which, cell] = (
+                                    held_ref[i, place].astype(F32) + got_ref[i, place].astype(F32)
+                                ).astype(BF16)
+                    else:
+                        results[out][which] = (held_ref[i].astype(F32) + got_ref[i].astype(F32)).astype(
+                            results[out].dtype
+                        )
+
+    in_vmem = pl.BlockSpec(memory_space=pltpu.VMEM)
+    results = pl.pallas_call(
+        kernel,
+        in_specs=[pl.BlockSpec(memory_space=pltpu.SMEM)]
+        + [in_vmem] * len(operands)
+        + [pl.BlockSpec(memory_space=pl.ANY)] * len(after),
+        out_specs=[in_vmem] * len(out_shape),
+        out_shape=out_shape,
+        compiler_params=pltpu.CompilerParams(vmem_limit_bytes=VMEM_LIMIT),
+        cost_estimate=SHORT,
+        name="add_and_split",
+    )(bits, *operands, *after)
+    for chain, (kind, next_kind, size, ins, outs) in zip(chains, plans):
+        flat = lambda r: r.reshape(r.shape[0], -1, r.shape[-1])
+        if next_kind == "halve":
+            chain.keeps = [flat(results[o]) for o, _, _ in outs]
+            chain.gives = [flat(results[o + 1]) for o, _, _ in outs]
+        else:
+            chain.keeps = []
+            chain.gives = [flat(results[o]) for o, _, _ in outs]
+
+
+def gather_wide(rows, wide, order):
+    have = []
+    for i in order:
+        rows = double(rows, wide[i], sum(j < i for j in have))
+        have.append(i)
+    return rows
+
+
+def own_streams_plan(
+    inputs,
+    memory,
+    compressed,
+    seg_len,
+    gain_first,
+    shift_first,
+    w_query,
+    w_key,
+    w_value,
+    w_rel,
+    bias_content,
+    bias_position,
+    w_out,
+    gain_second,
+    shift_second,
+    w_up,
+    bias_up,
+    w_down,
+    bias_down,
+    w_comp,
+    comp_bias,
+    grad_out,
+    grad_comp,
+):
+    seq_parts = lax.axis_size("seq")
+    dp_parts = lax.axis_size("dp")
+    me = lax.axis_index("seq")
+    seg_dev, streams, width = inputs.shape
+    seg = seg_dev * seq_parts
+    split = CMEM + MEM
+    hidden_dev = w_down.shape[0]
+
+    core = ("dp", 1)
+    wide = [("dp", d) for d in bits_below(dp_parts)[1:]]
+    line = [("seq", d) for d in bits_below(seq_parts)]
+    there = list(range(len(wide)))
+    back = there[::-1]
+    core_bit = bit_of(*core)
+
+    bit_names = [core] + wide + line
+    bits = jnp.stack([bit_of(*name) for name in bit_names]).astype(jnp.int32)
+    wide_in = [[(wide[i], 1), (wide[j], 1 << j)] for i, j in zip(there, back)]
+    core_cut, line_cuts, wide_cuts = [(core, 1)], [[(s, 1)] for s in line], [[(s, 1)] for s in wide]
+
+    def moves_of(cuts, collected):
+        return [("halve", c) for c in cuts] + [("double", c) for c in reversed(collected)]
+
+    piece = hidden_dev // 2 >> len(wide)
+    place = core_bit
+    for step in wide:
+        place = place * 2 + bit_of(*step)
+
+    def gathered(rows):
+        rows = jnp.swapaxes(rows.reshape(piece, 2, width // 2), 0, 1)
+        chain = Chain(moves_of([], wide_in + line_cuts), [], [rows])
+        chain.join = True
+        return chain
+
+    up_piece = lax.dynamic_slice_in_dim(w_up, place * piece, piece, 1).T
+    up_chain = gathered(up_piece)
+    round_of([up_chain], bits, bit_names)
+    order = token(up_chain.gives[0])
+    for step in line[:-1]:
+        round_of([up_chain], bits, bit_names)
+    order_two = token(up_chain.gives[0])
+
+    key_cos, key_sin = sinusoids(jnp.arange(split + seg, dtype=jnp.int32))
+    table = jnp.concatenate([key_cos, key_sin], -1).astype(BF16)
+    cos, sin = key_cos[split:], key_sin[split:]
+
+    owners = jnp.stack([(me - shift) % seq_parts for shift in range(seq_parts)]).astype(jnp.int32)
+
+    def send(parts):
+        return [parts[0]] + [
+            lax.ppermute(part, "seq", [(i, (i + shift) % seq_parts) for i in range(seq_parts)])
+            for shift, part in enumerate(parts)
+            if shift
+        ]
+
+    def parts_for(rows, order=0):
+        return [pick(rows, (me + shift) % seq_parts + order, 0) for shift in range(seq_parts)]
+
+    def from_streams(parts):
+        return by_stream(place_rows(send(parts), owners))
+
+    blocks = [by_stream(rows) for rows in (compressed, memory, inputs)]
+    parts = send(parts_for(jnp.concatenate(blocks, 1), order))
+    down_piece = lax.dynamic_slice_in_dim(w_down, place * piece + order_two, piece, 0)
+    down_chain = gathered(down_piece)
+    round_of([up_chain], bits, bit_names)
+    normed, x_rows = norm_context(
+        parts, owners, gain_first, shift_first, [*up_chain.gives, *down_chain.gives, table, cos, sin]
+    )
+    length = lax.dynamic_slice_in_dim(seg_len, me, 1)
+    order = token(normed)
+    go_parts = parts_for(by_stream(grad_out), order)
+    bias_all = lax.dynamic_slice_in_dim(bias_up.reshape(2, -1), core_bit + order, 1, 0)
+
+    seg_normed = normed[split:]
+    queries = jnp.dot(seg_normed, w_query, preferred_element_type=F32)
+    keys = jnp.dot(normed, w_key, preferred_element_type=F32).astype(BF16)
+    values = jnp.dot(normed, w_value, preferred_element_type=F32).astype(BF16)
+    content = (queries + bias_content).astype(BF16)
+    position = (queries + bias_position).astype(BF16)
+    given = (length, content, position, keys, values, w_rel, table, cos, sin)
+    round_of([down_chain], bits, bit_names, [normed])
+    round_of([down_chain], bits, bit_names, [values])
+    go_rows = send(go_parts)
+    prob, attn_out = attend(range(H // 2), *given, first=down_chain.gives + go_parts[1:])
+    go_rows = place_rows(go_rows, owners, [attn_out]).reshape(seg, width)
+    round_of([down_chain], bits, bit_names, [attn_out])
+    while up_chain.moves:
+        round_of([up_chain], bits, bit_names, [attn_out])
+    up_half = up_chain.gives[0][0]
+    bias_all = double(bias_all, line[-1], 0)
+    prob, attn_out = attend(
+        range(H // 2, H),
+        *given,
+        first=down_chain.gives + [go_rows, bias_all, up_half],
+        into=[prob, attn_out],
+    )
+    while down_chain.moves:
+        round_of([down_chain], bits, bit_names, [attn_out])
+    down_half = down_chain.gives[0][0]
+    for step in line[-2::-1]:
+        bias_all = double(bias_all, step, 0)
+    bias_half = jnp.swapaxes(bias_all.reshape(seq_parts, -1, piece), 0, 1).reshape(-1).astype(F32)
+    memory_rows = copy_after(by_stream(memory), attn_out)
+    memory_all = lax.all_gather(memory_rows, "seq", axis=1, tiled=True)
+    x_f = x_rows.astype(F32)
+    hidden = x_f + jnp.dot(attn_out, w_out, preferred_element_type=F32)
+    normed_two = layer_norm(hidden, gain_second, shift_second).astype(BF16)
+
+    pair_normed = double(normed_two, core).reshape(-1, width)
+    pair_grad = double(go_rows, core).reshape(-1, width)
+    pre_act = contract(pair_normed, up_half, 1, 1) + bias_half
+    activated = gelu_tanh(pre_act).astype(BF16)
+    ffn_rows = jnp.dot(activated, down_half, preferred_element_type=F32)
+    ffn_rows = halve(ffn_rows.reshape(2, seg, width), core)
+    output = (hidden + ffn_rows + bias_down).astype(BF16)
+    output_parts = parts_for(output.reshape(seq_parts, seg_dev, width))
+    down_grad = functools.partial(half_grad, bits, 1, 1, activated, pair_grad)
+    down_give = down_grad(True)
+    d_activated = contract(pair_grad, down_half, 1, 1)
+    _, gelu_back = jax.vjp(gelu_tanh, pre_act)
+    d_pre = gelu_back(d_activated)[0].astype(BF16)
+    up_grad = functools.partial(half_grad, bits, len(wide), 1 << (len(wide) - 1), d_pre, pair_normed)
+    up_give = up_grad(True)
+    d_normed_two = jnp.dot(d_pre, up_half, preferred_element_type=F32)
+    d_normed_two = halve(d_normed_two.reshape(2, seg, width), core)
+    grad_bias_half = jnp.sum(d_pre.astype(F32), 0)
+    ffn = Chain(
+        moves_of(wide_in + line_cuts, [core_cut] + wide_in),
+        [down_grad(False), up_grad(False)],
+        [down_give, up_give],
+    )
+
+    go_f = go_rows.astype(F32)
+    _, norm_two_back = jax.vjp(layer_norm, hidden, gain_second, shift_second)
+    d_hidden_ffn, grad_gain_second, grad_shift_second = norm_two_back(d_normed_two)
+    d_hidden = go_f + d_hidden_ffn
+    grad_bias_down = jnp.sum(go_f, 0)
+    d_branch = d_hidden.astype(BF16)
+    d_attn = contract(d_branch, w_out, 1, 1).astype(BF16)
+
+    new_rows = memory_all.shape[1] // RATE
+    windows = memory_all[:, : new_rows * RATE].reshape(streams, new_rows, RATE, width)
+    new_compressed = (
+        jnp.einsum("srtd,tde->rse", windows, w_comp, preferred_element_type=F32) + comp_bias
+    ).astype(BF16)
+    grad_w_comp = jnp.einsum("srtd,rse->tde", windows, grad_comp, preferred_element_type=F32)
+    grad_comp_bias = jnp.sum(grad_comp.astype(F32), (0, 1))
+    comp_moves = moves_of([core_cut] + wide_cuts, [core_cut] + wide_cuts)
+    comp_shape = grad_w_comp.shape
+    comp = Chain(
+        comp_moves, *first_halves(grad_w_comp.astype(BF16).reshape(1, -1, comp_shape[2]), comp_moves[0])
+    )
+
+    normed_t = flip_after(normed, normed_two)
+    half_heads = H // 2
+    group_moves = moves_of([core_cut] + wide_in + line_cuts, [core_cut] + wide_in + line_cuts)
+    groups, biases, head_sums = [], [], []
+    output_rows = send(output_parts)
+    first = ffn.gives + output_parts[1:] + [memory_rows]
+    beside = [[], [], [ffn, comp], [ffn, comp]]
+    for start in range(0, H, HEADS_A_CALL):
+        base = start // half_heads * half_heads
+        group_heads = range(base, base + half_heads)
+        if start == 0:
+            halves = out_grad(bits, attn_out, d_branch)
+        elif start == base:
+            halves = []
+        *halves, d_rows, along, shift_part, bias_part = attend_back(
+            start, HEADS_A_CALL, group_heads, bits, prob, d_attn, content, position, keys, values,
+            w_rel, w_query, w_key, w_value, normed_t, table, cos, sin, head_sums, halves, first,
+        )
+        head_sums = [d_rows, along, shift_part]
+        biases.append(bias_part)
+        active = beside[start // HEADS_A_CALL] + groups
+        if active:
+            round_of(active, bits, bit_names, [bias_part])
+        first = [g for c in active for g in c.gives]
+        if start == 0:
+            output_rows = place_rows(output_rows, owners, [bias_part])
+            first += [output_rows]
+        if start + HEADS_A_CALL == group_heads.stop:
+            groups.append(Chain(group_moves, [halves[0]], [halves[1]]))
+            first += groups[-1].gives
+            if start + HEADS_A_CALL == half_heads:
+                first += comp.gives + ffn.keeps
+    output = by_stream(output_rows)
+    d_normed = d_rows
+    _, norm_one_back = jax.vjp(lambda v: layer_norm(v, gain_first, shift_first), x_f)
+    (d_context,) = norm_one_back(d_normed)
+    grad_inputs = (d_hidden + d_context).astype(BF16).reshape(seq_parts, seg_dev, width)
+    input_parts = parts_for(grad_inputs)
+    input_rows = send(input_parts)
+
+    grad_shift_first = jnp.sum(shift_part, 1)
+    grad_gain_first = (jnp.sum(along, 1) - shift_first * grad_shift_first) / gain_first
+    vectors = jnp.concatenate(
+        [
+            jnp.concatenate(biases, 1).reshape(-1),
+            grad_gain_first,
+            grad_shift_first,
+            grad_gain_second,
+            grad_shift_second,
+            grad_bias_down,
+        ]
+    )
+    count = vectors.shape[0]
+    hidden_sums = jnp.zeros((2, grad_bias_half.shape[0]), F32)
+    hidden_sums = lax.dynamic_update_slice(hidden_sums, grad_bias_half[None], (core_bit, 0))
+    comp_sums = jnp.zeros((seq_parts, grad_comp_bias.shape[0]), F32)
+    comp_sums = lax.dynamic_update_slice(comp_sums, grad_comp_bias[None], (me, 0))
+    vectors = jnp.concatenate([vectors, hidden_sums.reshape(-1), comp_sums.reshape(-1)])
+    vector = Chain([("add", [(name, 1)]) for name in bit_names], [], [vectors.reshape(1, -1, DH)])
+
+    one, two = groups
+    rounds = [
+        [ffn, one, two, vector],
+        [ffn, one, two, vector],
+        [ffn, one, two],
+        [ffn, one, two, vector, comp],
+        [ffn, one, two, vector, comp],
+        [one, two, vector, comp],
+        [one, two, comp],
+    ]
+    turn = 0
+    while len(two.moves) > 1 or vector.moves or comp.moves or ffn.moves:
+        active = rounds[turn] if turn < len(rounds) else [ffn, one, two, vector, comp]
+        active = [c for c in active if len(c.moves) > (c in groups)]
+        if turn == 5:
+            fence = input_parts
+        elif turn == 8:
+            input_rows = place_rows(input_rows, owners)
+            fence = [input_rows]
+        else:
+            fence = []
+        round_of(active, bits, bit_names, fence)
+        turn += 1
+    grad_inputs = by_stream(input_rows)
+    vectors = vector.gives[0].reshape(-1)
+
+    grad_w_down = ffn.gives[0][0].astype(F32)
+    grad_w_up = ffn.gives[0][1].astype(F32).T
+    grad_w_comp = comp.gives[0].astype(F32).reshape(comp_shape)
+    results = []
+    for column, group in enumerate(groups):
+        own = group.gives[0]
+        results = finish(bits, column, len(groups), own, swap(own, *core), results)
+    grad_w_query, grad_w_rel, grad_w_key, grad_w_value, grad_w_out = results
+
+    totals = vectors[:count].reshape(-1, width)
+    hidden_sums = vectors[count : count + hidden_sums.size].reshape(
+        [2, 1 << len(wide)] + [2] * len(line) + [piece]
+    )
+    for step in line:
+        hidden_sums = pick(hidden_sums, bit_of(*step), 2)
+    grad_bias_up = hidden_sums.reshape(-1)
+    comp_sums = vectors[count + grad_bias_half.size * 2 :].reshape(comp_sums.shape)
+    grad_comp_bias = pick(comp_sums, me, 0)
+
+    return (
+        output,
+        grad_inputs,
+        new_compressed,
+        totals[2],
+        totals[3],
+        grad_w_query,
+        grad_w_key,
+        grad_w_value,
+        grad_w_rel,
+        totals[0],
+        totals[1],
+        grad_w_out,
+        totals[4],
+        totals[5],
+        grad_w_up,
+        grad_bias_up,
+        grad_w_down,
+        totals[6],
+        grad_w_comp,
+        grad_comp_bias,
+    )
+
+
+def on_device(*arrays):
+    streams = arrays[0].shape[1]
+    dp_parts, seq_parts = lax.axis_size("dp"), lax.axis_size("seq")
+    fits = streams == seq_parts and seq_parts > 1 and dp_parts >= 4
+    powers = (seq_parts & (seq_parts - 1)) == 0 and (dp_parts & (dp_parts - 1)) == 0
+    plan = own_streams_plan if fits and powers else split_rows_plan
+    return plan(*arrays)
+
+
 def solution(mesh):
     in_specs = (
         P("seq", "dp", None),

time: 1850 us -> 751 us (0.41)
  waiting for transfers between devices: 1270 us -> 189 us
  Pallas kernels: 0 us -> 241 us
  matrix products: 269 us -> 49.8 us
  starting transfers between devices: 1.41 us -> 93.2 us
  other arithmetic: 115 us -> 47.4 us
  blocking collectives: 58.5 us -> 0 us
    all_gather x5 -> x1, waiting for transfers between devices: 470 us -> 0.01 us  [own_streams_plan(): memory_all = lax.all_gather(memory_rows, 'seq', axis=1, tiled=True)]
    reduce_scatter x3 -> x0, waiting for transfers between devices: 440 us -> none  [the longest x1 313 us: on_device(): lax.psum_scatter(jnp.concatenate([key_part.reshape(ctx_dev * lax.axis_siz...]
    psum x2 -> x0, waiting for transfers between devices: 358 us -> none  [the longest x1 290 us: on_device(): lax.psum((grad_w_query, grad_w_key, grad_w_value, grad_w_rel, grad_w_out,...]
    pallas_call x0 -> x38, Pallas kernels: none -> 241 us  [the longest x4 91.9 us: attend_back(): pl.pallas_call(functools.partial(attend_back_kernel, bool(sums)), grid=(c...]
    dot_general x31 -> x11, matrix products: 269 us -> 49.8 us  [the longest x3 21.1 us: contract(): lax.dot_general(left, right, (((left_dim,), (right_dim,)), ((), ())), pre...]
    ppermute x0 -> x80, waiting for transfers between devices: none -> 189 us  [the longest x68 137 us: swap(): return lax.ppermute(rows, axis, [(i, i ^ distance) for i in range(count)])]
    ppermute x0 -> x80, starting transfers between devices: none -> 93.2 us  [the longest x68 72.3 us: swap(): return lax.ppermute(rows, axis, [(i, i ^ distance) for i in range(count)])]
    reshape x8 -> x4, local copies, waits for them, and re-layouts: 65.2 us -> 0.31 us  [the longest x2 0.29 us: gathered(): rows = jnp.swapaxes(rows.reshape(piece, 2, width // 2), 0, 1)]
  transfers between devices with their start and end apart: 10 -> 81, of which waited for: 9 -> 32; matrix products, arithmetic and copies ran while one was open for 23% -> 20% of each run, Pallas kernels for 0% -> 28%
where the time goes in v1:
time: 751 us; the launch traced here: 742 us
  Pallas kernels  241 us (32%)
  waiting for transfers between devices  189 us (25%)
  local copies, waits for them, and re-layouts  104 us (14%)
  starting transfers between devices  93.2 us (12%)
  matrix products  49.8 us (7%)
  other arithmetic  47.4 us (6%)
  between operations  17.7 us (2%)
    ppermute x68, waiting for transfers between devices, swap(): return lax.ppermute(rows, axis, [(i, i ^ distance) for i in range(count)])  137 us
    pallas_call x4, Pallas kernels, attend_back(): pl.pallas_call(functools.partial(attend_back_kernel, bool(sums)), grid=(c...  91.9 us
    ppermute x68, starting transfers between devices, swap(): return lax.ppermute(rows, axis, [(i, i ^ distance) for i in range(count)])  72.3 us
    unnamed x273, local copies, waits for them, and re-layouts  63.6 us
    ppermute x12, waiting for transfers between devices, send(): lax.ppermute(part, 'seq', [(i, (i + shift) % seq_parts) for i in range(se...  52.2 us
    pallas_call x19, Pallas kernels, round_of(): pl.pallas_call(kernel, in_specs=[pl.BlockSpec(memory_space=pltpu.SMEM)] +...  50.8 us
    pallas_call x2, Pallas kernels, attend(): pl.pallas_call(attend_kernel, grid=(count, seg // block), in_specs=[pl.Bl...  43.3 us
    dot_general x3, matrix products, contract(): lax.dot_general(left, right, (((left_dim,), (right_dim,)), ((), ())), pre...  21.1 us
  transfers between devices with their start and end apart: 81, of which 32 were waited for; matrix products, arithmetic and copies ran while one was open for 20% of the time, Pallas kernels for 28%

profile of v1, /device:TPU:0, one launch (start us, length us, event | category | flops | bytes accessed | tf_op | source)
XLA Modules:
  0.0 742.1 jit_solution(10194611854178736713)
XLA Ops:
  8.6 4.1 collective-permute-start
  16.3 8.3 %collective-permute-done = bf16[2,128,512]{2,1,0:T(8,128)(2,1)S(1)} collective-permute-done((bf16[2,128,512]{2,1,0:T(8,128)(2,1)S(1)}, bf16[2,128,512]{2,1,0:T(8,128)(2,1)S(1)}, u32[]{:S(2)}, u32[]{:S(2)}) %collective-permute-start) | collective-permute-done | bytes 262176 | tf_op jit(solution)/shard_map/ppermute | solution.py:359
  44.9 13.9 %multiply_sine_fusion = (f32[1536,512]{1,0:T(8,128)}, bf16[1536,512]{1,0:T(8,128)(2,1)}, bf16[1536,512]{1,0:T(8,128)(2,1)}, f32[1536,512]{1,0:T(8,128)}) fusion(f32[512]{0:T(512)S(1)} %multiply_exponential_fusion, f32[1536]{0:T(1024)S(1)} %iota_convert_fusion), kind=kLoop, calls=%fused_computation.11 | loop fusion | flops 2359296 | bytes 9445376 | tf_op jit(solution)/shard_map/sin | solution.py:33
  78.7 35.7 %collective-permute-done.2.refs_2_ = bf16[384,1024]{1,0:T(8,128)(2,1)} collective-permute-done((bf16[384,1024]{1,0:T(8,128)(2,1)}, bf16[384,1024]{1,0:T(8,128)(2,1)}, u32[]{:S(2)}, u32[]{:S(2)}) %collective-permute-start.2) | collective-permute-done | bytes 786464 | tf_op jit(solution)/shard_map/ppermute | solution.py:1081
  114.4 5.6 norm_context.1
  127.2 4.9 constant_dynamic-slice_fusion.4
  134.8 5.2 convolution_convert_fusion.refs_2_.v_ref
  140.0 4.8 convolution_convert_fusion.1.k_ref
  153.1 5.5 collective-permute-done.12.refs_2_
  160.0 21.7 %attend.2 = (bf16[8,512,1536]{2,1,0:T(8,128)(2,1)}, bf16[512,1024]{1,0:T(8,128)(2,1)S(1)}) custom-call(s32[1]{0:T(128)} %dynamic_slice.90.len_ref, bf16[512,1024]{1,0:T(8,128)(2,1)S(1)} %get-tuple-element.326.qc_ref, bf16[512,1024]{1,0:T(8,128)(2,1)S(1)} %get-tuple-element.325.qp_ref, bf16[1536,1024]{1,0:T(8,128)(2,1)} %convolution_convert_fusion.1.k_ref, ...), custom_call_target="tpu_custom_call" | custom-call | flops 1024 | bytes 1024 | tf_op jit(solution)/shard_map/attend/pallas_call | solution.py:448
  185.8 4.7 add_and_split.25
  193.7 21.5 %attend.3 = (bf16[8,512,1536]{2,1,0:T(8,128)(2,1)}, bf16[512,1024]{1,0:T(8,128)(2,1)S(1)}) custom-call(s32[1]{0:T(128)} %dynamic_slice.90.len_ref, bf16[512,1024]{1,0:T(8,128)(2,1)S(1)} %copy-done.17, bf16[512,1024]{1,0:T(8,128)(2,1)S(1)} %copy-done.13, ...), custom_call_target="tpu_custom_call", output_to_operand_aliasing={{0}: (9, {}), {1}: (10, {})} | custom-call | flops 1024 | bytes 1024 | tf_op jit(solution)/shard_map/attend/pallas_call | solution.py:448
  237.3 6.7 fusion.60
  244.0 5.6 collective-permute-done.20
  250.9 4.6 add_and_split.26
  255.4 13.1 %convert_reduce_fusion = (f32[2048]{0:T(1024)S(1)}, bf16[1024,2048]{1,0:T(8,128)(2,1)S(1)}, bf16[1024,2048]{1,0:T(8,128)(2,1)S(1)}) fusion(f32[1024,2048]{1,0:T(8,128)} %fusion.60, f32[2048]{0:T(1024)S(1)} %bitcast.563, bf16[1024,1024]{1,0:T(8,128)(2,1)S(1)} %bitcast.396, bf16[2048,1024]{1,0:T(8,128)(2,1)} %bitcast.534), kind=kOutput, calls=%fused_computation.9 | convolution fusion | flops 4347394048 | bytes 23085056 | tf_op jit(solution)/shard_map/dot_general | solution.py:348
  268.6 4.5 fusion.62
  274.4 4.5 fusion.61
  281.8 4.9 flip_after.1.normed_ref
  288.3 5.5 half_grad.5
  293.9 5.6 half_grad.4
  314.1 22.5 %attend_back.4 = (bf16[6,512,512]{2,1,0:T(8,128)(2,1)}, bf16[6,512,512]{2,1,0:T(8,128)(2,1)}, f32[512,1024]{1,0:T(8,128)}, f32[1024,128]{1,0:T(8,128)S(1)}, f32[...) custom-call(s32[5]{0:T(128)S(1)} %stack.79.bits_ref.refs_0_, ...), custom_call_target="tpu_custom_call", output_to_operand_aliasing={{0}: (15, {}), {1}: (16, {})} | custom-call | flops 1024 | bytes 1024 | tf_op jit(solution)/shard_map/attend_back/pallas_call | solution.py:628
  345.2 23.0 %attend_back.5 = (bf16[6,512,512]{2,1,0:T(8,128)(2,1)}, bf16[6,512,512]{2,1,0:T(8,128)(2,1)}, f32[512,1024]{1,0:T(8,128)}, f32[1024,128]{1,0:T(8,128)S(1)}, f32[...) custom-call(s32[5]{0:T(128)S(1)} %stack.79.bits_ref.refs_0_, ...), custom_call_target="tpu_custom_call", output_to_operand_aliasing={{2}: (15, {}), {3}: (16, {}), {4}: (17, {}), {0}: (18, {}),... | custom-call | flops 1024 | bytes 1024 | tf_op jit(solution)/shard_map/attend_back/pallas_call | solution.py:628
  371.9 5.5 copy.117
  382.0 4.4 half_grad.7
  387.7 4.4 half_grad.6
  393.5 23.1 %attend_back.6 = (bf16[4,512,512]{2,1,0:T(8,128)(2,1)}, bf16[4,512,512]{2,1,0:T(8,128)(2,1)}, f32[512,1024]{1,0:T(8,128)}, f32[1024,128]{1,0:T(8,128)S(1)}, f32[...) custom-call(s32[5]{0:T(128)S(1)} %stack.79.bits_ref.refs_0_, ...), custom_call_target="tpu_custom_call", output_to_operand_aliasing={{2}: (15, {}), {3}: (16, {}), {4}: (17, {})} | custom-call | flops 1024 | bytes 1024 | tf_op jit(solution)/shard_map/attend_back/pallas_call | solution.py:628
  419.5 9.0 %add_and_split.27 = (bf16[1,1,512,1024]{3,2,1,0:T(8,128)(2,1)}, bf16[1,1,512,1024]{3,2,1,0:T(8,128)(2,1)}, bf16[1,1,512,1024]{3,2,1,0:T(8,128)(2,1)}, bf16[1,1,5...) custom-call(s32[5]{0:T(128)S(1)} %stack.79.bits_ref.refs_0_, ...), custom_call_target="tpu_custom_call" | custom-call | flops 1024 | bytes 1024 | tf_op jit(solution)/shard_map/add_and_split/pallas_call | solution.py:977
  431.0 23.3 %attend_back.7 = (bf16[4,512,512]{2,1,0:T(8,128)(2,1)}, bf16[4,512,512]{2,1,0:T(8,128)(2,1)}, f32[512,1024]{1,0:T(8,128)}, f32[1024,128]{1,0:T(8,128)S(1)}, f32[...) custom-call(s32[5]{0:T(128)S(1)} %stack.79.bits_ref.refs_0_, ...), custom_call_target="tpu_custom_call", output_to_operand_aliasing={{2}: (15, {}), {3}: (16, {}), {4}: (17, {}), {0}: (18, {}),... | custom-call | flops 1024 | bytes 1024 | tf_op jit(solution)/shard_map/attend_back/pallas_call | solution.py:628
  461.0 17.2 %collective-permute-done.37 = bf16[3,256,512]{2,1,0:T(8,128)(2,1)S(1)} collective-permute-done((bf16[3,256,512]{2,1,0:T(8,128)(2,1)}, bf16[3,256,512]{2,1,0:T(8,128)(2,1)S(1)}, u32[]{:S(2)}, u32[]{:S(2)}) %collective-permute-start.37) | collective-permute-done | bytes 786464 | tf_op jit(solution)/shard_map/ppermute | solution.py:359
  484.4 4.4 add_and_split.28
  497.6 6.9 collective-permute-done.40
  505.4 11.2 %collective-permute-done.39 = bf16[2,256,1024]{2,1,0:T(8,128)(2,1)S(1)} collective-permute-done((bf16[2,256,1024]{2,1,0:T(8,128)(2,1)}, bf16[2,256,1024]{2,1,0:T(8,128)(2,1)S(1)}, u32[]{:S(2)}, u32[]{:S(2)}) %collective-permute-start.39) | collective-permute-done | bytes 1048608 | tf_op jit(solution)/shard_map/ppermute | solution.py:359
  530.5 7.6 %collective-permute-done.48.refs_9_ = f32[1,96,128]{2,1,0:T(8,128)S(1)} collective-permute-done((f32[1,96,128]{2,1,0:T(8,128)S(1)}, f32[1,96,128]{2,1,0:T(8,128)S(1)}, u32[]{:S(2)}, u32[]{:S(2)}) %collective-permute-start.48) | collective-permute-done | bytes 49184 | tf_op jit(solution)/shard_map/ppermute | solution.py:359
  538.1 5.2 collective-permute-done.45
  552.4 9.8 %collective-permute-done.51.refs_5_ = bf16[6,32,512]{2,1,0:T(8,128)(2,1)S(1)} collective-permute-done((bf16[6,32,512]{2,1,0:T(8,128)(2,1)S(1)}, bf16[6,32,512]{2,1,0:T(8,128)(2,1)S(1)}, u32[]{:S(2)}, u32[]{:S(2)}) %collective-permute-start.51) | collective-permute-done | bytes 196640 | tf_op jit(solution)/shard_map/ppermute | solution.py:359
  571.2 8.4 %collective-permute-done.59.refs_11_ = bf16[1,384,256]{2,1,0:T(8,128)(2,1)S(1)} collective-permute-done((bf16[1,384,256]{2,1,0:T(8,128)(2,1)S(1)}, bf16[1,384,256]{2,1,0:T(8,128)(2,1)S(1)}, u32[]{:S(2)}, u32[]{:S(2)}) %collective-permute-start.59) | collective-permute-done | bytes 196640 | tf_op jit(solution)/shard_map/ppermute | solution.py:359
  593.9 8.8 %collective-permute-done.63.refs_7_ = f32[1,96,128]{2,1,0:T(8,128)S(1)} collective-permute-done((f32[1,96,128]{2,1,0:T(8,128)S(1)}, f32[1,96,128]{2,1,0:T(8,128)S(1)}, u32[]{:S(2)}, u32[]{:S(2)}) %collective-permute-start.63) | collective-permute-done | bytes 49184 | tf_op jit(solution)/shard_map/ppermute | solution.py:359
  604.0 4.1 add_and_split.33
  618.6 5.3 collective-permute-done.67
  634.2 6.4 collective-permute-done.72
  640.6 8.4 %collective-permute-done.71 = bf16[3,256,512]{2,1,0:T(8,128)(2,1)S(1)} collective-permute-done((bf16[3,256,512]{2,1,0:T(8,128)(2,1)S(1)}, bf16[3,256,512]{2,1,0:T(8,128)(2,1)S(1)}, u32[]{:S(2)}, u32[]{:S(2)}) %collective-permute-start.71) | collective-permute-done | bytes 786464 | tf_op jit(solution)/shard_map/ppermute | solution.py:359
  656.1 4.4 collective-permute-start.33
  674.2 11.0 %collective-permute-done.32.refs_2_ = bf16[128,1024]{1,0:T(8,128)(2,1)S(1)} collective-permute-done((bf16[128,1024]{1,0:T(8,128)(2,1)S(1)}, bf16[128,1024]{1,0:T(8,128)(2,1)S(1)}, u32[]{:S(2)}, u32[]{:S(2)}) %collective-permute-start.32) | collective-permute-done | bytes 262176 | tf_op jit(solution)/shard_map/ppermute | solution.py:1081
  707.9 5.3 copy.121
  713.2 4.1 bitcast_convert_fusion.1
  722.6 7.1 finish.2
  729.7 5.4 finish.3
  (514 shorter events, 276.8 us)
Async XLA Ops:
  7.2 364.7 %all-gather.2.cloned.1.call-start = ((), (), s32[]{:S(2)}) async-start(), calls=%async_computation | async-start | bytes 5242880 | tf_op jit(solution)/shard_map/all_gather | solution.py:1135
  36.2 42.0 %collective-permute-start.3 = (bf16[384,1024]{1,0:T(8,128)(2,1)}, bf16[384,1024]{1,0:T(8,128)(2,1)}, u32[]{:S(2)}, u32[]{:S(2)}) collective-permute-start(bf16[384,1024]{1,0:T(8,128)(2,1)} %get-tuple-element.316), channel_id=1, source_target_pairs={{0,3},{1,0},{2,1},{3,2},{4,7},{5,4},{6,5},{7,6},{8,11},{9,8},{10,9... | collective-permute-start | bytes 2359304 | tf_op jit(solution)/shard_map/ppermute | solution.py:1081
  39.0 75.4 %collective-permute-start.2 = (bf16[384,1024]{1,0:T(8,128)(2,1)}, bf16[384,1024]{1,0:T(8,128)(2,1)}, u32[]{:S(2)}, u32[]{:S(2)}) collective-permute-start(bf16[384,1024]{1,0:T(8,128)(2,1)} %get-tuple-element.317), channel_id=1, source_target_pairs={{0,2},{1,3},{2,0},{3,1},{4,6},{5,7},{6,4},{7,5},{8,10},{9,11},{10,... | collective-permute-start | bytes 2359304 | tf_op jit(solution)/shard_map/ppermute | solution.py:1081
  39.5 74.9 %collective-permute-start.1 = (bf16[384,1024]{1,0:T(8,128)(2,1)}, bf16[384,1024]{1,0:T(8,128)(2,1)}, u32[]{:S(2)}, u32[]{:S(2)}) collective-permute-start(bf16[384,1024]{1,0:T(8,128)(2,1)} %get-tuple-element.318), channel_id=1, source_target_pairs={{0,1},{1,2},{2,3},{3,0},{4,5},{5,6},{6,7},{7,4},{8,9},{9,10},{10,1... | collective-permute-start | bytes 2359304 | tf_op jit(solution)/shard_map/ppermute | solution.py:1081
  43.5 19.5 %collective-permute-start.6 = (bf16[1,512,512]{2,1,0:T(8,128)(2,1)}, bf16[1,512,512]{2,1,0:T(8,128)(2,1)}, u32[]{:S(2)}, u32[]{:S(2)}) collective-permute-start(bf16[1,512,512]{2,1,0:T(8,128)(2,1)} %bitcast.33), channel_id=1, source_target_pairs={{0,8},{4,12},{8,0},{12,4},{16,24},{20,28},{24,16},{28,20},{1,9},{5... | collective-permute-start | bytes 1572872 | tf_op jit(solution)/shard_map/ppermute | solution.py:359
  63.0 61.7 %collective-permute-start.7 = (bf16[2,128,512]{2,1,0:T(8,128)(2,1)S(1)}, bf16[2,128,512]{2,1,0:T(8,128)(2,1)S(1)}, u32[]{:S(2)}, u32[]{:S(2)}) collective-permute-start(bf16[2,128,512]{2,1,0:T(8,128)(2,1)S(1)} %bitcast.413), channel_id=1, source_target_pairs={{0,2},{1,3},{2,0},{3,1},{4,6},{5,7},{6,4},{7,5},{8,10},{9,11},{10,... | collective-permute-start | bytes 786440 | tf_op jit(solution)/shard_map/ppermute | solution.py:359
  76.7 109.1 %collective-permute-start.16 = (bf16[1,1024,512]{2,1,0:T(8,128)(2,1)}, bf16[1,1024,512]{2,1,0:T(8,128)(2,1)}, u32[]{:S(2)}, u32[]{:S(2)}) collective-permute-start(bf16[1,1024,512]{2,1,0:T(8,128)(2,1)} %bitcast.36.refs_7_), channel_id=1, source_target_pairs={{0,16},{4,20},{8,24},{12,28},{16,0},{20,4},{24,8},{28,12},{1,17},{... | collective-permute-start | bytes 3145736 | tf_op jit(solution)/shard_map/ppermute | solution.py:359
  78.2 107.6 %collective-permute-start.15 = (bf16[1,1024,512]{2,1,0:T(8,128)(2,1)}, bf16[1,1024,512]{2,1,0:T(8,128)(2,1)}, u32[]{:S(2)}, u32[]{:S(2)}) collective-permute-start(bf16[1,1024,512]{2,1,0:T(8,128)(2,1)} %bitcast.35.refs_6_), channel_id=1, source_target_pairs={{0,8},{4,12},{8,0},{12,4},{16,24},{20,28},{24,16},{28,20},{1,9},{5... | collective-permute-start | bytes 3145736 | tf_op jit(solution)/shard_map/ppermute | solution.py:359
  123.0 24.9 %collective-permute-start.14 = (bf16[1,512]{1,0:T(2,128)(2,1)S(1)}, bf16[1,512]{1,0:T(2,128)(2,1)S(1)}, u32[]{:S(2)}, u32[]{:S(2)}) collective-permute-start(bf16[1,512]{1,0:T(2,128)(2,1)S(1)} %constant_dynamic-slice_fusion.3), channel_id=1, source_target_pairs={{0,2},{1,3},{2,0},{3,1},{4,6},{5,7},{6,4},{7,5},{8,10},{9,11},{10,... | collective-permute-start | bytes 3080 | tf_op jit(solution)/shard_map/ppermute | solution.py:359
  127.1 19.2 %collective-permute-start.8 = (bf16[2,256,512]{2,1,0:T(8,128)(2,1)S(1)}, bf16[2,256,512]{2,1,0:T(8,128)(2,1)S(1)}, u32[]{:S(2)}, u32[]{:S(2)}) collective-permute-start(bf16[2,256,512]{2,1,0:T(8,128)(2,1)S(1)} %bitcast.418), channel_id=1, source_target_pairs={{0,1},{1,0},{2,3},{3,2},{4,5},{5,4},{6,7},{7,6},{8,9},{9,8},{10,11... | collective-permute-start | bytes 1572872 | tf_op jit(solution)/shard_map/ppermute | solution.py:359
  132.3 17.1 %collective-permute-start.11 = (bf16[128,1024]{1,0:T(8,128)(2,1)S(1)}, bf16[128,1024]{1,0:T(8,128)(2,1)S(1)}, u32[]{:S(2)}, u32[]{:S(2)}) collective-permute-start(bf16[128,1024]{1,0:T(8,128)(2,1)S(1)} %bitcast.423), channel_id=1, source_target_pairs={{0,1},{1,2},{2,3},{3,0},{4,5},{5,6},{6,7},{7,4},{8,9},{9,10},{10,1... | collective-permute-start | bytes 786440 | tf_op jit(solution)/shard_map/ppermute | solution.py:1081
  147.9 42.6 %collective-permute-start.10 = (bf16[1,512,512]{2,1,0:T(8,128)(2,1)}, bf16[1,512,512]{2,1,0:T(8,128)(2,1)}, u32[]{:S(2)}, u32[]{:S(2)}) collective-permute-start(bf16[1,512,512]{2,1,0:T(8,128)(2,1)} %bitcast.50.rest_1_), channel_id=1, source_target_pairs={{0,8},{4,12},{8,0},{12,4},{16,24},{20,28},{24,16},{28,20},{1,9},{5... | collective-permute-start | bytes 1572872 | tf_op jit(solution)/shard_map/ppermute | solution.py:359
  149.4 41.1 %collective-permute-start.9 = (bf16[1,512,512]{2,1,0:T(8,128)(2,1)}, bf16[1,512,512]{2,1,0:T(8,128)(2,1)}, u32[]{:S(2)}, u32[]{:S(2)}) collective-permute-start(bf16[1,512,512]{2,1,0:T(8,128)(2,1)} %bitcast.49.rest_0_), channel_id=1, source_target_pairs={{0,16},{4,20},{8,24},{12,28},{16,0},{20,4},{24,8},{28,12},{1,17},{... | collective-permute-start | bytes 1572872 | tf_op jit(solution)/shard_map/ppermute | solution.py:359
  158.6 24.2 %collective-permute-start.13 = (bf16[128,1024]{1,0:T(8,128)(2,1)S(1)}, bf16[128,1024]{1,0:T(8,128)(2,1)S(1)}, u32[]{:S(2)}, u32[]{:S(2)}) collective-permute-start(bf16[128,1024]{1,0:T(8,128)(2,1)S(1)} %bitcast.427), channel_id=1, source_target_pairs={{0,3},{1,0},{2,1},{3,2},{4,7},{5,4},{6,5},{7,6},{8,11},{9,8},{10,9... | collective-permute-start | bytes 786440 | tf_op jit(solution)/shard_map/ppermute | solution.py:1081
  185.8 42.6 %collective-permute-start.25 = (bf16[512,1024]{1,0:T(8,128)(2,1)}, bf16[512,1024]{1,0:T(8,128)(2,1)}, u32[]{:S(2)}, u32[]{:S(2)}) collective-permute-start(bf16[512,1024]{1,0:T(8,128)(2,1)} %bitcast.524), channel_id=1, source_target_pairs={{0,4},{4,0},{8,12},{12,8},{16,20},{20,16},{24,28},{28,24},{1,5},{5... | collective-permute-start | bytes 3145736 | tf_op jit(solution)/shard_map/ppermute | solution.py:359
  225.4 24.2 %collective-permute-start.20 = (bf16[1,1024,512]{2,1,0:T(8,128)(2,1)}, bf16[1,1024,512]{2,1,0:T(8,128)(2,1)}, u32[]{:S(2)}, u32[]{:S(2)}) collective-permute-start(bf16[1,1024,512]{2,1,0:T(8,128)(2,1)} %bitcast.60.rest_3_), channel_id=1, source_target_pairs={{0,16},{4,20},{8,24},{12,28},{16,0},{20,4},{24,8},{28,12},{1,17},{... | collective-permute-start | bytes 3145736 | tf_op jit(solution)/shard_map/ppermute | solution.py:359
  226.9 24.0 %collective-permute-start.19 = (bf16[1,1024,512]{2,1,0:T(8,128)(2,1)}, bf16[1,1024,512]{2,1,0:T(8,128)(2,1)}, u32[]{:S(2)}, u32[]{:S(2)}) collective-permute-start(bf16[1,1024,512]{2,1,0:T(8,128)(2,1)} %bitcast.59.rest_2_), channel_id=1, source_target_pairs={{0,8},{4,12},{8,0},{12,4},{16,24},{20,28},{24,16},{28,20},{1,9},{5... | collective-permute-start | bytes 3145736 | tf_op jit(solution)/shard_map/ppermute | solution.py:359
  274.4 25.1 %collective-permute-start.26 = (bf16[512,1024]{1,0:T(8,128)(2,1)}, bf16[512,1024]{1,0:T(8,128)(2,1)}, u32[]{:S(2)}, u32[]{:S(2)}) collective-permute-start(bf16[512,1024]{1,0:T(8,128)(2,1)} %fusion.44), channel_id=1, source_target_pairs={{0,4},{4,0},{8,12},{12,8},{16,20},{20,16},{24,28},{28,24},{1,5},{5... | collective-permute-start | bytes 3145736 | tf_op jit(solution)/shard_map/ppermute | solution.py:359
  281.3 20.5 %collective-permute-start.21 = (bf16[512,1024]{1,0:T(8,128)(2,1)}, bf16[512,1024]{1,0:T(8,128)(2,1)}, u32[]{:S(2)}, u32[]{:S(2)}) collective-permute-start(bf16[512,1024]{1,0:T(8,128)(2,1)} %fusion.43), channel_id=1, source_target_pairs={{0,4},{4,0},{8,12},{12,8},{16,20},{20,16},{24,28},{28,24},{1,5},{5... | collective-permute-start | bytes 3145736 | tf_op jit(solution)/shard_map/ppermute | solution.py:359
  305.5 32.7 %collective-permute-start.24 = (bf16[128,1024]{1,0:T(8,128)(2,1)S(1)}, bf16[128,1024]{1,0:T(8,128)(2,1)S(1)}, u32[]{:S(2)}, u32[]{:S(2)}) collective-permute-start(bf16[128,1024]{1,0:T(8,128)(2,1)S(1)} %get-tuple-element.333.rest_6_), channel_id=1, source_target_pairs={{0,3},{1,0},{2,1},{3,2},{4,7},{5,4},{6,5},{7,6},{8,11},{9,8},{10,9... | collective-permute-start | bytes 786440 | tf_op jit(solution)/shard_map/ppermute | solution.py:1081
  306.2 32.1 %collective-permute-start.23 = (bf16[128,1024]{1,0:T(8,128)(2,1)S(1)}, bf16[128,1024]{1,0:T(8,128)(2,1)S(1)}, u32[]{:S(2)}, u32[]{:S(2)}) collective-permute-start(bf16[128,1024]{1,0:T(8,128)(2,1)S(1)} %get-tuple-element.334.rest_5_), channel_id=1, source_target_pairs={{0,2},{1,3},{2,0},{3,1},{4,6},{5,7},{6,4},{7,5},{8,10},{9,11},{10,... | collective-permute-start | bytes 786440 | tf_op jit(solution)/shard_map/ppermute | solution.py:1081
  307.9 30.4 %collective-permute-start.22 = (bf16[128,1024]{1,0:T(8,128)(2,1)S(1)}, bf16[128,1024]{1,0:T(8,128)(2,1)S(1)}, u32[]{:S(2)}, u32[]{:S(2)}) collective-permute-start(bf16[128,1024]{1,0:T(8,128)(2,1)S(1)} %get-tuple-element.335.rest_4_), channel_id=1, source_target_pairs={{0,1},{1,2},{2,3},{3,0},{4,5},{5,6},{6,7},{7,4},{8,9},{9,10},{10,1... | collective-permute-start | bytes 786440 | tf_op jit(solution)/shard_map/ppermute | solution.py:1081
  369.9 49.6 %collective-permute-start.30 = (bf16[6,512,512]{2,1,0:T(8,128)(2,1)}, bf16[6,512,512]{2,1,0:T(8,128)(2,1)}, u32[]{:S(2)}, u32[]{:S(2)}) collective-permute-start(bf16[6,512,512]{2,1,0:T(8,128)(2,1)} %get-tuple-element.158.rest_3_), channel_id=1, source_target_pairs={{0,4},{4,0},{8,12},{12,8},{16,20},{20,16},{24,28},{28,24},{1,5},{5... | collective-permute-start | bytes 9437192 | tf_op jit(solution)/shard_map/ppermute | solution.py:359
  369.9 48.4 %collective-permute-start.27 = (bf16[1,1024,1024]{2,1,0:T(8,128)(2,1)}, bf16[1,1024,1024]{2,1,0:T(8,128)(2,1)}, u32[]{:S(2)}, u32[]{:S(2)}) collective-permute-start(bf16[1,1024,1024]{2,1,0:T(8,128)(2,1)} %bitcast.92.rest_2_), channel_id=1, source_target_pairs={{0,8},{4,12},{8,0},{12,4},{16,24},{20,28},{24,16},{28,20},{1,9},{5... | collective-permute-start | bytes 6291464 | tf_op jit(solution)/shard_map/ppermute | solution.py:359
  371.4 48.1 %collective-permute-start.28 = (bf16[1,1024,1024]{2,1,0:T(8,128)(2,1)}, bf16[1,1024,1024]{2,1,0:T(8,128)(2,1)}, u32[]{:S(2)}, u32[]{:S(2)}) collective-permute-start(bf16[1,1024,1024]{2,1,0:T(8,128)(2,1)} %bitcast.93.rest_3_), channel_id=1, source_target_pairs={{0,16},{4,20},{8,24},{12,28},{16,0},{20,4},{24,8},{28,12},{1,17},{... | collective-permute-start | bytes 6291464 | tf_op jit(solution)/shard_map/ppermute | solution.py:359
  380.6 38.9 %collective-permute-start.29 = (bf16[1,1536,256]{2,1,0:T(8,128)(2,1)S(1)}, bf16[1,1536,256]{2,1,0:T(8,128)(2,1)S(1)}, u32[]{:S(2)}, u32[]{:S(2)}) collective-permute-start(bf16[1,1536,256]{2,1,0:T(8,128)(2,1)S(1)} %get-tuple-element.328.rest_4_), channel_id=1, source_target_pairs={{0,4},{4,0},{8,12},{12,8},{16,20},{20,16},{24,28},{28,24},{1,5},{5... | collective-permute-start | bytes 2359304 | tf_op jit(solution)/shard_map/ppermute | solution.py:359
  428.5 28.0 %collective-permute-start.36 = (bf16[1,768,256]{2,1,0:T(8,128)(2,1)S(1)}, bf16[1,768,256]{2,1,0:T(8,128)(2,1)S(1)}, u32[]{:S(2)}, u32[]{:S(2)}) collective-permute-start(bf16[1,768,256]{2,1,0:T(8,128)(2,1)S(1)} %bitcast.456), channel_id=1, source_target_pairs={{0,8},{4,12},{8,0},{12,4},{16,24},{20,28},{24,16},{28,20},{1,9},{5... | collective-permute-start | bytes 1179656 | tf_op jit(solution)/shard_map/ppermute | solution.py:359
  429.0 51.0 %collective-permute-start.35 = (bf16[1,512,1024]{2,1,0:T(8,128)(2,1)}, bf16[1,512,1024]{2,1,0:T(8,128)(2,1)}, u32[]{:S(2)}, u32[]{:S(2)}) collective-permute-start(bf16[1,512,1024]{2,1,0:T(8,128)(2,1)} %bitcast.549), channel_id=1, source_target_pairs={{0,8},{4,12},{8,0},{12,4},{16,24},{20,28},{24,16},{28,20},{1,9},{5... | collective-permute-start | bytes 3145736 | tf_op jit(solution)/shard_map/ppermute | solution.py:359
  430.5 49.5 %collective-permute-start.34 = (bf16[1,512,1024]{2,1,0:T(8,128)(2,1)}, bf16[1,512,1024]{2,1,0:T(8,128)(2,1)}, u32[]{:S(2)}, u32[]{:S(2)}) collective-permute-start(bf16[1,512,1024]{2,1,0:T(8,128)(2,1)} %bitcast.547), channel_id=1, source_target_pairs={{0,16},{4,20},{8,24},{12,28},{16,0},{20,4},{24,8},{28,12},{1,17},{... | collective-permute-start | bytes 3145736 | tf_op jit(solution)/shard_map/ppermute | solution.py:359
  455.9 60.7 %collective-permute-start.42 = (bf16[4,512,512]{2,1,0:T(8,128)(2,1)}, bf16[4,512,512]{2,1,0:T(8,128)(2,1)}, u32[]{:S(2)}, u32[]{:S(2)}) collective-permute-start(bf16[4,512,512]{2,1,0:T(8,128)(2,1)} %get-tuple-element.185), channel_id=1, source_target_pairs={{0,4},{4,0},{8,12},{12,8},{16,20},{20,16},{24,28},{28,24},{1,5},{5... | collective-permute-start | bytes 6291464 | tf_op jit(solution)/shard_map/ppermute | solution.py:359
  455.9 22.3 %collective-permute-start.37 = (bf16[3,256,512]{2,1,0:T(8,128)(2,1)}, bf16[3,256,512]{2,1,0:T(8,128)(2,1)S(1)}, u32[]{:S(2)}, u32[]{:S(2)}) collective-permute-start(bf16[3,256,512]{2,1,0:T(8,128)(2,1)} %bitcast.114.rest_8_), channel_id=1, source_target_pairs={{0,8},{4,12},{8,0},{12,4},{16,24},{20,28},{24,16},{28,20},{1,9},{5... | collective-permute-start | bytes 2359304 | tf_op jit(solution)/shard_map/ppermute | solution.py:359
  457.2 21.9 %collective-permute-start.38 = (bf16[3,256,512]{2,1,0:T(8,128)(2,1)}, bf16[3,256,512]{2,1,0:T(8,128)(2,1)S(1)}, u32[]{:S(2)}, u32[]{:S(2)}) collective-permute-start(bf16[3,256,512]{2,1,0:T(8,128)(2,1)} %bitcast.115.rest_9_), channel_id=1, source_target_pairs={{0,16},{4,20},{8,24},{12,28},{16,0},{20,4},{24,8},{28,12},{1,17},{... | collective-permute-start | bytes 2359304 | tf_op jit(solution)/shard_map/ppermute | solution.py:359
  492.5 24.1 %collective-permute-start.39 = (bf16[2,256,1024]{2,1,0:T(8,128)(2,1)}, bf16[2,256,1024]{2,1,0:T(8,128)(2,1)S(1)}, u32[]{:S(2)}, u32[]{:S(2)}) collective-permute-start(bf16[2,256,1024]{2,1,0:T(8,128)(2,1)} %bitcast.569), channel_id=1, source_target_pairs={{0,1},{1,0},{2,3},{3,2},{4,5},{5,4},{6,7},{7,6},{8,9},{9,8},{10,11... | collective-permute-start | bytes 3145736 | tf_op jit(solution)/shard_map/ppermute | solution.py:359
  523.3 23.9 %collective-permute-start.44 = (bf16[2,128,1024]{2,1,0:T(8,128)(2,1)S(1)}, bf16[2,128,1024]{2,1,0:T(8,128)(2,1)S(1)}, u32[]{:S(2)}, u32[]{:S(2)}) collective-permute-start(bf16[2,128,1024]{2,1,0:T(8,128)(2,1)S(1)} %bitcast.514), channel_id=1, source_target_pairs={{0,2},{1,3},{2,0},{3,1},{4,6},{5,7},{6,4},{7,5},{8,10},{9,11},{10,... | collective-permute-start | bytes 1572872 | tf_op jit(solution)/shard_map/ppermute | solution.py:359
  526.0 21.2 %collective-permute-start.46 = (bf16[2,256,512]{2,1,0:T(8,128)(2,1)S(1)}, bf16[2,256,512]{2,1,0:T(8,128)(2,1)S(1)}, u32[]{:S(2)}, u32[]{:S(2)}) collective-permute-start(bf16[2,256,512]{2,1,0:T(8,128)(2,1)S(1)} %bitcast.513), channel_id=1, source_target_pairs={{0,8},{4,12},{8,0},{12,4},{16,24},{20,28},{24,16},{28,20},{1,9},{5... | collective-permute-start | bytes 1572872 | tf_op jit(solution)/shard_map/ppermute | solution.py:359
  526.7 20.5 %collective-permute-start.47 = (bf16[2,256,512]{2,1,0:T(8,128)(2,1)S(1)}, bf16[2,256,512]{2,1,0:T(8,128)(2,1)S(1)}, u32[]{:S(2)}, u32[]{:S(2)}) collective-permute-start(bf16[2,256,512]{2,1,0:T(8,128)(2,1)S(1)} %bitcast.512), channel_id=1, source_target_pairs={{0,16},{4,20},{8,24},{12,28},{16,0},{20,4},{24,8},{28,12},{1,17},{... | collective-permute-start | bytes 1572872 | tf_op jit(solution)/shard_map/ppermute | solution.py:359
  563.3 20.5 %collective-permute-start.55 = (bf16[1,256,1024]{2,1,0:T(8,128)(2,1)S(1)}, bf16[1,256,1024]{2,1,0:T(8,128)(2,1)S(1)}, u32[]{:S(2)}, u32[]{:S(2)}) collective-permute-start(bf16[1,256,1024]{2,1,0:T(8,128)(2,1)S(1)} %bitcast.449), channel_id=1, source_target_pairs={{0,16},{4,20},{8,24},{12,28},{16,0},{20,4},{24,8},{28,12},{1,17},{... | collective-permute-start | bytes 1572872 | tf_op jit(solution)/shard_map/ppermute | solution.py:359
  564.6 19.1 %collective-permute-start.54 = (bf16[1,256,1024]{2,1,0:T(8,128)(2,1)S(1)}, bf16[1,256,1024]{2,1,0:T(8,128)(2,1)S(1)}, u32[]{:S(2)}, u32[]{:S(2)}) collective-permute-start(bf16[1,256,1024]{2,1,0:T(8,128)(2,1)S(1)} %bitcast.448), channel_id=1, source_target_pairs={{0,8},{4,12},{8,0},{12,4},{16,24},{20,28},{24,16},{28,20},{1,9},{5... | collective-permute-start | bytes 1572872 | tf_op jit(solution)/shard_map/ppermute | solution.py:359
  565.7 18.0 %collective-permute-start.57 = (bf16[4,64,512]{2,1,0:T(8,128)(2,1)S(1)}, bf16[4,64,512]{2,1,0:T(8,128)(2,1)S(1)}, u32[]{:S(2)}, u32[]{:S(2)}) collective-permute-start(bf16[4,64,512]{2,1,0:T(8,128)(2,1)S(1)} %bitcast.518), channel_id=1, source_target_pairs={{0,1},{1,0},{2,3},{3,2},{4,5},{5,4},{6,7},{7,6},{8,9},{9,8},{10,11... | collective-permute-start | bytes 786440 | tf_op jit(solution)/shard_map/ppermute | solution.py:359
  609.2 18.2 %collective-permute-start.66 = (bf16[3,128,512]{2,1,0:T(8,128)(2,1)S(1)}, bf16[3,128,512]{2,1,0:T(8,128)(2,1)S(1)}, u32[]{:S(2)}, u32[]{:S(2)}) collective-permute-start(bf16[3,128,512]{2,1,0:T(8,128)(2,1)S(1)} %bitcast.471), channel_id=1, source_target_pairs={{0,8},{4,12},{8,0},{12,4},{16,24},{20,28},{24,16},{28,20},{1,9},{5... | collective-permute-start | bytes 1179656 | tf_op jit(solution)/shard_map/ppermute | solution.py:359
  610.1 17.3 %collective-permute-start.65 = (bf16[3,128,512]{2,1,0:T(8,128)(2,1)S(1)}, bf16[3,128,512]{2,1,0:T(8,128)(2,1)S(1)}, u32[]{:S(2)}, u32[]{:S(2)}) collective-permute-start(bf16[3,128,512]{2,1,0:T(8,128)(2,1)S(1)} %bitcast.469), channel_id=1, source_target_pairs={{0,16},{4,20},{8,24},{12,28},{16,0},{20,4},{24,8},{28,12},{1,17},{... | collective-permute-start | bytes 1179656 | tf_op jit(solution)/shard_map/ppermute | solution.py:359
  629.0 20.0 %collective-permute-start.71 = (bf16[3,256,512]{2,1,0:T(8,128)(2,1)S(1)}, bf16[3,256,512]{2,1,0:T(8,128)(2,1)S(1)}, u32[]{:S(2)}, u32[]{:S(2)}) collective-permute-start(bf16[3,256,512]{2,1,0:T(8,128)(2,1)S(1)} %bitcast.435), channel_id=1, source_target_pairs={{0,16},{4,20},{8,24},{12,28},{16,0},{20,4},{24,8},{28,12},{1,17},{... | collective-permute-start | bytes 2359304 | tf_op jit(solution)/shard_map/ppermute | solution.py:359
  630.2 19.7 %collective-permute-start.70 = (bf16[3,256,512]{2,1,0:T(8,128)(2,1)S(1)}, bf16[3,256,512]{2,1,0:T(8,128)(2,1)S(1)}, u32[]{:S(2)}, u32[]{:S(2)}) collective-permute-start(bf16[3,256,512]{2,1,0:T(8,128)(2,1)S(1)} %bitcast.434), channel_id=1, source_target_pairs={{0,8},{4,12},{8,0},{12,4},{16,24},{20,28},{24,16},{28,20},{1,9},{5... | collective-permute-start | bytes 2359304 | tf_op jit(solution)/shard_map/ppermute | solution.py:359
  654.0 68.5 %collective-permute-start.79 = (bf16[6,512,512]{2,1,0:T(8,128)(2,1)}, bf16[6,512,512]{2,1,0:T(8,128)(2,1)}, u32[]{:S(2)}, u32[]{:S(2)}) collective-permute-start(bf16[6,512,512]{2,1,0:T(8,128)(2,1)} %bitcast.411), channel_id=1, source_target_pairs={{0,4},{4,0},{8,12},{12,8},{16,20},{20,16},{24,28},{28,24},{1,5},{5... | collective-permute-start | bytes 9437192 | tf_op jit(solution)/shard_map/ppermute | solution.py:359
  664.2 24.8 %collective-permute-start.77 = (bf16[2,256,512]{2,1,0:T(8,128)(2,1)S(1)}, bf16[2,256,512]{2,1,0:T(8,128)(2,1)S(1)}, u32[]{:S(2)}, u32[]{:S(2)}) collective-permute-start(bf16[2,256,512]{2,1,0:T(8,128)(2,1)S(1)} %bitcast.453), channel_id=1, source_target_pairs={{0,16},{4,20},{8,24},{12,28},{16,0},{20,4},{24,8},{28,12},{1,17},{... | collective-permute-start | bytes 1572872 | tf_op jit(solution)/shard_map/ppermute | solution.py:359
  665.2 24.5 %collective-permute-start.76 = (bf16[2,256,512]{2,1,0:T(8,128)(2,1)S(1)}, bf16[2,256,512]{2,1,0:T(8,128)(2,1)S(1)}, u32[]{:S(2)}, u32[]{:S(2)}) collective-permute-start(bf16[2,256,512]{2,1,0:T(8,128)(2,1)S(1)} %bitcast.452), channel_id=1, source_target_pairs={{0,8},{4,12},{8,0},{12,4},{16,24},{20,28},{24,16},{28,20},{1,9},{5... | collective-permute-start | bytes 1572872 | tf_op jit(solution)/shard_map/ppermute | solution.py:359
  666.1 19.2 %collective-permute-start.32 = (bf16[128,1024]{1,0:T(8,128)(2,1)S(1)}, bf16[128,1024]{1,0:T(8,128)(2,1)S(1)}, u32[]{:S(2)}, u32[]{:S(2)}) collective-permute-start(bf16[128,1024]{1,0:T(8,128)(2,1)S(1)} %get-tuple-element.330.refs_12_), channel_id=1, source_target_pairs={{0,2},{1,3},{2,0},{3,1},{4,6},{5,7},{6,4},{7,5},{8,10},{9,11},{10,... | collective-permute-start | bytes 786440 | tf_op jit(solution)/shard_map/ppermute | solution.py:1081
  694.5 35.1 %collective-permute-start.78 = (bf16[4,512,512]{2,1,0:T(8,128)(2,1)S(1)}, bf16[4,512,512]{2,1,0:T(8,128)(2,1)}, u32[]{:S(2)}, u32[]{:S(2)}) collective-permute-start(bf16[4,512,512]{2,1,0:T(8,128)(2,1)S(1)} %bitcast.408), channel_id=1, source_target_pairs={{0,4},{4,0},{8,12},{12,8},{16,20},{20,16},{24,28},{28,24},{1,5},{5... | collective-permute-start | bytes 6291464 | tf_op jit(solution)/shard_map/ppermute | solution.py:359
  (160 other events, 1434.3 us)
Sparse Core Ops, SparseCore 0:
  228.5 77.1 all-gather.1

commit v2 on v1

--- a/solution.py
+++ b/solution.py
@@ -338,9 +338,10 @@
 
 BF16 = jnp.bfloat16
 F32 = jnp.float32
-QUERY_BLOCK = 256
-HEADS_A_CALL = 2
-VMEM_LIMIT = 48 * 1024 * 1024
+ATTEND_PARTS = 2
+BACK_PARTS = 1
+CALLS = (2, 2, 2, 2)
+MIB = 1024 * 1024
 SHORT = pl.CostEstimate(flops=1024, bytes_accessed=1024, transcendentals=0)
 
 
@@ -407,37 +408,39 @@
     len_ref, qc_ref, qp_ref, k_ref, v_ref, rel_ref, table_ref, cos_ref, sin_ref, *rest
 ):
     p_ref, o_ref = rest[-2:]
-    rows = qc_ref.shape[0]
+    rows = qc_ref.shape[0] // ATTEND_PARTS
     keys = k_ref.shape[0]
     half = cos_ref.shape[1]
     split = CMEM + MEM
-    mixed = contract(qp_ref[...], rel_ref[...], 1, 1)
-    lead, tail = mixed[:, :half], mixed[:, half:]
-    cos, sin = cos_ref[...], sin_ref[...]
-    rotated = jnp.concatenate(
-        [(lead * sin + tail * cos).astype(BF16), (tail * sin - lead * cos).astype(BF16)], 1
-    )
-    scores = contract(qc_ref[...], k_ref[...], 1, 1) + contract(rotated, table_ref[...], 1, 1)
-    scores = scores * (1.0 / math.sqrt(DH))
-    row_ids = pl.program_id(1) * rows + lax.broadcasted_iota(jnp.int32, (rows, keys - split), 0)
-    col_ids = lax.broadcasted_iota(jnp.int32, (rows, keys - split), 1)
-    visible = (col_ids <= row_ids) & (col_ids < len_ref[0])
-    past = scores[:, :split]
-    own = jnp.where(visible, scores[:, split:], -1e30)
-    top = jnp.maximum(jnp.max(past, 1, keepdims=True), jnp.max(own, 1, keepdims=True))
-    past = jnp.exp(past - top)
-    own = jnp.exp(own - top)
-    total = jnp.sum(past, 1, keepdims=True) + jnp.sum(own, 1, keepdims=True)
-    scale = 1.0 / total
-    prob = jnp.concatenate([(past * scale).astype(BF16), (own * scale).astype(BF16)], 1)
-    p_ref[0] = prob
-    o_ref[...] = jnp.dot(prob, v_ref[...], preferred_element_type=F32).astype(BF16)
+    for part in range(ATTEND_PARTS):
+        at = slice(part * rows, (part + 1) * rows)
+        mixed = contract(qp_ref[at], rel_ref[...], 1, 1)
+        lead, tail = mixed[:, :half], mixed[:, half:]
+        cos, sin = cos_ref[at], sin_ref[at]
+        rotated = jnp.concatenate(
+            [(lead * sin + tail * cos).astype(BF16), (tail * sin - lead * cos).astype(BF16)], 1
+        )
+        scores = contract(qc_ref[at], k_ref[...], 1, 1) + contract(rotated, table_ref[...], 1, 1)
+        row_ids = part * rows + lax.broadcasted_iota(jnp.int32, (rows, keys - split), 0)
+        col_ids = lax.broadcasted_iota(jnp.int32, (rows, keys - split), 1)
+        visible = (col_ids <= row_ids) & (col_ids < len_ref[0])
+        past = scores[:, :split]
+        own = jnp.where(visible, scores[:, split:], -1e30)
+        top = jnp.maximum(jnp.max(past, 1, keepdims=True), jnp.max(own, 1, keepdims=True))
+        factor = math.log2(math.e) / math.sqrt(DH)
+        past = jnp.exp2((past - top) * factor)
+        own = jnp.exp2((own - top) * factor)
+        total = jnp.sum(past, 1, keepdims=True) + jnp.sum(own, 1, keepdims=True)
+        scale = 1.0 / total
+        prob = jnp.concatenate([(past * scale).astype(BF16), (own * scale).astype(BF16)], 1)
+        p_ref[0, at] = prob
+        o_ref[at] = jnp.dot(prob, v_ref[...], preferred_element_type=F32).astype(BF16)
 
 
 def attend(heads, length, content, position, keys, values, w_rel, table, cos, sin, first=(), into=()):
     seg, width = content.shape
     total = keys.shape[0]
-    block = QUERY_BLOCK
+    block = seg
     start, count = heads.start, len(heads)
     head = lambda h, q: (0, start + h)
     rows = lambda h, q: (q, start + h)
@@ -469,7 +472,7 @@
             jax.ShapeDtypeStruct((seg, width), BF16),
         ],
         input_output_aliases=aliases,
-        compiler_params=pltpu.CompilerParams(vmem_limit_bytes=VMEM_LIMIT),
+        compiler_params=pltpu.CompilerParams(vmem_limit_bytes=52 * MIB),
         cost_estimate=SHORT,
         name="attend",
     )(*operands)
@@ -494,89 +497,79 @@
     sin_ref,
     *rest,
 ):
-    keep_ref, give_ref, rows_ref, along_ref, shift_ref, bias_ref = rest[-10:-4]
-    dk_sum, dv_sum, drel_sum, dq_all = rest[-4:]
-    head, step = pl.program_id(0), pl.program_id(1)
+    keep_ref, give_ref, rows_ref, along_ref, shift_ref, bias_ref = rest[-6:]
+    head = pl.program_id(0)
     scale = 1.0 / math.sqrt(DH)
     half = cos_ref.shape[1]
-    block = da_ref.shape[0]
-    seg = dq_all.shape[0]
-
-    @pl.when(step == 0)
+    seg = da_ref.shape[0]
+    past = k_ref.shape[0] - seg
+    block = seg // BACK_PARTS
+    dk_t = dv_t = drel_t = 0.0
+    d_content_sum = d_position_sum = 0.0
+    d_queries = []
+    for part in range(BACK_PARTS):
+        at = slice(part * block, (part + 1) * block)
+        prob = p_ref[0, at]
+        d_attn = da_ref[at]
+        dv_t = dv_t + contract(d_attn, prob, 0, 0)
+        d_prob = contract(d_attn, v_ref[...], 1, 1)
+        prob_f = prob.astype(F32)
+        weighted = prob_f * d_prob
+        inner = jnp.sum(weighted, 1, keepdims=True)
+        d_scores = (weighted - prob_f * inner).astype(BF16)
+        dk_t = dk_t + contract(qc_ref[at], d_scores, 0, 0)
+        d_content = jnp.dot(d_scores, k_ref[...], preferred_element_type=F32) * scale
+        d_rotated = jnp.dot(d_scores, table_ref[...], preferred_element_type=F32)
+        lead, tail = d_rotated[:, :half], d_rotated[:, half:]
+        cos, sin = cos_ref[at] * scale, sin_ref[at] * scale
+        d_mixed = jnp.concatenate(
+            [(lead * sin - tail * cos).astype(BF16), (lead * cos + tail * sin).astype(BF16)], 1
+        )
+        d_position = jnp.dot(d_mixed, rel_ref[...], preferred_element_type=F32)
+        drel_t = drel_t + contract(qp_ref[at], d_mixed, 0, 0)
+        d_queries.append((d_content + d_position).astype(BF16))
+        d_content_sum = d_content_sum + jnp.sum(d_content, 0, keepdims=True)
+        d_position_sum = d_position_sum + jnp.sum(d_position, 0, keepdims=True)
+    bias_ref[...] = jnp.concatenate([d_content_sum, d_position_sum], 0)
+
+    d_query = jnp.concatenate(d_queries, 0)
+    d_kv_t = jnp.concatenate([(dk_t * scale).astype(BF16), dv_t.astype(BF16)], 0)
+    d_kv = d_kv_t[:, past:].T
+    of_kv_t = jnp.dot(d_kv_t, normed_ref[...], preferred_element_type=F32)
+    of_query_t = contract(d_query, normed_ref[past:, :], 0, 0)
+    of_query, of_key, of_value = of_query_t.T, of_kv_t[:DH].T, of_kv_t[DH:].T
+    mine = bits_ref[0] == 1
+    for i, grad in enumerate((of_query, drel_t.T, of_key, of_value)):
+        middle = grad.shape[0] // 2
+        low, high = grad[:middle].astype(BF16), grad[middle:].astype(BF16)
+        keep_ref[i] = jnp.where(mine, high, low)
+        give_ref[i] = jnp.where(mine, low, high)
+    own_rows = (
+        contract(d_query, wq_ref[...], 1, 1)
+        + contract(d_kv[:, :DH], wk_ref[...], 1, 1)
+        + contract(d_kv[:, DH:], wv_ref[...], 1, 1)
+    )
+    wq = wq_ref[...].astype(F32)
+    wk = wk_ref[...].astype(F32)
+    wv = wv_ref[...].astype(F32)
+    sums = jnp.sum(d_kv_t.astype(F32), 1, keepdims=True).T
+    own_along = of_query * wq + of_key * wk + of_value * wv
+    own_shift = (
+        jnp.sum(d_query.astype(F32), 0, keepdims=True) * wq + sums[:, :DH] * wk + sums[:, DH:] * wv
+    )
+
+    @pl.when(head == 0)
     def _():
-        dk_sum[...] = jnp.zeros_like(dk_sum)
-        dv_sum[...] = jnp.zeros_like(dv_sum)
-        drel_sum[...] = jnp.zeros_like(drel_sum)
-        bias_ref[...] = jnp.zeros_like(bias_ref)
-
-    prob = p_ref[0]
-    d_attn = da_ref[...]
-    dv_sum[...] += contract(prob, d_attn, 0, 0)
-    d_prob = contract(d_attn, v_ref[...], 1, 1)
-    prob_f = prob.astype(F32)
-    weighted = prob_f * d_prob
-    inner = jnp.sum(weighted, 1, keepdims=True)
-    d_scores = (weighted - prob_f * inner).astype(BF16)
-    dk_sum[...] += contract(d_scores, qc_ref[...], 0, 0)
-    d_content = jnp.dot(d_scores, k_ref[...], preferred_element_type=F32) * scale
-    d_rotated = jnp.dot(d_scores, table_ref[...], preferred_element_type=F32) * scale
-    lead, tail = d_rotated[:, :half], d_rotated[:, half:]
-    cos, sin = cos_ref[...], sin_ref[...]
-    d_mixed = jnp.concatenate(
-        [(lead * sin - tail * cos).astype(BF16), (lead * cos + tail * sin).astype(BF16)], 1
-    )
-    d_position = jnp.dot(d_mixed, rel_ref[...], preferred_element_type=F32)
-    drel_sum[...] += contract(d_mixed, qp_ref[...], 0, 0)
-    dq_all[pl.ds(pl.multiple_of(step * block, block), block), :] = (d_content + d_position).astype(
-        BF16
-    )
-    bias_ref[...] += jnp.concatenate(
-        [jnp.sum(d_content, 0, keepdims=True), jnp.sum(d_position, 0, keepdims=True)], 0
-    )
-
-    @pl.when(step == pl.num_programs(1) - 1)
+        before = rest[:3] if with_sums else None
+        rows_ref[...] = own_rows + before[0][...] if with_sums else own_rows
+        along_ref[...] = own_along + before[1][...] if with_sums else own_along
+        shift_ref[...] = own_shift + before[2][...] if with_sums else own_shift
+
+    @pl.when(head > 0)
     def _():
-        d_key = (dk_sum[...] * scale).astype(BF16)
-        d_value = dv_sum[...].astype(BF16)
-        d_query = dq_all[...]
-        past = d_key.shape[0] - seg
-        of_kv = jnp.dot(
-            normed_ref[...], jnp.concatenate([d_key, d_value], 1), preferred_element_type=F32
-        )
-        of_query = jnp.dot(normed_ref[:, past:], d_query, preferred_element_type=F32)
-        mine = bits_ref[0] == 1
-        for i, grad in enumerate((of_query, drel_sum[...], of_kv[:, :DH], of_kv[:, DH:])):
-            middle = grad.shape[0] // 2
-            low, high = grad[:middle].astype(BF16), grad[middle:].astype(BF16)
-            keep_ref[i] = jnp.where(mine, high, low)
-            give_ref[i] = jnp.where(mine, low, high)
-        own_rows = (
-            contract(d_query, wq_ref[...], 1, 1)
-            + contract(d_key[past:], wk_ref[...], 1, 1)
-            + contract(d_value[past:], wv_ref[...], 1, 1)
-        )
-        wq = wq_ref[...].astype(F32)
-        wk = wk_ref[...].astype(F32)
-        wv = wv_ref[...].astype(F32)
-        own_along = of_query * wq + of_kv[:, :DH] * wk + of_kv[:, DH:] * wv
-        own_shift = (
-            jnp.sum(d_query.astype(F32), 0, keepdims=True) * wq
-            + jnp.sum(d_key.astype(F32), 0, keepdims=True) * wk
-            + jnp.sum(d_value.astype(F32), 0, keepdims=True) * wv
-        )
-
-        @pl.when(head == 0)
-        def _():
-            before = rest[:3] if with_sums else None
-            rows_ref[...] = own_rows + before[0][...] if with_sums else own_rows
-            along_ref[...] = own_along + before[1][...] if with_sums else own_along
-            shift_ref[...] = own_shift + before[2][...] if with_sums else own_shift
-
-        @pl.when(head > 0)
-        def _():
-            rows_ref[...] += own_rows
-            along_ref[...] += own_along
-            shift_ref[...] += own_shift
+        rows_ref[...] += own_rows
+        along_ref[...] += own_along
+        shift_ref[...] += own_shift
 
 
 def attend_back(
@@ -594,7 +587,7 @@
     w_query,
     w_key,
     w_value,
-    normed_t,
+    normed,
     table,
     cos,
     sin,
@@ -604,13 +597,13 @@
 ):
     seg, width = content.shape
     total = keys.shape[0]
-    block = QUERY_BLOCK
-    column = lambda h, q: (0, start + h)
-    rows = lambda h, q: (q, start + h)
-    fixed = lambda h, q: (0, 0)
+    block = seg
+    column = lambda h: (0, start + h)
+    rows = lambda h: (0, start + h)
+    fixed = lambda h: (0, 0)
     whole = pl.BlockSpec(memory_space=pl.ANY)
     operands = [bits, prob, d_attn, content, position, keys, values, w_rel]
-    operands += [w_query, w_key, w_value, normed_t, table, cos, sin]
+    operands += [w_query, w_key, w_value, normed, table, cos, sin]
     aliases = {}
     sum_specs = [
         pl.BlockSpec((seg, width), fixed),
@@ -624,13 +617,13 @@
         aliases[len(operands) + i] = i
     operands += [*into, *first]
     half = jax.ShapeDtypeStruct(into[0].shape if into else (4, width // 2, len(heads) * DH), BF16)
-    half_spec = pl.BlockSpec((4, width // 2, DH), lambda h, q: (0, 0, start - heads.start + h))
+    half_spec = pl.BlockSpec((4, width // 2, DH), lambda h: (0, 0, start - heads.start + h))
     return pl.pallas_call(
         functools.partial(attend_back_kernel, bool(sums)),
-        grid=(count, seg // block),
+        grid=(count,),
         in_specs=[
             pl.BlockSpec(memory_space=pltpu.SMEM),
-            pl.BlockSpec((1, block, total), lambda h, q: (start + h, q, 0)),
+            pl.BlockSpec((1, block, total), lambda h: (start + h, 0, 0)),
             pl.BlockSpec((block, DH), rows),
             pl.BlockSpec((block, DH), rows),
             pl.BlockSpec((block, DH), rows),
@@ -640,14 +633,14 @@
             pl.BlockSpec((width, DH), column),
             pl.BlockSpec((width, DH), column),
             pl.BlockSpec((width, DH), column),
-            pl.BlockSpec((width, total), fixed),
-            pl.BlockSpec((total, width), fixed),
-            pl.BlockSpec((block, width // 2), rows_of_block),
-            pl.BlockSpec((block, width // 2), rows_of_block),
+            pl.BlockSpec(memory_space=pltpu.VMEM),
+            pl.BlockSpec(memory_space=pltpu.VMEM),
+            pl.BlockSpec(memory_space=pltpu.VMEM),
+            pl.BlockSpec(memory_space=pltpu.VMEM),
         ]
         + sum_specs[: len(sums)]
         + [whole] * (len(into) + len(first)),
-        out_specs=[half_spec, half_spec] + sum_specs + [pl.BlockSpec((2, DH), lambda h, q: (0, h))],
+        out_specs=[half_spec, half_spec] + sum_specs + [pl.BlockSpec((2, DH), lambda h: (0, h))],
         out_shape=[
             half,
             half,
@@ -656,21 +649,11 @@
             jax.ShapeDtypeStruct((width, DH), F32),
             jax.ShapeDtypeStruct((2, count * DH), F32),
         ],
-        scratch_shapes=[
-            pltpu.VMEM((total, DH), F32),
-            pltpu.VMEM((total, DH), F32),
-            pltpu.VMEM((width, DH), F32),
-            pltpu.VMEM((seg, DH), BF16),
-        ],
         input_output_aliases=aliases,
-        compiler_params=pltpu.CompilerParams(vmem_limit_bytes=VMEM_LIMIT),
+        compiler_params=pltpu.CompilerParams(vmem_limit_bytes=52 * MIB),
         cost_estimate=SHORT,
         name="attend_back",
     )(*operands)
-
-
-def rows_of_block(h, q):
-    return (q, 0)
 
 
 def in_vmem():
@@ -705,7 +688,7 @@
             jax.ShapeDtypeStruct((3, len(parts), block, width), BF16),
             jax.ShapeDtypeStruct((len(parts), block, width), BF16),
         ],
-        compiler_params=pltpu.CompilerParams(vmem_limit_bytes=VMEM_LIMIT),
+        compiler_params=pltpu.CompilerParams(vmem_limit_bytes=48 * MIB),
         cost_estimate=SHORT,
         name="norm_context",
     )(owners, *parts, gain.reshape(1, -1), shift.reshape(1, -1), *after)
@@ -731,6 +714,19 @@
     )(owners, *parts, *after)
 
 
+def hold(values, *others):
+    whole = pl.BlockSpec(memory_space=pl.ANY)
+    return pl.pallas_call(
+        lambda *refs: None,
+        in_specs=[whole] * (len(values) + len(others)),
+        out_specs=[whole] * len(values),
+        out_shape=[jax.ShapeDtypeStruct(v.shape, v.dtype) for v in values],
+        input_output_aliases={i: i for i in range(len(values))},
+        cost_estimate=SHORT,
+        name="hold",
+    )(*values, *others)
+
+
 def copy_kernel(rows_ref, *refs):
     refs[-1][...] = rows_ref[...]
 
@@ -744,57 +740,6 @@
         cost_estimate=SHORT,
         name="copy_after",
     )(rows, *others)
-
-
-def flip_kernel(rows_ref, *refs):
-    refs[-1][...] = rows_ref[...].T
-
-
-def flip_after(rows, *others):
-    count, width = rows.shape
-    block = width // 2
-    return pl.pallas_call(
-        flip_kernel,
-        grid=(count // block,),
-        in_specs=[pl.BlockSpec((block, width), lambda i: (i, 0))]
-        + [pl.BlockSpec(memory_space=pl.ANY)] * len(others),
-        out_specs=pl.BlockSpec((width, block), lambda i: (0, i)),
-        out_shape=jax.ShapeDtypeStruct((width, count), rows.dtype),
-        cost_estimate=SHORT,
-        name="flip_after",
-    )(rows, *others)
-
-
-def half_grad_kernel(bits_ref, left_ref, right_ref, out_ref):
-    out_ref[...] = contract(left_ref[...], right_ref[...], 0, 0).astype(BF16)
-
-
-def half_grad(bits, which, pre, left, right, give):
-    rows, units = left.shape
-    width = right.shape[1]
-    cells = 1 << max(pre.bit_length(), 2)
-    run = cells // (2 * pre)
-
-    def column(i, bits):
-        side = 1 - bits[which] if give else bits[which]
-        return (0, (i // run * 2 + side) * run + i % run)
-
-    return pl.pallas_call(
-        half_grad_kernel,
-        grid_spec=pltpu.PrefetchScalarGridSpec(
-            num_scalar_prefetch=1,
-            grid=(cells // 2,),
-            in_specs=[
-                pl.BlockSpec((rows, units // cells), column),
-                pl.BlockSpec((rows, width), lambda i, bits: (0, 0)),
-            ],
-            out_specs=pl.BlockSpec((units // cells, width), lambda i, bits: (i, 0)),
-        ),
-        out_shape=jax.ShapeDtypeStruct((units // 2, width), BF16),
-        compiler_params=pltpu.CompilerParams(vmem_limit_bytes=VMEM_LIMIT),
-        cost_estimate=SHORT,
-        name="half_grad",
-    )(bits, left, right)[None]
 
 
 def out_grad_kernel(bits_ref, left_ref, right_ref, keep_ref, give_ref):
@@ -819,7 +764,7 @@
         in_specs=[pl.BlockSpec(memory_space=pltpu.SMEM), whole, whole],
         out_specs=[spec, spec],
         out_shape=[half, half],
-        compiler_params=pltpu.CompilerParams(vmem_limit_bytes=VMEM_LIMIT),
+        compiler_params=pltpu.CompilerParams(vmem_limit_bytes=48 * MIB),
         cost_estimate=SHORT,
         name="out_grad",
     )(bits, left, right)
@@ -859,7 +804,7 @@
         out_specs=out_specs,
         out_shape=[out] * len(out_specs),
         input_output_aliases={3 + i: i for i in range(len(before))},
-        compiler_params=pltpu.CompilerParams(vmem_limit_bytes=VMEM_LIMIT),
+        compiler_params=pltpu.CompilerParams(vmem_limit_bytes=48 * MIB),
         cost_estimate=SHORT,
         name="finish",
     )(bits, own, got, *before)
@@ -870,6 +815,7 @@
     def __init__(self, moves, keeps, gives):
         self.moves, self.keeps, self.gives = list(moves), keeps, gives
         self.join = False
+        self.got = None
 
 
 def parts_of(move):
@@ -893,12 +839,13 @@
     return keeps, gives
 
 
-def round_of(chains, bits, bit_names, after=()):
+def round_of(chains, bits, bit_names, after=(), through=()):
     operands, plans, out_shape = [], [], []
     for chain in chains:
         kind, cuts = chain.moves.pop(0)
         nexts = chain.moves[0] if chain.moves else None
-        got = [swap(give, *step) for give, (step, _) in zip(chain.gives, cuts)]
+        got = chain.got or [[swap(give, *step)] for give, (step, _) in zip(chain.gives, cuts)]
+        chain.got = None
         held = chain.keeps if kind == "halve" else chain.gives
         leads, columns = [h.shape[0] for h in held], held[0].shape[2]
         total = sum(leads)
@@ -912,14 +859,15 @@
                 view = (h.shape[0], cells, h.shape[1] // cells, columns)
                 bit = (bit_names.index(cuts[i][0]), cuts[i][1])
             elif next_kind == "halve":
-                cells = max(2 * pre for _, pre in next_cuts)
+                cells = max([2 * pre for _, pre in next_cuts] + [len(g) for g in got])
                 view = (h.shape[0], cells, h.shape[1] // cells, columns)
                 bit = None
             else:
                 view = h.shape
                 bit = None
-            ins.append((len(operands), base, bit, view))
-            operands += [h.reshape(view), g.reshape(view)]
+            ins.append((len(operands), base, bit, view, len(g)))
+            operands += [h.reshape(view)]
+            operands += [r.reshape(view[0], -1, *view[2:]) if len(g) > 1 else r.reshape(view) for r in g]
         rows = held[0].shape[1]
         outs = []
         for j, cut in enumerate(next_cuts):
@@ -941,10 +889,11 @@
         plans.append((kind, next_kind, size, ins, outs))
 
     def kernel(bits_ref, *refs):
-        inputs, results = refs[: len(operands)], refs[-len(out_shape) :]
+        inputs, results = refs[: len(operands)], refs[len(refs) - len(out_shape) - len(through) :]
         for kind, next_kind, size, ins, outs in plans:
-            for at, base, bit, view in ins:
+            for at, base, bit, view, count in ins:
                 held_ref, got_ref = inputs[at], inputs[at + 1]
+                got_refs = inputs[at + 1 : at + 1 + count]
                 for i in range(view[0]):
                     where, which = divmod(base + i, size)
                     out, out_bit, out_pre = outs[where]
@@ -963,6 +912,17 @@
                         mine = bits_ref[out_bit]
                         run = view[1] // (2 * out_pre)
                         for cell in range(view[1] // 2):
+                            if count > 1:
+                                sums = []
+                                for side in range(2):
+                                    place = (cell // run * 2 + side) * run + cell % run
+                                    piece, rest = divmod(place * count, view[1])
+                                    more = got_refs[piece][i, rest // count].astype(F32)
+                                    sums.append(held_ref[i, place].astype(F32) + more)
+                                high = mine == 1
+                                results[out][which, cell] = jnp.where(high, sums[1], sums[0]).astype(BF16)
+                                results[out + 1][which, cell] = jnp.where(high, *sums).astype(BF16)
+                                continue
                             for side, slot in ((mine, out), (1 - mine, out + 1)):
                                 place = (cell // run * 2 + side) * run + cell % run
                                 results[slot][which, cell] = (
@@ -978,13 +938,16 @@
         kernel,
         in_specs=[pl.BlockSpec(memory_space=pltpu.SMEM)]
         + [in_vmem] * len(operands)
-        + [pl.BlockSpec(memory_space=pl.ANY)] * len(after),
-        out_specs=[in_vmem] * len(out_shape),
-        out_shape=out_shape,
-        compiler_params=pltpu.CompilerParams(vmem_limit_bytes=VMEM_LIMIT),
+        + [pl.BlockSpec(memory_space=pl.ANY)] * (len(through) + len(after)),
+        out_specs=[in_vmem] * len(out_shape) + [pl.BlockSpec(memory_space=pl.ANY)] * len(through),
+        out_shape=out_shape + [jax.ShapeDtypeStruct(r.shape, r.dtype) for r in through],
+        input_output_aliases={
+            1 + len(operands) + i: len(out_shape) + i for i in range(len(through))
+        },
+        compiler_params=pltpu.CompilerParams(vmem_limit_bytes=48 * MIB),
         cost_estimate=SHORT,
         name="add_and_split",
-    )(bits, *operands, *after)
+    )(bits, *operands, *through, *after)
     for chain, (kind, next_kind, size, ins, outs) in zip(chains, plans):
         flat = lambda r: r.reshape(r.shape[0], -1, r.shape[-1])
         if next_kind == "halve":
@@ -993,14 +956,7 @@
         else:
             chain.keeps = []
             chain.gives = [flat(results[o]) for o, _, _ in outs]
-
-
-def gather_wide(rows, wide, order):
-    have = []
-    for i in order:
-        rows = double(rows, wide[i], sum(j < i for j in have))
-        have.append(i)
-    return rows
+    return results[len(out_shape) :]
 
 
 def own_streams_plan(
@@ -1037,7 +993,7 @@
     hidden_dev = w_down.shape[0]
 
     core = ("dp", 1)
-    wide = [("dp", d) for d in bits_below(dp_parts)[1:]]
+    wide = [("dp", d) for d in reversed(bits_below(dp_parts)[1:])]
     line = [("seq", d) for d in bits_below(seq_parts)]
     there = list(range(len(wide)))
     back = there[::-1]
@@ -1046,26 +1002,24 @@
     bit_names = [core] + wide + line
     bits = jnp.stack([bit_of(*name) for name in bit_names]).astype(jnp.int32)
     wide_in = [[(wide[i], 1), (wide[j], 1 << j)] for i, j in zip(there, back)]
+    line_in = [[(step, 1 << i)] for i, step in enumerate(reversed(line))][::-1]
     core_cut, line_cuts, wide_cuts = [(core, 1)], [[(s, 1)] for s in line], [[(s, 1)] for s in wide]
 
     def moves_of(cuts, collected):
         return [("halve", c) for c in cuts] + [("double", c) for c in reversed(collected)]
 
-    piece = hidden_dev // 2 >> len(wide)
-    place = core_bit
-    for step in wide:
-        place = place * 2 + bit_of(*step)
+    piece = hidden_dev // dp_parts
+    place = lax.axis_index("dp")
 
     def gathered(rows):
         rows = jnp.swapaxes(rows.reshape(piece, 2, width // 2), 0, 1)
-        chain = Chain(moves_of([], wide_in + line_cuts), [], [rows])
+        chain = Chain(moves_of([], wide_in + line_in), [], [rows])
         chain.join = True
         return chain
 
     up_piece = lax.dynamic_slice_in_dim(w_up, place * piece, piece, 1).T
     up_chain = gathered(up_piece)
     round_of([up_chain], bits, bit_names)
-    order = token(up_chain.gives[0])
     for step in line[:-1]:
         round_of([up_chain], bits, bit_names)
     order_two = token(up_chain.gives[0])
@@ -1090,17 +1044,18 @@
         return by_stream(place_rows(send(parts), owners))
 
     blocks = [by_stream(rows) for rows in (compressed, memory, inputs)]
-    parts = send(parts_for(jnp.concatenate(blocks, 1), order))
+    parts = send(parts_for(jnp.concatenate(blocks, 1)))
     down_piece = lax.dynamic_slice_in_dim(w_down, place * piece + order_two, piece, 0)
     down_chain = gathered(down_piece)
     round_of([up_chain], bits, bit_names)
-    normed, x_rows = norm_context(
-        parts, owners, gain_first, shift_first, [*up_chain.gives, *down_chain.gives, table, cos, sin]
-    )
+    go_parts = parts_for(by_stream(grad_out))
+    memory_rows = by_stream(memory)
+    idle = [*up_chain.gives, *down_chain.gives, table, cos, sin, *go_parts, memory_rows]
+    normed, x_rows = norm_context(parts, owners, gain_first, shift_first, idle)
     length = lax.dynamic_slice_in_dim(seg_len, me, 1)
     order = token(normed)
-    go_parts = parts_for(by_stream(grad_out), order)
-    bias_all = lax.dynamic_slice_in_dim(bias_up.reshape(2, -1), core_bit + order, 1, 0)
+    bias_all = lax.dynamic_slice_in_dim(bias_up.reshape(-1, 2, piece), core_bit + order, 1, 1)
+    bias_all = bias_all.reshape(1, -1)
 
     seg_normed = normed[split:]
     queries = jnp.dot(seg_normed, w_query, preferred_element_type=F32)
@@ -1108,58 +1063,53 @@
     values = jnp.dot(normed, w_value, preferred_element_type=F32).astype(BF16)
     content = (queries + bias_content).astype(BF16)
     position = (queries + bias_position).astype(BF16)
+    memory_rows = copy_after(memory_rows, keys)
+    memory_all = lax.all_gather(memory_rows, "seq", axis=1, tiled=True)
     given = (length, content, position, keys, values, w_rel, table, cos, sin)
     round_of([down_chain], bits, bit_names, [normed])
     round_of([down_chain], bits, bit_names, [values])
-    go_rows = send(go_parts)
-    prob, attn_out = attend(range(H // 2), *given, first=down_chain.gives + go_parts[1:])
-    go_rows = place_rows(go_rows, owners, [attn_out]).reshape(seg, width)
-    round_of([down_chain], bits, bit_names, [attn_out])
+    prob, attn_out = attend(range(H // 2), *given, first=down_chain.gives)
+    prob, attn_out = round_of([up_chain, down_chain], bits, bit_names, [], [prob, attn_out])
     while up_chain.moves:
         round_of([up_chain], bits, bit_names, [attn_out])
     up_half = up_chain.gives[0][0]
     bias_all = double(bias_all, line[-1], 0)
     prob, attn_out = attend(
-        range(H // 2, H),
-        *given,
-        first=down_chain.gives + [go_rows, bias_all, up_half],
-        into=[prob, attn_out],
-    )
+        range(H // 2, H), *given, first=down_chain.gives + [bias_all], into=[prob, attn_out]
+    )
+    (attn_out,) = round_of([down_chain], bits, bit_names, [], [attn_out])
     while down_chain.moves:
-        round_of([down_chain], bits, bit_names, [attn_out])
+        round_of([down_chain], bits, bit_names)
     down_half = down_chain.gives[0][0]
-    for step in line[-2::-1]:
-        bias_all = double(bias_all, step, 0)
+    for i, step in enumerate(line[-2::-1]):
+        bias_all = double(bias_all, step, i + 1)
     bias_half = jnp.swapaxes(bias_all.reshape(seq_parts, -1, piece), 0, 1).reshape(-1).astype(F32)
-    memory_rows = copy_after(by_stream(memory), attn_out)
-    memory_all = lax.all_gather(memory_rows, "seq", axis=1, tiled=True)
     x_f = x_rows.astype(F32)
     hidden = x_f + jnp.dot(attn_out, w_out, preferred_element_type=F32)
     normed_two = layer_norm(hidden, gain_second, shift_second).astype(BF16)
 
     pair_normed = double(normed_two, core).reshape(-1, width)
-    pair_grad = double(go_rows, core).reshape(-1, width)
     pre_act = contract(pair_normed, up_half, 1, 1) + bias_half
     activated = gelu_tanh(pre_act).astype(BF16)
+    go_rows = place_rows(send(go_parts), owners, [activated, memory_all]).reshape(seg, width)
+    pair_grad = double(go_rows, core).reshape(-1, width)
     ffn_rows = jnp.dot(activated, down_half, preferred_element_type=F32)
     ffn_rows = halve(ffn_rows.reshape(2, seg, width), core)
     output = (hidden + ffn_rows + bias_down).astype(BF16)
     output_parts = parts_for(output.reshape(seq_parts, seg_dev, width))
-    down_grad = functools.partial(half_grad, bits, 1, 1, activated, pair_grad)
-    down_give = down_grad(True)
+    groups_of = [list(range(c, dp_parts, 2)) for c in range(2)]
+
+    def over_rows(grad):
+        return lax.psum_scatter(grad, "dp", axis_index_groups=groups_of, tiled=True)
+
+    down_sum = over_rows(contract(activated, pair_grad, 0, 0).astype(BF16))
     d_activated = contract(pair_grad, down_half, 1, 1)
     _, gelu_back = jax.vjp(gelu_tanh, pre_act)
     d_pre = gelu_back(d_activated)[0].astype(BF16)
-    up_grad = functools.partial(half_grad, bits, len(wide), 1 << (len(wide) - 1), d_pre, pair_normed)
-    up_give = up_grad(True)
     d_normed_two = jnp.dot(d_pre, up_half, preferred_element_type=F32)
     d_normed_two = halve(d_normed_two.reshape(2, seg, width), core)
+    up_sum = over_rows(contract(d_pre, pair_normed, 0, 0).astype(BF16))
     grad_bias_half = jnp.sum(d_pre.astype(F32), 0)
-    ffn = Chain(
-        moves_of(wide_in + line_cuts, [core_cut] + wide_in),
-        [down_grad(False), up_grad(False)],
-        [down_give, up_give],
-    )
 
     go_f = go_rows.astype(F32)
     _, norm_two_back = jax.vjp(layer_norm, hidden, gain_second, shift_second)
@@ -1168,6 +1118,48 @@
     grad_bias_down = jnp.sum(go_f, 0)
     d_branch = d_hidden.astype(BF16)
     d_attn = contract(d_branch, w_out, 1, 1).astype(BF16)
+
+    half_heads = H // 2
+    group_moves = moves_of([core_cut] + wide_in + line_cuts, [core_cut] + wide_in + line_cuts)
+    groups, biases, head_sums = [], [], []
+    output_rows = send(output_parts)
+
+    first, start = [], 0
+    for call, heads in enumerate(CALLS):
+        base = start // half_heads * half_heads
+        group_heads = range(base, base + half_heads)
+        if start == 0:
+            halves = out_grad(bits, attn_out, d_branch)
+        elif start == base:
+            halves = []
+        *halves, d_rows, along, shift_part, bias_part = attend_back(
+            start, heads, group_heads, bits, prob, d_attn, content, position, keys, values,
+            w_rel, w_query, w_key, w_value, normed, table, cos, sin, head_sums, halves, first,
+        )
+        start += heads
+        passing = [*halves, d_rows, along, shift_part, bias_part]
+        if call == 0:
+            down_sum, *passing = hold([down_sum, *passing])
+            down_sum = lax.psum_scatter(down_sum, "seq", tiled=True)
+            first = output_parts[1:]
+        elif call == 1:
+            output_rows = place_rows(output_rows, owners, [bias_part])
+            up_sum, *passing = hold([up_sum, *passing], output_rows)
+            up_sum = lax.psum_scatter(up_sum, "seq", tiled=True)
+            first = []
+        elif call == 2:
+            down_sum, *passing = round_of(groups, bits, bit_names, [], [down_sum, *passing])
+            down_sum = lax.all_gather(down_sum, "dp", tiled=True)
+            first = [g for c in groups for g in c.gives]
+        else:
+            memory_all, *passing = round_of(groups, bits, bit_names, [], [memory_all, *passing])
+        *halves, d_rows, along, shift_part, bias_part = passing
+        head_sums = [d_rows, along, shift_part]
+        biases.append(bias_part)
+        if start == group_heads.stop:
+            groups.append(Chain(group_moves, [halves[0]], [halves[1]]))
+            first += [halves[1]]
+    output = by_stream(output_rows)
 
     new_rows = memory_all.shape[1] // RATE
     windows = memory_all[:, : new_rows * RATE].reshape(streams, new_rows, RATE, width)
@@ -1182,39 +1174,6 @@
         comp_moves, *first_halves(grad_w_comp.astype(BF16).reshape(1, -1, comp_shape[2]), comp_moves[0])
     )
 
-    normed_t = flip_after(normed, normed_two)
-    half_heads = H // 2
-    group_moves = moves_of([core_cut] + wide_in + line_cuts, [core_cut] + wide_in + line_cuts)
-    groups, biases, head_sums = [], [], []
-    output_rows = send(output_parts)
-    first = ffn.gives + output_parts[1:] + [memory_rows]
-    beside = [[], [], [ffn, comp], [ffn, comp]]
-    for start in range(0, H, HEADS_A_CALL):
-        base = start // half_heads * half_heads
-        group_heads = range(base, base + half_heads)
-        if start == 0:
-            halves = out_grad(bits, attn_out, d_branch)
-        elif start == base:
-            halves = []
-        *halves, d_rows, along, shift_part, bias_part = attend_back(
-            start, HEADS_A_CALL, group_heads, bits, prob, d_attn, content, position, keys, values,
-            w_rel, w_query, w_key, w_value, normed_t, table, cos, sin, head_sums, halves, first,
-        )
-        head_sums = [d_rows, along, shift_part]
-        biases.append(bias_part)
-        active = beside[start // HEADS_A_CALL] + groups
-        if active:
-            round_of(active, bits, bit_names, [bias_part])
-        first = [g for c in active for g in c.gives]
-        if start == 0:
-            output_rows = place_rows(output_rows, owners, [bias_part])
-            first += [output_rows]
-        if start + HEADS_A_CALL == group_heads.stop:
-            groups.append(Chain(group_moves, [halves[0]], [halves[1]]))
-            first += groups[-1].gives
-            if start + HEADS_A_CALL == half_heads:
-                first += comp.gives + ffn.keeps
-    output = by_stream(output_rows)
     d_normed = d_rows
     _, norm_one_back = jax.vjp(lambda v: layer_norm(v, gain_first, shift_first), x_f)
     (d_context,) = norm_one_back(d_normed)
@@ -1243,47 +1202,49 @@
     vector = Chain([("add", [(name, 1)]) for name in bit_names], [], [vectors.reshape(1, -1, DH)])
 
     one, two = groups
-    rounds = [
-        [ffn, one, two, vector],
-        [ffn, one, two, vector],
-        [ffn, one, two],
-        [ffn, one, two, vector, comp],
-        [ffn, one, two, vector, comp],
-        [one, two, vector, comp],
-        [one, two, comp],
-    ]
-    turn = 0
-    while len(two.moves) > 1 or vector.moves or comp.moves or ffn.moves:
-        active = rounds[turn] if turn < len(rounds) else [ffn, one, two, vector, comp]
+    def finished(column, group, results):
+        own = group.gives[0]
+        return finish(bits, column, len(groups), own, swap(own, *core), results)
+
+    turn, results = 0, []
+    pinned = {
+        1: input_parts,
+        2: [input_rows[1]],
+        3: [new_compressed],
+        5: [*input_rows[2:-1]],
+        6: [input_rows[-1]],
+    }
+    while len(two.moves) > 1 or vector.moves or comp.moves:
+        active = [one, two] + [comp] * (turn > 0) + [vector] * (turn > 2)
         active = [c for c in active if len(c.moves) > (c in groups)]
-        if turn == 5:
-            fence = input_parts
-        elif turn == 8:
-            input_rows = place_rows(input_rows, owners)
-            fence = [input_rows]
-        else:
-            fence = []
-        round_of(active, bits, bit_names, fence)
+        fence = pinned.get(turn, [])
+        if turn == 7:
+            grad_inputs = by_stream(place_rows(input_rows, owners))
+            fence = [grad_inputs]
+        if not results and len(one.moves) == 1:
+            results = finished(0, one, results)
+            fence = [*fence, *results]
+        through = [up_sum] if turn == 0 else []
+        through = round_of(active, bits, bit_names, fence, through)
+        if turn == 0:
+            up_sum = lax.all_gather(through[0], "dp", tiled=True)
+            grad_w_down, grad_w_up = down_sum.astype(F32), up_sum.astype(F32).T
+            pinned[4] = [grad_w_down]
+            pinned[5] = [*pinned[5], grad_w_up]
         turn += 1
-    grad_inputs = by_stream(input_rows)
     vectors = vector.gives[0].reshape(-1)
 
-    grad_w_down = ffn.gives[0][0].astype(F32)
-    grad_w_up = ffn.gives[0][1].astype(F32).T
     grad_w_comp = comp.gives[0].astype(F32).reshape(comp_shape)
-    results = []
-    for column, group in enumerate(groups):
-        own = group.gives[0]
-        results = finish(bits, column, len(groups), own, swap(own, *core), results)
+    results = finished(1, two, results)
     grad_w_query, grad_w_rel, grad_w_key, grad_w_value, grad_w_out = results
 
     totals = vectors[:count].reshape(-1, width)
     hidden_sums = vectors[count : count + hidden_sums.size].reshape(
         [2, 1 << len(wide)] + [2] * len(line) + [piece]
     )
-    for step in line:
+    for step in reversed(line):
         hidden_sums = pick(hidden_sums, bit_of(*step), 2)
-    grad_bias_up = hidden_sums.reshape(-1)
+    grad_bias_up = jnp.swapaxes(hidden_sums, 0, 1).reshape(-1)
     comp_sums = vectors[count + grad_bias_half.size * 2 :].reshape(comp_sums.shape)
     grad_comp_bias = pick(comp_sums, me, 0)
 

time: 751 us -> 669 us (0.89)
  waiting for transfers between devices: 189 us -> 126 us
  Pallas kernels: 241 us -> 195 us
  matrix products: 49.8 us -> 72.3 us
  starting transfers between devices: 93.2 us -> 78.5 us
  local copies, waits for them, and re-layouts: 104 us -> 118 us
    ppermute x12, waiting for transfers between devices: 52.2 us -> 7.17 us  [send(): lax.ppermute(part, 'seq', [(i, (i + shift) % seq_parts) for i in range(se...]
    pallas_call x5 -> x2, Pallas kernels: 24.9 us -> 0.01 us  [hold(): pl.pallas_call(lambda *refs: None, in_specs=[whole] * (len(values) + len(...]
    ppermute x68 -> x57, waiting for transfers between devices: 137 us -> 114 us  [swap(): return lax.ppermute(rows, axis, [(i, i ^ distance) for i in range(count)])]
    ppermute x68 -> x57, starting transfers between devices: 72.3 us -> 50 us  [swap(): return lax.ppermute(rows, axis, [(i, i ^ distance) for i in range(count)])]
    unnamed x273 -> x295, local copies, waits for them, and re-layouts: 63.6 us -> 81.2 us
    dot_general x3 -> x5, matrix products: 21.1 us -> 37.2 us  [contract(): lax.dot_general(left, right, (((left_dim,), (right_dim,)), ((), ())), pre...]
    pallas_call x19 -> x18, Pallas kernels: 50.8 us -> 37.1 us  [round_of(): pl.pallas_call(kernel, in_specs=[pl.BlockSpec(memory_space=pltpu.SMEM)] +...]
  transfers between devices with their start and end apart: 81 -> 76, of which waited for: 32 -> 22; matrix products, arithmetic and copies ran while one was open for 20% -> 24% of each run, Pallas kernels for 28% -> 28%
where the time goes in v2:
time: 669 us; the launch traced here: 658 us
  Pallas kernels  195 us (29%)
  waiting for transfers between devices  126 us (19%)
  local copies, waits for them, and re-layouts  118 us (18%)
  starting transfers between devices  78.5 us (12%)
  matrix products  72.3 us (11%)
  other arithmetic  51.3 us (8%)
  between operations  17.1 us (3%)
    ppermute x57, waiting for transfers between devices, swap(): return lax.ppermute(rows, axis, [(i, i ^ distance) for i in range(count)])  114 us
    pallas_call x4, Pallas kernels, attend_back(): pl.pallas_call(functools.partial(attend_back_kernel, bool(sums)), grid=(c...  85.8 us
    unnamed x295, local copies, waits for them, and re-layouts  81.2 us
    ppermute x57, starting transfers between devices, swap(): return lax.ppermute(rows, axis, [(i, i ^ distance) for i in range(count)])  50 us
    pallas_call x2, Pallas kernels, attend(): pl.pallas_call(attend_kernel, grid=(count, seg // block), in_specs=[pl.Bl...  41.9 us
    dot_general x5, matrix products, contract(): lax.dot_general(left, right, (((left_dim,), (right_dim,)), ((), ())), pre...  37.2 us
    pallas_call x18, Pallas kernels, round_of(): pl.pallas_call(kernel, in_specs=[pl.BlockSpec(memory_space=pltpu.SMEM)] +...  37.1 us
    ppermute x12, starting transfers between devices, send(): lax.ppermute(part, 'seq', [(i, (i + shift) % seq_parts) for i in range(se...  27.8 us
  transfers between devices with their start and end apart: 76, of which 22 were waited for; matrix products, arithmetic and copies ran while one was open for 24% of the time, Pallas kernels for 28%

profile of v2, /device:TPU:0, one launch (start us, length us, event | category | flops | bytes accessed | tf_op | source)
XLA Modules:
  0.0 658.0 jit_solution(9693264148356040205)
XLA Ops:
  8.5 4.1 collective-permute-start.3
  26.1 13.9 %multiply_sine_fusion = (f32[1536,512]{1,0:T(8,128)}, bf16[1536,512]{1,0:T(8,128)(2,1)}, bf16[1536,512]{1,0:T(8,128)(2,1)}, f32[1536,512]{1,0:T(8,128)}) fusion(f32[512]{0:T(512)S(1)} %multiply_exponential_fusion, f32[1536]{0:T(1024)S(1)} %iota_convert_fusion), kind=kLoop, calls=%fused_computation.11 | loop fusion | flops 2359296 | bytes 9445376 | tf_op jit(solution)/shard_map/sin | solution.py:33
  40.0 4.9 constant_dynamic-slice_fusion.4
  52.6 33.8 %collective-permute-done.4 = bf16[2,256,512]{2,1,0:T(8,128)(2,1)S(1)} collective-permute-done((bf16[2,256,512]{2,1,0:T(8,128)(2,1)S(1)}, bf16[2,256,512]{2,1,0:T(8,128)(2,1)S(1)}, u32[]{:S(2)}, u32[]{:S(2)}) %collective-permute-start.4) | collective-permute-done | bytes 524320 | tf_op jit(solution)/shard_map/ppermute | solution.py:360
  92.8 4.0 pad_maximum_fusion.1.refs_9_.table_ref
  114.7 5.7 norm_context.1
  120.5 7.2 %convolution_convert_fusion.k_ref.refs_0_ = bf16[1536,1024]{1,0:T(8,128)(2,1)} fusion(bf16[1536,1024]{1,0:T(8,128)(2,1)} %bitcast.353, bf16[1024,1024]{1,0:T(8,128)(2,1)S(1)} %copy-done.103), kind=kOutput, calls=%fused_computation.18 | convolution fusion | flops 3222798336 | bytes 8388608 | tf_op jit(solution)/shard_map/dot_general | solution.py:1062
  131.8 6.0 convolution_convert_fusion.1.refs_2_.v_ref
  137.8 3.6 collective-permute-done.10
  150.5 21.0 %attend.2 = (bf16[8,512,1536]{2,1,0:T(8,128)(2,1)}, bf16[512,1024]{1,0:T(8,128)(2,1)}) custom-call(s32[1]{0:T(128)} %dynamic_slice.90.len_ref, bf16[512,1024]{1,0:T(8,128)(2,1)} %get-tuple-element.363.qc_ref, bf16[512,1024]{1,0:T(8,128)(2,1)} %get-tuple-element.362.qp_ref, bf16[1536,1024]{1,0:T(8,128)(2,1)} %convolution_convert_fusion.k_ref.refs_0_, ...), custom_call_target="tpu_custom_call" | custom-call | flops 1024 | bytes 1024 | tf_op jit(solution)/shard_map/attend/pallas_call | solution.py:451
  172.8 5.9 add_and_split.23
  189.3 20.9 %attend.3 = (bf16[8,512,1536]{2,1,0:T(8,128)(2,1)}, bf16[512,1024]{1,0:T(8,128)(2,1)S(1)}) custom-call(s32[1]{0:T(128)} %dynamic_slice.90.len_ref, bf16[512,1024]{1,0:T(8,128)(2,1)} %get-tuple-element.363.qc_ref, bf16[512,1024]{1,0:T(8,128)(2,1)} %get-tuple-element.362.qp_ref, ...), custom_call_target="tpu_custom_call", output_to_operand_aliasing={{0}: (9, {}), {1}: (10, {})} | custom-call | flops 1024 | bytes 1024 | tf_op jit(solution)/shard_map/attend/pallas_call | solution.py:451
  212.4 4.5 add_and_split.24
  222.5 3.1 collective-permute-start.23
  234.1 9.2 %multiply_convert_fusion = (bf16[1024,2048]{1,0:T(8,128)(2,1)}, f32[1024,2048]{1,0:T(8,128)}) fusion(f32[2048]{0:T(1024)S(1)} %bitcast.493, bf16[1024,1024]{1,0:T(8,128)(2,1)S(1)} %bitcast.477, bf16[2048,1024]{1,0:T(8,128)(2,1)S(1)} %bitcast.503), kind=kOutput, calls=%fused_computation.10 | convolution fusion | flops 4315938816 | bytes 18882560 | tf_op jit(solution)/shard_map/dot_general | solution.py:349
  253.5 6.2 convolution_convert_fusion.3
  259.8 13.3 %convert_reduce_fusion = (f32[2048]{0:T(1024)S(1)}, bf16[1024,2048]{1,0:T(8,128)(2,1)S(1)}) fusion(f32[1024,2048]{1,0:T(8,128)} %get-tuple-element.401, f32[2048]{0:T(1024)S(1)} %bitcast.494, bf16[1024,1024]{1,0:T(8,128)(2,1)} %bitcast.480, bf16[2048,1024]{1,0:T(8,128)(2,1)} %bitcast.504), kind=kOutput, calls=%fused_computation.9 | convolution fusion | flops 4343199744 | bytes 18890752 | tf_op jit(solution)/shard_map/dot_general | solution.py:349
  275.1 6.2 convolution_convert_fusion.2
  281.4 8.1 %fusion.48 = f32[2,512,1024]{2,1,0:T(8,128)S(1)} fusion(bf16[2,512,2048]{2,1,0:T(8,128)(2,1)} %bitcast.506, bf16[2048,1024,1]{1,0,2:T(8,128)(2,1)} %bitcast.502), kind=kOutput, calls=%fused_computation.151 | convolution fusion | flops 4294967296 | bytes 12582912 | tf_op jit(solution)/shard_map/dot_general | solution.py:1109
  290.7 4.5 fusion.47
  298.1 3.2 multiply_reduce_fusion
  301.4 4.7 fusion.44
  313.2 20.8 %attend_back.4 = (bf16[6,512,512]{2,1,0:T(8,128)(2,1)}, bf16[6,512,512]{2,1,0:T(8,128)(2,1)}, f32[512,1024]{1,0:T(8,128)}, f32[1024,128]{1,0:T(8,128)S(1)}, f32[...) custom-call(s32[5]{0:T(128)S(1)} %stack.79.bits_ref.refs_0_, ...), custom_call_target="tpu_custom_call", output_to_operand_aliasing={{0}: (15, {}), {1}: (16, {})} | custom-call | flops 1024 | bytes 1024 | tf_op jit(solution)/shard_map/attend_back/pallas_call | solution.py:621
  338.2 5.3 collective-permute-start.19
  343.4 3.1 collective-permute-start.20
  346.5 21.9 %attend_back.5 = (bf16[6,512,512]{2,1,0:T(8,128)(2,1)}, bf16[6,512,512]{2,1,0:T(8,128)(2,1)}, f32[512,1024]{1,0:T(8,128)}, f32[1024,128]{1,0:T(8,128)S(1)}, f32[...) custom-call(s32[5]{0:T(128)S(1)} %stack.79.bits_ref.refs_0_, ...), custom_call_target="tpu_custom_call", output_to_operand_aliasing={{2}: (15, {}), {3}: (16, {}), {4}: (17, {}), {0}: (18, {}),... | custom-call | flops 1024 | bytes 1024 | tf_op jit(solution)/shard_map/attend_back/pallas_call | solution.py:621
  374.8 21.5 %attend_back.6 = (bf16[4,512,512]{2,1,0:T(8,128)(2,1)}, bf16[4,512,512]{2,1,0:T(8,128)(2,1)}, f32[512,1024]{1,0:T(8,128)}, f32[1024,128]{1,0:T(8,128)S(1)}, f32[...) custom-call(s32[5]{0:T(128)S(1)} %stack.79.bits_ref.refs_0_, ...), custom_call_target="tpu_custom_call", output_to_operand_aliasing={{2}: (15, {}), {3}: (16, {}), {4}: (17, {})} | custom-call | flops 1024 | bytes 1024 | tf_op jit(solution)/shard_map/attend_back/pallas_call | solution.py:621
  397.9 4.0 reduce-scatter.9.cloned.1.call-done.refs_2_
  405.0 4.4 add_and_split.25
  418.6 21.6 %attend_back.7 = (bf16[4,512,512]{2,1,0:T(8,128)(2,1)}, bf16[4,512,512]{2,1,0:T(8,128)(2,1)}, f32[512,1024]{1,0:T(8,128)}, f32[1024,128]{1,0:T(8,128)S(1)}, f32[...) custom-call(s32[5]{0:T(128)S(1)} %stack.79.bits_ref.refs_0_, ...), custom_call_target="tpu_custom_call", output_to_operand_aliasing={{2}: (15, {}), {3}: (16, {}), {4}: (17, {}), {0}: (18, {}),... | custom-call | flops 1024 | bytes 1024 | tf_op jit(solution)/shard_map/attend_back/pallas_call | solution.py:621
  452.2 5.5 copy.150
  457.7 3.0 bitcast_convert_fusion
  471.7 2.9 add_and_split.27
  489.5 14.4 %collective-permute-done.36 = bf16[6,64,512]{2,1,0:T(8,128)(2,1)S(1)} collective-permute-done((bf16[6,64,512]{2,1,0:T(8,128)(2,1)S(1)}, bf16[6,64,512]{2,1,0:T(8,128)(2,1)S(1)}, u32[]{:S(2)}, u32[]{:S(2)}) %collective-permute-start.36) | collective-permute-done | bytes 393248 | tf_op jit(solution)/shard_map/ppermute | solution.py:360
  510.6 8.4 %collective-permute-done.40.refs_1_ = bf16[6,32,512]{2,1,0:T(8,128)(2,1)S(1)} collective-permute-done((bf16[6,32,512]{2,1,0:T(8,128)(2,1)S(1)}, bf16[6,32,512]{2,1,0:T(8,128)(2,1)S(1)}, u32[]{:S(2)}, u32[]{:S(2)}) %collective-permute-start.40) | collective-permute-done | bytes 196640 | tf_op jit(solution)/shard_map/ppermute | solution.py:360
  519.1 3.2 collective-permute-done.42
  531.2 6.8 %collective-permute-done.44 = bf16[6,32,512]{2,1,0:T(8,128)(2,1)S(1)} collective-permute-done((bf16[6,32,512]{2,1,0:T(8,128)(2,1)S(1)}, bf16[6,32,512]{2,1,0:T(8,128)(2,1)S(1)}, u32[]{:S(2)}, u32[]{:S(2)}) %collective-permute-start.44) | collective-permute-done | bytes 196640 | tf_op jit(solution)/shard_map/ppermute | solution.py:360
  543.7 4.1 convert_element_type.214.refs_8_
  548.4 9.2 %collective-permute-done.49.refs_3_ = bf16[4,32,512]{2,1,0:T(8,128)(2,1)S(1)} collective-permute-done((bf16[4,32,512]{2,1,0:T(8,128)(2,1)S(1)}, bf16[4,32,512]{2,1,0:T(8,128)(2,1)S(1)}, u32[]{:S(2)}, u32[]{:S(2)}) %collective-permute-start.49) | collective-permute-done | bytes 131104 | tf_op jit(solution)/shard_map/ppermute | solution.py:360
  568.9 4.1 convert_bitcast_fusion.refs_11_
  576.1 4.1 collective-permute-done.55
  585.1 3.2 collective-permute-start.32
  588.8 7.1 %collective-permute-done.32.refs_3_.refs_10_ = bf16[128,1024]{1,0:T(8,128)(2,1)S(1)} collective-permute-done((bf16[128,1024]{1,0:T(8,128)(2,1)S(1)}, bf16[128,1024]{1,0:T(8,128)(2,1)S(1)}, u32[]{:S(2)}, u32[]{:S(2)}) %collective-permute-start.32) | collective-permute-done | bytes 262176 | tf_op jit(solution)/shard_map/ppermute | solution.py:1035
  597.5 4.9 collective-permute-done.61.refs_9_
  602.4 3.1 add_and_split.33
  615.8 6.9 %finish.2 = (f32[1024,1024]{1,0:T(8,128)}, f32[1024,1024]{1,0:T(8,128)}, f32[1024,1024]{1,0:T(8,128)}, f32[1024,1024]{1,0:T(8,128)}, f32[1024,1024]{1,0:T(8,128)}) custom-call(s32[5]{0:T(128)S(1)} %stack.79.bits_ref.refs_0_, bf16[6,512,512]{2,1,0:T(8,128)(2,1)S(1)} %bitcast.367, bf16[6,512,512]{2,1,0:T(8,128)(2,1)} %collective-permute-done.65.got_ref), custom_call_target="tpu_custom_call" | custom-call | flops 1024 | bytes 1024 | tf_op jit(solution)/shard_map/finish/pallas_call | solution.py:799
  624.6 12.3 %collective-permute-done.66 = bf16[2,256,512]{2,1,0:T(8,128)(2,1)S(1)} collective-permute-done((bf16[2,256,512]{2,1,0:T(8,128)(2,1)S(1)}, bf16[2,256,512]{2,1,0:T(8,128)(2,1)S(1)}, u32[]{:S(2)}, u32[]{:S(2)}) %collective-permute-start.66) | collective-permute-done | bytes 524320 | tf_op jit(solution)/shard_map/ppermute | solution.py:360
  645.6 5.3 finish.3
  (531 shorter events, 235.8 us)
Async XLA Ops:
  7.2 236.2 %all-gather.4.cloned.1.call-start = ((), (), s32[]{:S(2)}) async-start(), calls=%async_computation.4 | async-start | bytes 5242880 | tf_op jit(solution)/shard_map/all_gather | solution.py:1067
  8.5 16.0 %collective-permute-start.3 = (bf16[2,128,512]{2,1,0:T(8,128)(2,1)S(1)}, bf16[2,128,512]{2,1,0:T(8,128)(2,1)S(1)}, u32[]{:S(2)}, u32[]{:S(2)}) collective-permute-start(bf16[2,128,512]{2,1,0:T(8,128)(2,1)S(1)} %bitcast.380), channel_id=1, source_target_pairs={{0,2},{1,3},{2,0},{3,1},{4,6},{5,7},{6,4},{7,5},{8,10},{9,11},{10,... | collective-permute-start | bytes 786440 | tf_op jit(solution)/shard_map/ppermute | solution.py:360
  20.5 88.7 %collective-permute-start = (bf16[384,1024]{1,0:T(8,128)(2,1)}, bf16[384,1024]{1,0:T(8,128)(2,1)}, u32[]{:S(2)}, u32[]{:S(2)}) collective-permute-start(bf16[384,1024]{1,0:T(8,128)(2,1)} %get-tuple-element.355), channel_id=1, source_target_pairs={{0,1},{1,2},{2,3},{3,0},{4,5},{5,6},{6,7},{7,4},{8,9},{9,10},{10,1... | collective-permute-start | bytes 2359304 | tf_op jit(solution)/shard_map/ppermute | solution.py:1035
  22.1 87.7 %collective-permute-start.1 = (bf16[384,1024]{1,0:T(8,128)(2,1)}, bf16[384,1024]{1,0:T(8,128)(2,1)}, u32[]{:S(2)}, u32[]{:S(2)}) collective-permute-start(bf16[384,1024]{1,0:T(8,128)(2,1)} %get-tuple-element.354), channel_id=1, source_target_pairs={{0,2},{1,3},{2,0},{3,1},{4,6},{5,7},{6,4},{7,5},{8,10},{9,11},{10,... | collective-permute-start | bytes 2359304 | tf_op jit(solution)/shard_map/ppermute | solution.py:1035
  22.4 87.3 %collective-permute-start.2 = (bf16[384,1024]{1,0:T(8,128)(2,1)}, bf16[384,1024]{1,0:T(8,128)(2,1)}, u32[]{:S(2)}, u32[]{:S(2)}) collective-permute-start(bf16[384,1024]{1,0:T(8,128)(2,1)} %get-tuple-element.353), channel_id=1, source_target_pairs={{0,3},{1,0},{2,1},{3,2},{4,7},{5,4},{6,5},{7,6},{8,11},{9,8},{10,9... | collective-permute-start | bytes 2359304 | tf_op jit(solution)/shard_map/ppermute | solution.py:1035
  25.1 61.3 %collective-permute-start.4 = (bf16[2,256,512]{2,1,0:T(8,128)(2,1)S(1)}, bf16[2,256,512]{2,1,0:T(8,128)(2,1)S(1)}, u32[]{:S(2)}, u32[]{:S(2)}) collective-permute-start(bf16[2,256,512]{2,1,0:T(8,128)(2,1)S(1)} %bitcast.373), channel_id=1, source_target_pairs={{0,1},{1,0},{2,3},{3,2},{4,5},{5,4},{6,7},{7,6},{8,9},{9,8},{10,11... | collective-permute-start | bytes 1572872 | tf_op jit(solution)/shard_map/ppermute | solution.py:360
  103.5 24.1 %collective-permute-start.9 = (bf16[2,128,512]{2,1,0:T(8,128)(2,1)S(1)}, bf16[2,128,512]{2,1,0:T(8,128)(2,1)S(1)}, u32[]{:S(2)}, u32[]{:S(2)}) collective-permute-start(bf16[2,128,512]{2,1,0:T(8,128)(2,1)S(1)} %bitcast.368), channel_id=1, source_target_pairs={{0,2},{1,3},{2,0},{3,1},{4,6},{5,7},{6,4},{7,5},{8,10},{9,11},{10,... | collective-permute-start | bytes 786440 | tf_op jit(solution)/shard_map/ppermute | solution.py:360
  107.7 63.8 %collective-permute-start.7 = (bf16[1,1024,512]{2,1,0:T(8,128)(2,1)}, bf16[1,1024,512]{2,1,0:T(8,128)(2,1)}, u32[]{:S(2)}, u32[]{:S(2)}) collective-permute-start(bf16[1,1024,512]{2,1,0:T(8,128)(2,1)} %bitcast.32.refs_6_), channel_id=1, source_target_pairs={{0,16},{4,20},{8,24},{12,28},{16,0},{20,4},{24,8},{28,12},{1,17},{... | collective-permute-start | bytes 3145736 | tf_op jit(solution)/shard_map/ppermute | solution.py:360
  109.2 62.3 %collective-permute-start.8 = (bf16[1,1024,512]{2,1,0:T(8,128)(2,1)}, bf16[1,1024,512]{2,1,0:T(8,128)(2,1)}, u32[]{:S(2)}, u32[]{:S(2)}) collective-permute-start(bf16[1,1024,512]{2,1,0:T(8,128)(2,1)} %bitcast.33.refs_7_), channel_id=1, source_target_pairs={{0,8},{4,12},{8,0},{12,4},{16,24},{20,28},{24,16},{28,20},{1,9},{5... | collective-permute-start | bytes 3145736 | tf_op jit(solution)/shard_map/ppermute | solution.py:360
  131.3 204.3 %reduce-scatter.5.cloned.1.call-start = ((), (), s32[]{:S(2)}) async-start(), calls=%async_computation.5 | async-start | bytes 5242880 | tf_op jit(solution)/shard_map/reduce_scatter | solution.py:1103
  143.7 27.8 %collective-permute-start.11 = (bf16[1,512,512]{2,1,0:T(8,128)(2,1)}, bf16[1,512,512]{2,1,0:T(8,128)(2,1)}, u32[]{:S(2)}, u32[]{:S(2)}) collective-permute-start(bf16[1,512,512]{2,1,0:T(8,128)(2,1)} %bitcast.51.rest_0_), channel_id=1, source_target_pairs={{0,8},{4,12},{8,0},{12,4},{16,24},{20,28},{24,16},{28,20},{1,9},{5... | collective-permute-start | bytes 1572872 | tf_op jit(solution)/shard_map/ppermute | solution.py:360
  145.3 26.2 %collective-permute-start.12 = (bf16[1,512,512]{2,1,0:T(8,128)(2,1)}, bf16[1,512,512]{2,1,0:T(8,128)(2,1)}, u32[]{:S(2)}, u32[]{:S(2)}) collective-permute-start(bf16[1,512,512]{2,1,0:T(8,128)(2,1)} %bitcast.54.rest_1_), channel_id=1, source_target_pairs={{0,16},{4,20},{8,24},{12,28},{16,0},{20,4},{24,8},{28,12},{1,17},{... | collective-permute-start | bytes 1572872 | tf_op jit(solution)/shard_map/ppermute | solution.py:360
  179.6 31.5 %collective-permute-start.13 = (bf16[1,1024,512]{2,1,0:T(8,128)(2,1)}, bf16[1,1024,512]{2,1,0:T(8,128)(2,1)}, u32[]{:S(2)}, u32[]{:S(2)}) collective-permute-start(bf16[1,1024,512]{2,1,0:T(8,128)(2,1)} %bitcast.57.rest_2_), channel_id=1, source_target_pairs={{0,16},{4,20},{8,24},{12,28},{16,0},{20,4},{24,8},{28,12},{1,17},{... | collective-permute-start | bytes 3145736 | tf_op jit(solution)/shard_map/ppermute | solution.py:360
  181.1 30.1 %collective-permute-start.14 = (bf16[1,1024,512]{2,1,0:T(8,128)(2,1)}, bf16[1,1024,512]{2,1,0:T(8,128)(2,1)}, u32[]{:S(2)}, u32[]{:S(2)}) collective-permute-start(bf16[1,1024,512]{2,1,0:T(8,128)(2,1)} %bitcast.59.rest_3_), channel_id=1, source_target_pairs={{0,8},{4,12},{8,0},{12,4},{16,24},{20,28},{24,16},{28,20},{1,9},{5... | collective-permute-start | bytes 3145736 | tf_op jit(solution)/shard_map/ppermute | solution.py:360
  220.9 22.5 %collective-permute-start.22 = (bf16[128,1024]{1,0:T(8,128)(2,1)S(1)}, bf16[128,1024]{1,0:T(8,128)(2,1)S(1)}, u32[]{:S(2)}, u32[]{:S(2)}) collective-permute-start(bf16[128,1024]{1,0:T(8,128)(2,1)S(1)} %bitcast.379), channel_id=1, source_target_pairs={{0,1},{1,2},{2,3},{3,0},{4,5},{5,6},{6,7},{7,4},{8,9},{9,10},{10,1... | collective-permute-start | bytes 786440 | tf_op jit(solution)/shard_map/ppermute | solution.py:1035
  222.5 20.9 %collective-permute-start.23 = (bf16[128,1024]{1,0:T(8,128)(2,1)S(1)}, bf16[128,1024]{1,0:T(8,128)(2,1)}, u32[]{:S(2)}, u32[]{:S(2)}) collective-permute-start(bf16[128,1024]{1,0:T(8,128)(2,1)S(1)} %bitcast.377), channel_id=1, source_target_pairs={{0,2},{1,3},{2,0},{3,1},{4,6},{5,7},{6,4},{7,5},{8,10},{9,11},{10,... | collective-permute-start | bytes 786440 | tf_op jit(solution)/shard_map/ppermute | solution.py:1035
  225.5 17.8 %collective-permute-start.24 = (bf16[128,1024]{1,0:T(8,128)(2,1)S(1)}, bf16[128,1024]{1,0:T(8,128)(2,1)}, u32[]{:S(2)}, u32[]{:S(2)}) collective-permute-start(bf16[128,1024]{1,0:T(8,128)(2,1)S(1)} %bitcast.375), channel_id=1, source_target_pairs={{0,3},{1,0},{2,1},{3,2},{4,7},{5,4},{6,5},{7,6},{8,11},{9,8},{10,9... | collective-permute-start | bytes 786440 | tf_op jit(solution)/shard_map/ppermute | solution.py:1035
  259.7 113.0 %reduce-scatter.7.cloned.1.call-start = ((), (), s32[]{:S(2)}) async-start(), calls=%async_computation.6 | async-start | bytes 5242880 | tf_op jit(solution)/shard_map/reduce_scatter | solution.py:1103
  281.3 120.7 %reduce-scatter.9.cloned.1.call-start = ((), (), s32[]{:S(2)}) async-start(), calls=%async_computation.7 | async-start | bytes 1310720 | tf_op jit(solution)/shard_map/reduce_scatter | solution.py:1143
  336.2 127.3 %reduce-scatter.11.cloned.1.call-start = ((), (), s32[]{:S(2)}) async-start(), calls=%async_computation.8 | async-start | bytes 1310720 | tf_op jit(solution)/shard_map/reduce_scatter | solution.py:1148
  338.2 30.8 %collective-permute-start.19 = (bf16[128,1024]{1,0:T(8,128)(2,1)S(1)}, bf16[128,1024]{1,0:T(8,128)(2,1)S(1)}, u32[]{:S(2)}, u32[]{:S(2)}) collective-permute-start(bf16[128,1024]{1,0:T(8,128)(2,1)S(1)} %get-tuple-element.372.rest_5_), channel_id=1, source_target_pairs={{0,1},{1,2},{2,3},{3,0},{4,5},{5,6},{6,7},{7,4},{8,9},{9,10},{10,1... | collective-permute-start | bytes 786440 | tf_op jit(solution)/shard_map/ppermute | solution.py:1035
  343.4 25.6 %collective-permute-start.20 = (bf16[128,1024]{1,0:T(8,128)(2,1)S(1)}, bf16[128,1024]{1,0:T(8,128)(2,1)S(1)}, u32[]{:S(2)}, u32[]{:S(2)}) collective-permute-start(bf16[128,1024]{1,0:T(8,128)(2,1)S(1)} %get-tuple-element.371.rest_6_), channel_id=1, source_target_pairs={{0,2},{1,3},{2,0},{3,1},{4,6},{5,7},{6,4},{7,5},{8,10},{9,11},{10,... | collective-permute-start | bytes 786440 | tf_op jit(solution)/shard_map/ppermute | solution.py:1035
  346.5 22.5 %collective-permute-start.21 = (bf16[128,1024]{1,0:T(8,128)(2,1)S(1)}, bf16[128,1024]{1,0:T(8,128)(2,1)S(1)}, u32[]{:S(2)}, u32[]{:S(2)}) collective-permute-start(bf16[128,1024]{1,0:T(8,128)(2,1)S(1)} %get-tuple-element.370.rest_7_), channel_id=1, source_target_pairs={{0,3},{1,0},{2,1},{3,2},{4,7},{5,4},{6,5},{7,6},{8,11},{9,8},{10,9... | collective-permute-start | bytes 786440 | tf_op jit(solution)/shard_map/ppermute | solution.py:1035
  372.7 29.3 %collective-permute-start.27 = (bf16[6,512,512]{2,1,0:T(8,128)(2,1)}, bf16[6,512,512]{2,1,0:T(8,128)(2,1)}, u32[]{:S(2)}, u32[]{:S(2)}) collective-permute-start(bf16[6,512,512]{2,1,0:T(8,128)(2,1)} %get-tuple-element.192.rest_3_), channel_id=1, source_target_pairs={{0,4},{4,0},{8,12},{12,8},{16,20},{20,16},{24,28},{28,24},{1,5},{5... | collective-permute-start | bytes 9437192 | tf_op jit(solution)/shard_map/ppermute | solution.py:360
  372.7 171.0 %all-gather.6.cloned.1.call-start = ((), (), s32[]{:S(2)}) async-start(), calls=%async_computation.9 | async-start | bytes 2359296 | tf_op jit(solution)/shard_map/all_gather | solution.py:1152
  413.4 155.5 %all-gather.8.cloned.1.call-start = ((), (), s32[]{:S(2)}) async-start(), calls=%async_computation.10 | async-start | bytes 2359296 | tf_op jit(solution)/shard_map/all_gather | solution.py:1230
  413.5 28.3 %collective-permute-start.28 = (bf16[3,256,512]{2,1,0:T(8,128)(2,1)}, bf16[3,256,512]{2,1,0:T(8,128)(2,1)S(1)}, u32[]{:S(2)}, u32[]{:S(2)}) collective-permute-start(bf16[3,256,512]{2,1,0:T(8,128)(2,1)} %bitcast.93.rest_5_), channel_id=1, source_target_pairs={{0,16},{4,20},{8,24},{12,28},{16,0},{20,4},{24,8},{28,12},{1,17},{... | collective-permute-start | bytes 2359304 | tf_op jit(solution)/shard_map/ppermute | solution.py:360
  415.0 26.8 %collective-permute-start.29 = (bf16[3,256,512]{2,1,0:T(8,128)(2,1)}, bf16[3,256,512]{2,1,0:T(8,128)(2,1)S(1)}, u32[]{:S(2)}, u32[]{:S(2)}) collective-permute-start(bf16[3,256,512]{2,1,0:T(8,128)(2,1)} %bitcast.391), channel_id=1, source_target_pairs={{0,8},{4,12},{8,0},{12,4},{16,24},{20,28},{24,16},{28,20},{1,9},{5... | collective-permute-start | bytes 2359304 | tf_op jit(solution)/shard_map/ppermute | solution.py:360
  447.9 18.8 %collective-permute-start.35 = (bf16[4,512,512]{2,1,0:T(8,128)(2,1)}, bf16[4,512,512]{2,1,0:T(8,128)(2,1)}, u32[]{:S(2)}, u32[]{:S(2)}) collective-permute-start(bf16[4,512,512]{2,1,0:T(8,128)(2,1)} %get-tuple-element.225), channel_id=1, source_target_pairs={{0,4},{4,0},{8,12},{12,8},{16,20},{20,16},{24,28},{28,24},{1,5},{5... | collective-permute-start | bytes 6291464 | tf_op jit(solution)/shard_map/ppermute | solution.py:360
  451.6 14.3 %collective-permute-start.34 = (bf16[3,128,512]{2,1,0:T(8,128)(2,1)S(1)}, bf16[3,128,512]{2,1,0:T(8,128)(2,1)S(1)}, u32[]{:S(2)}, u32[]{:S(2)}) collective-permute-start(bf16[3,128,512]{2,1,0:T(8,128)(2,1)S(1)} %bitcast.457), channel_id=1, source_target_pairs={{0,16},{4,20},{8,24},{12,28},{16,0},{20,4},{24,8},{28,12},{1,17},{... | collective-permute-start | bytes 1179656 | tf_op jit(solution)/shard_map/ppermute | solution.py:360
  462.1 27.4 %collective-permute-start.39 = (bf16[1,1536,256]{2,1,0:T(8,128)(2,1)}, bf16[1,1536,256]{2,1,0:T(8,128)(2,1)}, u32[]{:S(2)}, u32[]{:S(2)}) collective-permute-start(bf16[1,1536,256]{2,1,0:T(8,128)(2,1)} %get-tuple-element.364), channel_id=1, source_target_pairs={{0,4},{4,0},{8,12},{12,8},{16,20},{20,16},{24,28},{28,24},{1,5},{5... | collective-permute-start | bytes 2359304 | tf_op jit(solution)/shard_map/ppermute | solution.py:360
  483.8 20.1 %collective-permute-start.37 = (bf16[2,256,512]{2,1,0:T(8,128)(2,1)}, bf16[2,256,512]{2,1,0:T(8,128)(2,1)S(1)}, u32[]{:S(2)}, u32[]{:S(2)}) collective-permute-start(bf16[2,256,512]{2,1,0:T(8,128)(2,1)} %bitcast.455), channel_id=1, source_target_pairs={{0,16},{4,20},{8,24},{12,28},{16,0},{20,4},{24,8},{28,12},{1,17},{... | collective-permute-start | bytes 1572872 | tf_op jit(solution)/shard_map/ppermute | solution.py:360
  485.3 18.6 %collective-permute-start.38 = (bf16[2,256,512]{2,1,0:T(8,128)(2,1)S(1)}, bf16[2,256,512]{2,1,0:T(8,128)(2,1)S(1)}, u32[]{:S(2)}, u32[]{:S(2)}) collective-permute-start(bf16[2,256,512]{2,1,0:T(8,128)(2,1)S(1)} %bitcast.454), channel_id=1, source_target_pairs={{0,8},{4,12},{8,0},{12,4},{16,24},{20,28},{24,16},{28,20},{1,9},{5... | collective-permute-start | bytes 1572872 | tf_op jit(solution)/shard_map/ppermute | solution.py:360
  486.0 24.6 %collective-permute-start.30 = (bf16[128,1024]{1,0:T(8,128)(2,1)S(1)}, bf16[128,1024]{1,0:T(8,128)(2,1)S(1)}, u32[]{:S(2)}, u32[]{:S(2)}) collective-permute-start(bf16[128,1024]{1,0:T(8,128)(2,1)S(1)} %get-tuple-element.368.refs_9_), channel_id=1, source_target_pairs={{0,1},{1,2},{2,3},{3,0},{4,5},{5,6},{6,7},{7,4},{8,9},{9,10},{10,1... | collective-permute-start | bytes 786440 | tf_op jit(solution)/shard_map/ppermute | solution.py:1035
  488.0 15.9 %collective-permute-start.36 = (bf16[6,64,512]{2,1,0:T(8,128)(2,1)S(1)}, bf16[6,64,512]{2,1,0:T(8,128)(2,1)S(1)}, u32[]{:S(2)}, u32[]{:S(2)}) collective-permute-start(bf16[6,64,512]{2,1,0:T(8,128)(2,1)S(1)} %bitcast.456), channel_id=1, source_target_pairs={{0,1},{1,0},{2,3},{3,2},{4,5},{5,4},{6,7},{7,6},{8,9},{9,8},{10,11... | collective-permute-start | bytes 1179656 | tf_op jit(solution)/shard_map/ppermute | solution.py:360
  506.0 16.3 %collective-permute-start.43 = (bf16[1,768,256]{2,1,0:T(8,128)(2,1)S(1)}, bf16[1,768,256]{2,1,0:T(8,128)(2,1)S(1)}, u32[]{:S(2)}, u32[]{:S(2)}) collective-permute-start(bf16[1,768,256]{2,1,0:T(8,128)(2,1)S(1)} %bitcast.459), channel_id=1, source_target_pairs={{0,16},{4,20},{8,24},{12,28},{16,0},{20,4},{24,8},{28,12},{1,17},{... | collective-permute-start | bytes 1179656 | tf_op jit(solution)/shard_map/ppermute | solution.py:360
  507.9 14.3 %collective-permute-start.42 = (bf16[2,128,512]{2,1,0:T(8,128)(2,1)S(1)}, bf16[2,128,512]{2,1,0:T(8,128)(2,1)S(1)}, u32[]{:S(2)}, u32[]{:S(2)}) collective-permute-start(bf16[2,128,512]{2,1,0:T(8,128)(2,1)S(1)} %bitcast.460), channel_id=1, source_target_pairs={{0,16},{4,20},{8,24},{12,28},{16,0},{20,4},{24,8},{28,12},{1,17},{... | collective-permute-start | bytes 786440 | tf_op jit(solution)/shard_map/ppermute | solution.py:360
  510.6 20.6 %collective-permute-start.47 = (f32[1,96,128]{2,1,0:T(8,128)S(1)}, f32[1,96,128]{2,1,0:T(8,128)S(1)}, u32[]{:S(2)}, u32[]{:S(2)}) collective-permute-start(f32[1,96,128]{2,1,0:T(8,128)S(1)} %bitcast.451), channel_id=1, source_target_pairs={{0,4},{4,0},{8,12},{12,8},{16,20},{20,16},{24,28},{28,24},{1,5},{5... | collective-permute-start | bytes 147464 | tf_op jit(solution)/shard_map/ppermute | solution.py:360
  523.1 14.9 %collective-permute-start.45 = (bf16[4,64,512]{2,1,0:T(8,128)(2,1)S(1)}, bf16[4,64,512]{2,1,0:T(8,128)(2,1)S(1)}, u32[]{:S(2)}, u32[]{:S(2)}) collective-permute-start(bf16[4,64,512]{2,1,0:T(8,128)(2,1)S(1)} %bitcast.462), channel_id=1, source_target_pairs={{0,1},{1,0},{2,3},{3,2},{4,5},{5,4},{6,7},{7,6},{8,9},{9,8},{10,11... | collective-permute-start | bytes 786440 | tf_op jit(solution)/shard_map/ppermute | solution.py:360
  538.7 19.6 %collective-permute-start.48 = (bf16[6,64,512]{2,1,0:T(8,128)(2,1)S(1)}, bf16[6,64,512]{2,1,0:T(8,128)(2,1)S(1)}, u32[]{:S(2)}, u32[]{:S(2)}) collective-permute-start(bf16[6,64,512]{2,1,0:T(8,128)(2,1)S(1)} %bitcast.416), channel_id=1, source_target_pairs={{0,1},{1,0},{2,3},{3,2},{4,5},{5,4},{6,7},{7,6},{8,9},{9,8},{10,11... | collective-permute-start | bytes 1179656 | tf_op jit(solution)/shard_map/ppermute | solution.py:360
  538.8 29.5 %collective-permute-start.31 = (bf16[128,1024]{1,0:T(8,128)(2,1)S(1)}, bf16[128,1024]{1,0:T(8,128)(2,1)S(1)}, u32[]{:S(2)}, u32[]{:S(2)}) collective-permute-start(bf16[128,1024]{1,0:T(8,128)(2,1)S(1)} %get-tuple-element.367.refs_10_), channel_id=1, source_target_pairs={{0,2},{1,3},{2,0},{3,1},{4,6},{5,7},{6,4},{7,5},{8,10},{9,11},{10,... | collective-permute-start | bytes 786440 | tf_op jit(solution)/shard_map/ppermute | solution.py:1035
  541.6 16.1 %collective-permute-start.50 = (bf16[1,384,256]{2,1,0:T(8,128)(2,1)S(1)}, bf16[1,384,256]{2,1,0:T(8,128)(2,1)S(1)}, u32[]{:S(2)}, u32[]{:S(2)}) collective-permute-start(bf16[1,384,256]{2,1,0:T(8,128)(2,1)S(1)} %get-tuple-element.255), channel_id=1, source_target_pairs={{0,8},{4,12},{8,0},{12,4},{16,24},{20,28},{24,16},{28,20},{1,9},{5... | collective-permute-start | bytes 589832 | tf_op jit(solution)/shard_map/ppermute | solution.py:360
  543.0 14.6 %collective-permute-start.49 = (bf16[4,32,512]{2,1,0:T(8,128)(2,1)S(1)}, bf16[4,32,512]{2,1,0:T(8,128)(2,1)S(1)}, u32[]{:S(2)}, u32[]{:S(2)}) collective-permute-start(bf16[4,32,512]{2,1,0:T(8,128)(2,1)S(1)} %bitcast.465), channel_id=1, source_target_pairs={{0,2},{1,3},{2,0},{3,1},{4,6},{5,7},{6,4},{7,5},{8,10},{9,11},{10,... | collective-permute-start | bytes 393224 | tf_op jit(solution)/shard_map/ppermute | solution.py:360
  583.9 18.5 %collective-permute-start.57 = (bf16[3,256,512]{2,1,0:T(8,128)(2,1)S(1)}, bf16[3,256,512]{2,1,0:T(8,128)(2,1)S(1)}, u32[]{:S(2)}, u32[]{:S(2)}) collective-permute-start(bf16[3,256,512]{2,1,0:T(8,128)(2,1)S(1)} %bitcast.384), channel_id=1, source_target_pairs={{0,16},{4,20},{8,24},{12,28},{16,0},{20,4},{24,8},{28,12},{1,17},{... | collective-permute-start | bytes 2359304 | tf_op jit(solution)/shard_map/ppermute | solution.py:360
  584.6 17.9 %collective-permute-start.58 = (bf16[3,256,512]{2,1,0:T(8,128)(2,1)S(1)}, bf16[3,256,512]{2,1,0:T(8,128)(2,1)S(1)}, u32[]{:S(2)}, u32[]{:S(2)}) collective-permute-start(bf16[3,256,512]{2,1,0:T(8,128)(2,1)S(1)} %bitcast.385), channel_id=1, source_target_pairs={{0,8},{4,12},{8,0},{12,4},{16,24},{20,28},{24,16},{28,20},{1,9},{5... | collective-permute-start | bytes 2359304 | tf_op jit(solution)/shard_map/ppermute | solution.py:360
  585.1 17.3 %collective-permute-start.60 = (bf16[1,1536,256]{2,1,0:T(8,128)(2,1)S(1)}, bf16[1,1536,256]{2,1,0:T(8,128)(2,1)S(1)}, u32[]{:S(2)}, u32[]{:S(2)}) collective-permute-start(bf16[1,1536,256]{2,1,0:T(8,128)(2,1)S(1)} %bitcast.386), channel_id=1, source_target_pairs={{0,4},{4,0},{8,12},{12,8},{16,20},{20,16},{24,28},{28,24},{1,5},{5... | collective-permute-start | bytes 2359304 | tf_op jit(solution)/shard_map/ppermute | solution.py:360
  605.6 17.1 %collective-permute-start.62 = (bf16[2,128,512]{2,1,0:T(8,128)(2,1)S(1)}, bf16[2,128,512]{2,1,0:T(8,128)(2,1)S(1)}, u32[]{:S(2)}, u32[]{:S(2)}) collective-permute-start(bf16[2,128,512]{2,1,0:T(8,128)(2,1)S(1)} %bitcast.424), channel_id=1, source_target_pairs={{0,8},{4,12},{8,0},{12,4},{16,24},{20,28},{24,16},{28,20},{1,9},{5... | collective-permute-start | bytes 786440 | tf_op jit(solution)/shard_map/ppermute | solution.py:360
  607.1 15.6 %collective-permute-start.63 = (bf16[2,128,512]{2,1,0:T(8,128)(2,1)S(1)}, bf16[2,128,512]{2,1,0:T(8,128)(2,1)S(1)}, u32[]{:S(2)}, u32[]{:S(2)}) collective-permute-start(bf16[2,128,512]{2,1,0:T(8,128)(2,1)S(1)} %bitcast.426), channel_id=1, source_target_pairs={{0,16},{4,20},{8,24},{12,28},{16,0},{20,4},{24,8},{28,12},{1,17},{... | collective-permute-start | bytes 786440 | tf_op jit(solution)/shard_map/ppermute | solution.py:360
  (167 other events, 1097.1 us)
Sparse Core Ops, SparseCore 0:
  131.4 80.4 all-gather.3
  259.8 56.2 reduce-scatter.4
  319.9 52.6 reduce-scatter.6
  374.8 27.1 reduce-scatter.8
  404.2 25.8 reduce-scatter.10
  431.8 29.1 all-gather.5
  478.9 30.9 all-gather.7

commit v3 on v2

--- a/solution.py
+++ b/solution.py
@@ -959,6 +959,58 @@
     return results[len(out_shape) :]
 
 
+def input_grad_kernel(targets_ref, d_rows_ref, x_ref, d_hidden_ref, gain_ref, *outs):
+    block = outs[0].shape[0]
+    for i, out in enumerate(outs):
+        at = pl.ds(pl.multiple_of(targets_ref[i] * block, block), block)
+        values = x_ref[at, :].astype(F32)
+        center = values - jnp.mean(values, -1, keepdims=True)
+        spread = jnp.mean(center * center, -1, keepdims=True)
+        inverse = lax.rsqrt(spread + 1e-05)
+        unit = center * inverse
+        grad = d_rows_ref[at, :] * gain_ref[...]
+        mean = jnp.mean(grad, -1, keepdims=True)
+        along = jnp.mean(grad * unit, -1, keepdims=True)
+        out[...] = (d_hidden_ref[at, :] + inverse * (grad - mean - unit * along)).astype(BF16)
+
+
+def input_grad(targets, d_rows, rows, d_hidden, gain, count):
+    block = jax.ShapeDtypeStruct((rows.shape[0] // count, rows.shape[1]), BF16)
+    return pl.pallas_call(
+        input_grad_kernel,
+        in_specs=[pl.BlockSpec(memory_space=pltpu.SMEM)] + [in_vmem()] * 4,
+        out_specs=[in_vmem()] * count,
+        out_shape=[block] * count,
+        compiler_params=pltpu.CompilerParams(vmem_limit_bytes=48 * MIB),
+        cost_estimate=SHORT,
+        name="input_grad",
+    )(targets, d_rows, rows, d_hidden, gain.reshape(1, -1))
+
+
+def widen_kernel(rows_ref, out_ref):
+    out_ref[...] = rows_ref[...].astype(F32)
+
+
+def widen_flip_kernel(rows_ref, out_ref):
+    out_ref[...] = rows_ref[...].astype(F32).T
+
+
+def widen(rows, flip=False):
+    count, width = rows.shape
+    block = count // 4
+    out = pl.BlockSpec((width, block), lambda i: (0, i)) if flip else pl.BlockSpec((block, width), lambda i: (i, 0))
+    return pl.pallas_call(
+        widen_flip_kernel if flip else widen_kernel,
+        grid=(4,),
+        in_specs=[pl.BlockSpec((block, width), lambda i: (i, 0))],
+        out_specs=out,
+        out_shape=jax.ShapeDtypeStruct((width, count) if flip else (count, width), F32),
+        compiler_params=pltpu.CompilerParams(vmem_limit_bytes=48 * MIB),
+        cost_estimate=SHORT,
+        name="widen",
+    )(rows)
+
+
 def own_streams_plan(
     inputs,
     memory,
@@ -1047,12 +1099,12 @@
     parts = send(parts_for(jnp.concatenate(blocks, 1)))
     down_piece = lax.dynamic_slice_in_dim(w_down, place * piece + order_two, piece, 0)
     down_chain = gathered(down_piece)
-    round_of([up_chain], bits, bit_names)
     go_parts = parts_for(by_stream(grad_out))
     memory_rows = by_stream(memory)
     idle = [*up_chain.gives, *down_chain.gives, table, cos, sin, *go_parts, memory_rows]
     normed, x_rows = norm_context(parts, owners, gain_first, shift_first, idle)
     length = lax.dynamic_slice_in_dim(seg_len, me, 1)
+    round_of([up_chain], bits, bit_names, [normed])
     order = token(normed)
     bias_all = lax.dynamic_slice_in_dim(bias_up.reshape(-1, 2, piece), core_bit + order, 1, 1)
     bias_all = bias_all.reshape(1, -1)
@@ -1063,11 +1115,11 @@
     values = jnp.dot(normed, w_value, preferred_element_type=F32).astype(BF16)
     content = (queries + bias_content).astype(BF16)
     position = (queries + bias_position).astype(BF16)
-    memory_rows = copy_after(memory_rows, keys)
-    memory_all = lax.all_gather(memory_rows, "seq", axis=1, tiled=True)
     given = (length, content, position, keys, values, w_rel, table, cos, sin)
     round_of([down_chain], bits, bit_names, [normed])
     round_of([down_chain], bits, bit_names, [values])
+    memory_rows = copy_after(memory_rows, down_chain.gives[0])
+    memory_all = lax.all_gather(memory_rows, "seq", axis=1, tiled=True)
     prob, attn_out = attend(range(H // 2), *given, first=down_chain.gives)
     prob, attn_out = round_of([up_chain, down_chain], bits, bit_names, [], [prob, attn_out])
     while up_chain.moves:
@@ -1148,11 +1200,11 @@
             up_sum = lax.psum_scatter(up_sum, "seq", tiled=True)
             first = []
         elif call == 2:
+            passing = round_of(groups, bits, bit_names, [], passing)
+            first = [g for c in groups for g in c.gives]
+        else:
             down_sum, *passing = round_of(groups, bits, bit_names, [], [down_sum, *passing])
             down_sum = lax.all_gather(down_sum, "dp", tiled=True)
-            first = [g for c in groups for g in c.gives]
-        else:
-            memory_all, *passing = round_of(groups, bits, bit_names, [], [memory_all, *passing])
         *halves, d_rows, along, shift_part, bias_part = passing
         head_sums = [d_rows, along, shift_part]
         biases.append(bias_part)
@@ -1161,24 +1213,18 @@
             first += [halves[1]]
     output = by_stream(output_rows)
 
-    new_rows = memory_all.shape[1] // RATE
-    windows = memory_all[:, : new_rows * RATE].reshape(streams, new_rows, RATE, width)
-    new_compressed = (
-        jnp.einsum("srtd,tde->rse", windows, w_comp, preferred_element_type=F32) + comp_bias
-    ).astype(BF16)
-    grad_w_comp = jnp.einsum("srtd,rse->tde", windows, grad_comp, preferred_element_type=F32)
+    def compress(memory_all):
+        new_rows = memory_all.shape[1] // RATE
+        windows = memory_all[:, : new_rows * RATE].reshape(streams, new_rows, RATE, width)
+        made = jnp.einsum("srtd,tde->rse", windows, w_comp, preferred_element_type=F32)
+        grad = jnp.einsum("srtd,rse->tde", windows, grad_comp, preferred_element_type=F32)
+        grad = grad.astype(BF16).reshape(1, -1, grad.shape[2])
+        moves = moves_of([core_cut] + wide_cuts, [core_cut] + wide_cuts)
+        return (made + comp_bias).astype(BF16), Chain(moves, *first_halves(grad, moves[0]))
+
     grad_comp_bias = jnp.sum(grad_comp.astype(F32), (0, 1))
-    comp_moves = moves_of([core_cut] + wide_cuts, [core_cut] + wide_cuts)
-    comp_shape = grad_w_comp.shape
-    comp = Chain(
-        comp_moves, *first_halves(grad_w_comp.astype(BF16).reshape(1, -1, comp_shape[2]), comp_moves[0])
-    )
-
-    d_normed = d_rows
-    _, norm_one_back = jax.vjp(lambda v: layer_norm(v, gain_first, shift_first), x_f)
-    (d_context,) = norm_one_back(d_normed)
-    grad_inputs = (d_hidden + d_context).astype(BF16).reshape(seq_parts, seg_dev, width)
-    input_parts = parts_for(grad_inputs)
+    targets = jnp.stack([(me + shift) % seq_parts for shift in range(seq_parts)]).astype(jnp.int32)
+    input_parts = input_grad(targets, d_rows, x_rows, d_hidden, gain_first, seq_parts)
     input_rows = send(input_parts)
 
     grad_shift_first = jnp.sum(shift_part, 1)
@@ -1210,31 +1256,33 @@
     pinned = {
         1: input_parts,
         2: [input_rows[1]],
-        3: [new_compressed],
         5: [*input_rows[2:-1]],
         6: [input_rows[-1]],
     }
-    while len(two.moves) > 1 or vector.moves or comp.moves:
+    comp = None
+    while len(two.moves) > 1 or vector.moves:
         active = [one, two] + [comp] * (turn > 0) + [vector] * (turn > 2)
         active = [c for c in active if len(c.moves) > (c in groups)]
         fence = pinned.get(turn, [])
         if turn == 7:
             grad_inputs = by_stream(place_rows(input_rows, owners))
             fence = [grad_inputs]
-        if not results and len(one.moves) == 1:
+        if turn == 8:
             results = finished(0, one, results)
-            fence = [*fence, *results]
-        through = [up_sum] if turn == 0 else []
+            grad_w_comp = widen(comp.gives[0][0]).reshape(w_comp.shape)
+            fence = [*fence, *results, grad_w_comp]
+        through = [up_sum, memory_all] if turn == 0 else []
         through = round_of(active, bits, bit_names, fence, through)
         if turn == 0:
             up_sum = lax.all_gather(through[0], "dp", tiled=True)
-            grad_w_down, grad_w_up = down_sum.astype(F32), up_sum.astype(F32).T
+            new_compressed, comp = compress(through[1])
+            pinned[3] = [new_compressed, output]
+            grad_w_down, grad_w_up = widen(down_sum), widen(up_sum, True)
             pinned[4] = [grad_w_down]
             pinned[5] = [*pinned[5], grad_w_up]
         turn += 1
     vectors = vector.gives[0].reshape(-1)
 
-    grad_w_comp = comp.gives[0].astype(F32).reshape(comp_shape)
     results = finished(1, two, results)
     grad_w_query, grad_w_rel, grad_w_key, grad_w_value, grad_w_out = results
 

time: 669 us -> 657 us (0.982)
  other arithmetic: 51.3 us -> 37.1 us
  Pallas kernels: 195 us -> 204 us
  starting transfers between devices: 78.5 us -> 71.2 us
  matrix products: 72.3 us -> 79 us
    ppermute x57, waiting for transfers between devices: 114 us -> 99.3 us  [swap(): return lax.ppermute(rows, axis, [(i, i ^ distance) for i in range(count)])]
    ppermute x12, waiting for transfers between devices: 7.17 us -> 20.3 us  [send(): lax.ppermute(part, 'seq', [(i, (i + shift) % seq_parts) for i in range(se...]
    pallas_call x0 -> x4, Pallas kernels: none -> 10.6 us  [the longest x3 7.23 us: widen(): pl.pallas_call(widen_flip_kernel if flip else widen_kernel, grid=(4,), in...]
    ppermute x12, starting transfers between devices: 27.8 us -> 18.3 us  [send(): lax.ppermute(part, 'seq', [(i, (i + shift) % seq_parts) for i in range(se...]
    dot_general x5, matrix products: 37.2 us -> 45.7 us  [contract(): lax.dot_general(left, right, (((left_dim,), (right_dim,)), ((), ())), pre...]
    convert_element_type x4 -> x1, other arithmetic: 8.82 us -> 0.45 us  [compress(): (made + comp_bias).astype(BF16)]
    unnamed x295 -> x298, local copies, waits for them, and re-layouts: 81.2 us -> 79.8 us
  transfers between devices with their start and end apart: 76 -> 76, of which waited for: 22 -> 21; matrix products, arithmetic and copies ran while one was open for 24% -> 23% of each run, Pallas kernels for 28% -> 30%
where the time goes in v3:
time: 657 us; the launch traced here: 646 us
  Pallas kernels  204 us (31%)
  waiting for transfers between devices  120 us (18%)
  local copies, waits for them, and re-layouts  117 us (18%)
  matrix products  79 us (12%)
  starting transfers between devices  71.2 us (11%)
  other arithmetic  37.1 us (6%)
  between operations  17.5 us (3%)
    ppermute x57, waiting for transfers between devices, swap(): return lax.ppermute(rows, axis, [(i, i ^ distance) for i in range(count)])  99.3 us
    pallas_call x4, Pallas kernels, attend_back(): pl.pallas_call(functools.partial(attend_back_kernel, bool(sums)), grid=(c...  86.6 us
    unnamed x298, local copies, waits for them, and re-layouts  79.8 us
    ppermute x57, starting transfers between devices, swap(): return lax.ppermute(rows, axis, [(i, i ^ distance) for i in range(count)])  52.4 us
    dot_general x5, matrix products, contract(): lax.dot_general(left, right, (((left_dim,), (right_dim,)), ((), ())), pre...  45.7 us
    pallas_call x2, Pallas kernels, attend(): pl.pallas_call(attend_kernel, grid=(count, seg // block), in_specs=[pl.Bl...  41.7 us
    pallas_call x18, Pallas kernels, round_of(): pl.pallas_call(kernel, in_specs=[pl.BlockSpec(memory_space=pltpu.SMEM)] +...  35.2 us
    ppermute x12, waiting for transfers between devices, send(): lax.ppermute(part, 'seq', [(i, (i + shift) % seq_parts) for i in range(se...  20.3 us
  transfers between devices with their start and end apart: 76, of which 21 were waited for; matrix products, arithmetic and copies ran while one was open for 23% of the time, Pallas kernels for 30%

profile of v3, /device:TPU:0, one launch (start us, length us, event | category | flops | bytes accessed | tf_op | source)
XLA Modules:
  0.0 645.9 jit_solution(3533670906311194062)
XLA Ops:
  8.5 4.1 collective-permute-start.3
  24.2 32.9 %collective-permute-done.3 = bf16[2,128,512]{2,1,0:T(8,128)(2,1)S(1)} collective-permute-done((bf16[2,128,512]{2,1,0:T(8,128)(2,1)S(1)}, bf16[2,128,512]{2,1,0:T(8,128)(2,1)S(1)}, u32[]{:S(2)}, u32[]{:S(2)}) %collective-permute-start.3) | collective-permute-done | bytes 262176 | tf_op jit(solution)/shard_map/ppermute | solution.py:360
  58.6 13.9 %multiply_sine_fusion = (f32[1536,512]{1,0:T(8,128)}, bf16[1536,512]{1,0:T(8,128)(2,1)}, bf16[1536,512]{1,0:T(8,128)(2,1)}, f32[1536,512]{1,0:T(8,128)}) fusion(f32[512]{0:T(512)S(1)} %multiply_exponential_fusion, f32[1536]{0:T(1024)S(1)} %iota_convert_fusion), kind=kLoop, calls=%fused_computation.11 | loop fusion | flops 2359296 | bytes 9445376 | tf_op jit(solution)/shard_map/sin | solution.py:33
  72.5 4.9 constant_dynamic-slice_fusion.4
  94.0 4.1 pad_maximum_fusion.1.refs_9_.table_ref
  101.2 5.7 norm_context.1
  111.0 3.7 convolution_convert_fusion.1.refs_2_.v_ref
  120.0 3.5 collective-permute-done.10
  130.0 7.8 %convolution_convert_fusion.k_ref = bf16[1536,1024]{1,0:T(8,128)(2,1)} fusion(bf16[1536,1024]{1,0:T(8,128)(2,1)} %bitcast.327, bf16[1024,1024]{1,0:T(8,128)(2,1)} %wk_ref.7), kind=kOutput, calls=%fused_computation.17 | convolution fusion | flops 3222798336 | bytes 8388608 | tf_op jit(solution)/shard_map/dot_general | solution.py:1114
  141.7 20.8 %attend.2 = (bf16[8,512,1536]{2,1,0:T(8,128)(2,1)}, bf16[512,1024]{1,0:T(8,128)(2,1)}) custom-call(s32[1]{0:T(128)} %dynamic_slice.78.len_ref, bf16[512,1024]{1,0:T(8,128)(2,1)} %get-tuple-element.315.qc_ref, bf16[512,1024]{1,0:T(8,128)(2,1)} %get-tuple-element.314.qp_ref, bf16[1536,1024]{1,0:T(8,128)(2,1)} %convolution_convert_fusion.k_ref, ...), custom_call_target="tpu_custom_call" | custom-call | flops 1024 | bytes 1024 | tf_op jit(solution)/shard_map/attend/pallas_call | solution.py:451
  164.7 5.3 add_and_split.23
  175.5 3.4 collective-permute-done.15
  180.1 20.9 %attend.3 = (bf16[8,512,1536]{2,1,0:T(8,128)(2,1)}, bf16[512,1024]{1,0:T(8,128)(2,1)S(1)}) custom-call(s32[1]{0:T(128)} %dynamic_slice.78.len_ref, bf16[512,1024]{1,0:T(8,128)(2,1)} %get-tuple-element.315.qc_ref, bf16[512,1024]{1,0:T(8,128)(2,1)} %get-tuple-element.314.qp_ref, ...), custom_call_target="tpu_custom_call", output_to_operand_aliasing={{0}: (9, {}), {1}: (10, {})} | custom-call | flops 1024 | bytes 1024 | tf_op jit(solution)/shard_map/attend/pallas_call | solution.py:451
  204.5 4.2 add_and_split.24
  219.3 2.7 copy-done.134
  222.1 17.8 %multiply_convert_fusion = (bf16[1024,2048]{1,0:T(8,128)(2,1)}, f32[1024,2048]{1,0:T(8,128)}) fusion(f32[2048]{0:T(1024)S(1)} %bitcast.478, bf16[1024,1024]{1,0:T(8,128)(2,1)S(1)} %bitcast.463, bf16[2048,1024]{1,0:T(8,128)(2,1)S(1)} %bitcast.488), kind=kOutput, calls=%fused_computation.10 | convolution fusion | flops 4315938816 | bytes 18882560 | tf_op jit(solution)/shard_map/dot_general | solution.py:349
  242.8 2.9 collective-permute-done.25
  250.0 6.2 convolution_convert_fusion.3
  256.3 13.3 %convert_reduce_fusion = (f32[2048]{0:T(1024)S(1)}, bf16[1024,2048]{1,0:T(8,128)(2,1)S(1)}) fusion(f32[1024,2048]{1,0:T(8,128)} %get-tuple-element.343, f32[2048]{0:T(1024)S(1)} %bitcast.479, bf16[1024,1024]{1,0:T(8,128)(2,1)} %bitcast.466, bf16[2048,1024]{1,0:T(8,128)(2,1)} %bitcast.489), kind=kOutput, calls=%fused_computation.9 | convolution fusion | flops 4343199744 | bytes 18890752 | tf_op jit(solution)/shard_map/dot_general | solution.py:349
  271.6 6.2 convolution_convert_fusion.2
  277.9 8.0 %fusion.41 = f32[2,512,1024]{2,1,0:T(8,128)S(1)} fusion(bf16[2,512,2048]{2,1,0:T(8,128)(2,1)} %bitcast.491, bf16[2048,1024,1]{1,0,2:T(8,128)(2,1)} %bitcast.487), kind=kOutput, calls=%fused_computation.130 | convolution fusion | flops 4294967296 | bytes 12582912 | tf_op jit(solution)/shard_map/dot_general | solution.py:1161
  287.4 4.5 fusion.40
  294.7 3.2 multiply_reduce_fusion
  298.0 3.9 fusion.37
  310.9 2.8 out_grad.1
  315.4 21.4 %attend_back.4 = (bf16[6,512,512]{2,1,0:T(8,128)(2,1)}, bf16[6,512,512]{2,1,0:T(8,128)(2,1)}, f32[512,1024]{1,0:T(8,128)}, f32[1024,128]{1,0:T(8,128)S(1)}, f32[...) custom-call(s32[5]{0:T(128)S(1)} %stack.92.bits_ref.refs_0_, ...), custom_call_target="tpu_custom_call", output_to_operand_aliasing={{0}: (15, {}), {1}: (16, {})} | custom-call | flops 1024 | bytes 1024 | tf_op jit(solution)/shard_map/attend_back/pallas_call | solution.py:621
  341.2 21.9 %attend_back.5 = (bf16[6,512,512]{2,1,0:T(8,128)(2,1)}, bf16[6,512,512]{2,1,0:T(8,128)(2,1)}, f32[512,1024]{1,0:T(8,128)}, f32[1024,128]{1,0:T(8,128)S(1)}, f32[...) custom-call(s32[5]{0:T(128)S(1)} %stack.92.bits_ref.refs_0_, ...), custom_call_target="tpu_custom_call", output_to_operand_aliasing={{2}: (15, {}), {3}: (16, {}), {4}: (17, {}), {0}: (18, {}),... | custom-call | flops 1024 | bytes 1024 | tf_op jit(solution)/shard_map/attend_back/pallas_call | solution.py:621
  369.0 21.7 %attend_back.6 = (bf16[4,512,512]{2,1,0:T(8,128)(2,1)}, bf16[4,512,512]{2,1,0:T(8,128)(2,1)}, f32[512,1024]{1,0:T(8,128)}, f32[1024,128]{1,0:T(8,128)S(1)}, f32[...) custom-call(s32[5]{0:T(128)S(1)} %stack.92.bits_ref.refs_0_, ...), custom_call_target="tpu_custom_call", output_to_operand_aliasing={{2}: (15, {}), {3}: (16, {}), {4}: (17, {})} | custom-call | flops 1024 | bytes 1024 | tf_op jit(solution)/shard_map/attend_back/pallas_call | solution.py:621
  394.4 4.7 add_and_split.25
  406.6 21.6 %attend_back.7 = (bf16[4,512,512]{2,1,0:T(8,128)(2,1)}, bf16[4,512,512]{2,1,0:T(8,128)(2,1)}, f32[512,1024]{1,0:T(8,128)}, f32[1024,128]{1,0:T(8,128)S(1)}, f32[...) custom-call(s32[5]{0:T(128)S(1)} %stack.92.bits_ref.refs_0_, ...), custom_call_target="tpu_custom_call", output_to_operand_aliasing={{2}: (15, {}), {3}: (16, {}), {4}: (17, {}), {0}: (18, {}),... | custom-call | flops 1024 | bytes 1024 | tf_op jit(solution)/shard_map/attend_back/pallas_call | solution.py:621
  442.1 12.1 %collective-permute-done.33 = bf16[3,128,512]{2,1,0:T(8,128)(2,1)S(1)} collective-permute-done((bf16[3,128,512]{2,1,0:T(8,128)(2,1)}, bf16[3,128,512]{2,1,0:T(8,128)(2,1)S(1)}, u32[]{:S(2)}, u32[]{:S(2)}) %collective-permute-start.33) | collective-permute-done | bytes 393248 | tf_op jit(solution)/shard_map/ppermute | solution.py:360
  459.6 3.6 add_and_split.27
  467.4 3.0 copy.197
  470.4 5.5 copy.149
  475.9 3.0 bitcast_convert_fusion
  481.7 3.4 input_grad.1
  487.5 15.3 %collective-permute-done.36 = bf16[6,64,512]{2,1,0:T(8,128)(2,1)S(1)} collective-permute-done((bf16[6,64,512]{2,1,0:T(8,128)(2,1)}, bf16[6,64,512]{2,1,0:T(8,128)(2,1)S(1)}, u32[]{:S(2)}, u32[]{:S(2)}) %collective-permute-start.36) | collective-permute-done | bytes 393248 | tf_op jit(solution)/shard_map/ppermute | solution.py:360
  513.8 7.6 %collective-permute-done.40.refs_1_ = bf16[6,32,512]{2,1,0:T(8,128)(2,1)S(1)} collective-permute-done((bf16[6,32,512]{2,1,0:T(8,128)(2,1)S(1)}, bf16[6,32,512]{2,1,0:T(8,128)(2,1)S(1)}, u32[]{:S(2)}, u32[]{:S(2)}) %collective-permute-start.40) | collective-permute-done | bytes 196640 | tf_op jit(solution)/shard_map/ppermute | solution.py:360
  531.2 6.1 collective-permute-done.44
  539.8 3.4 collective-permute-start.49
  554.3 2.6 collective-permute-start.31
  557.2 13.4 %collective-permute-done.31.refs_2_.refs_10_ = bf16[128,1024]{1,0:T(8,128)(2,1)S(1)} collective-permute-done((bf16[128,1024]{1,0:T(8,128)(2,1)S(1)}, bf16[128,1024]{1,0:T(8,128)(2,1)S(1)}, u32[]{:S(2)}, u32[]{:S(2)}) %collective-permute-start.31) | collective-permute-done | bytes 262176 | tf_op jit(solution)/shard_map/ppermute | solution.py:1087
  573.3 2.7 widen.4.refs_11_
  586.8 6.9 %collective-permute-done.32.refs_3_.refs_10_ = bf16[128,1024]{1,0:T(8,128)(2,1)S(1)} collective-permute-done((bf16[128,1024]{1,0:T(8,128)(2,1)S(1)}, bf16[128,1024]{1,0:T(8,128)(2,1)S(1)}, u32[]{:S(2)}, u32[]{:S(2)}) %collective-permute-start.32) | collective-permute-done | bytes 262176 | tf_op jit(solution)/shard_map/ppermute | solution.py:1087
  593.7 6.3 collective-permute-done.61.refs_9_
  600.0 3.1 add_and_split.33
  618.2 7.0 %finish.2 = (f32[1024,1024]{1,0:T(8,128)}, f32[1024,1024]{1,0:T(8,128)}, f32[1024,1024]{1,0:T(8,128)}, f32[1024,1024]{1,0:T(8,128)}, f32[1024,1024]{1,0:T(8,128)}) custom-call(s32[5]{0:T(128)S(1)} %stack.92.bits_ref.refs_0_, bf16[6,512,512]{2,1,0:T(8,128)(2,1)S(1)} %bitcast.349, bf16[6,512,512]{2,1,0:T(8,128)(2,1)} %collective-permute-done.67.got_ref), custom_call_target="tpu_custom_call" | custom-call | flops 1024 | bytes 1024 | tf_op jit(solution)/shard_map/finish/pallas_call | solution.py:799
  633.3 5.3 finish.3
  (527 shorter events, 220.2 us)
Async XLA Ops:
  7.2 232.7 %all-gather.4.cloned.1.call-start = ((), (), s32[]{:S(2)}) async-start(), calls=%async_computation.4 | async-start | bytes 5242880 | tf_op jit(solution)/shard_map/all_gather | solution.py:1122
  8.5 48.6 %collective-permute-start.3 = (bf16[2,128,512]{2,1,0:T(8,128)(2,1)S(1)}, bf16[2,128,512]{2,1,0:T(8,128)(2,1)S(1)}, u32[]{:S(2)}, u32[]{:S(2)}) collective-permute-start(bf16[2,128,512]{2,1,0:T(8,128)(2,1)S(1)} %bitcast.373), channel_id=1, source_target_pairs={{0,2},{1,3},{2,0},{3,1},{4,6},{5,7},{6,4},{7,5},{8,10},{9,11},{10,... | collective-permute-start | bytes 786440 | tf_op jit(solution)/shard_map/ppermute | solution.py:360
  20.2 79.5 %collective-permute-start = (bf16[384,1024]{1,0:T(8,128)(2,1)}, bf16[384,1024]{1,0:T(8,128)(2,1)}, u32[]{:S(2)}, u32[]{:S(2)}) collective-permute-start(bf16[384,1024]{1,0:T(8,128)(2,1)} %get-tuple-element.307), channel_id=1, source_target_pairs={{0,1},{1,2},{2,3},{3,0},{4,5},{5,6},{6,7},{7,4},{8,9},{9,10},{10,1... | collective-permute-start | bytes 2359304 | tf_op jit(solution)/shard_map/ppermute | solution.py:1087
  21.7 79.4 %collective-permute-start.1 = (bf16[384,1024]{1,0:T(8,128)(2,1)}, bf16[384,1024]{1,0:T(8,128)(2,1)}, u32[]{:S(2)}, u32[]{:S(2)}) collective-permute-start(bf16[384,1024]{1,0:T(8,128)(2,1)} %get-tuple-element.306), channel_id=1, source_target_pairs={{0,2},{1,3},{2,0},{3,1},{4,6},{5,7},{6,4},{7,5},{8,10},{9,11},{10,... | collective-permute-start | bytes 2359304 | tf_op jit(solution)/shard_map/ppermute | solution.py:1087
  22.1 79.1 %collective-permute-start.2 = (bf16[384,1024]{1,0:T(8,128)(2,1)}, bf16[384,1024]{1,0:T(8,128)(2,1)}, u32[]{:S(2)}, u32[]{:S(2)}) collective-permute-start(bf16[384,1024]{1,0:T(8,128)(2,1)} %get-tuple-element.305), channel_id=1, source_target_pairs={{0,3},{1,0},{2,1},{3,2},{4,7},{5,4},{6,5},{7,6},{8,11},{9,8},{10,9... | collective-permute-start | bytes 2359304 | tf_op jit(solution)/shard_map/ppermute | solution.py:1087
  58.6 27.9 %collective-permute-start.4 = (bf16[2,256,512]{2,1,0:T(8,128)(2,1)}, bf16[2,256,512]{2,1,0:T(8,128)(2,1)}, u32[]{:S(2)}, u32[]{:S(2)}) collective-permute-start(bf16[2,256,512]{2,1,0:T(8,128)(2,1)} %bitcast.24), channel_id=1, source_target_pairs={{0,1},{1,0},{2,3},{3,2},{4,5},{5,4},{6,7},{7,6},{8,9},{9,8},{10,11... | collective-permute-start | bytes 1572872 | tf_op jit(solution)/shard_map/ppermute | solution.py:360
  98.1 16.5 %collective-permute-start.5 = (bf16[1,512,512]{2,1,0:T(8,128)(2,1)S(1)}, bf16[1,512,512]{2,1,0:T(8,128)(2,1)S(1)}, u32[]{:S(2)}, u32[]{:S(2)}) collective-permute-start(bf16[1,512,512]{2,1,0:T(8,128)(2,1)S(1)} %bitcast.360), channel_id=1, source_target_pairs={{0,8},{4,12},{8,0},{12,4},{16,24},{20,28},{24,16},{28,20},{1,9},{5... | collective-permute-start | bytes 1572872 | tf_op jit(solution)/shard_map/ppermute | solution.py:360
  99.6 15.0 %collective-permute-start.6 = (bf16[1,512,512]{2,1,0:T(8,128)(2,1)S(1)}, bf16[1,512,512]{2,1,0:T(8,128)(2,1)S(1)}, u32[]{:S(2)}, u32[]{:S(2)}) collective-permute-start(bf16[1,512,512]{2,1,0:T(8,128)(2,1)S(1)} %bitcast.363), channel_id=1, source_target_pairs={{0,16},{4,20},{8,24},{12,28},{16,0},{20,4},{24,8},{28,12},{1,17},{... | collective-permute-start | bytes 1572872 | tf_op jit(solution)/shard_map/ppermute | solution.py:360
  117.0 45.5 %collective-permute-start.7 = (bf16[1,1024,512]{2,1,0:T(8,128)(2,1)}, bf16[1,1024,512]{2,1,0:T(8,128)(2,1)}, u32[]{:S(2)}, u32[]{:S(2)}) collective-permute-start(bf16[1,1024,512]{2,1,0:T(8,128)(2,1)} %bitcast.41), channel_id=1, source_target_pairs={{0,16},{4,20},{8,24},{12,28},{16,0},{20,4},{24,8},{28,12},{1,17},{... | collective-permute-start | bytes 3145736 | tf_op jit(solution)/shard_map/ppermute | solution.py:360
  118.5 43.9 %collective-permute-start.8 = (bf16[1,1024,512]{2,1,0:T(8,128)(2,1)}, bf16[1,1024,512]{2,1,0:T(8,128)(2,1)}, u32[]{:S(2)}, u32[]{:S(2)}) collective-permute-start(bf16[1,1024,512]{2,1,0:T(8,128)(2,1)} %bitcast.43), channel_id=1, source_target_pairs={{0,8},{4,12},{8,0},{12,4},{16,24},{20,28},{24,16},{28,20},{1,9},{5... | collective-permute-start | bytes 3145736 | tf_op jit(solution)/shard_map/ppermute | solution.py:360
  124.2 38.2 %collective-permute-start.11 = (bf16[1,512,512]{2,1,0:T(8,128)(2,1)S(1)}, bf16[1,512,512]{2,1,0:T(8,128)(2,1)}, u32[]{:S(2)}, u32[]{:S(2)}) collective-permute-start(bf16[1,512,512]{2,1,0:T(8,128)(2,1)S(1)} %bitcast.338), channel_id=1, source_target_pairs={{0,8},{4,12},{8,0},{12,4},{16,24},{20,28},{24,16},{28,20},{1,9},{5... | collective-permute-start | bytes 1572872 | tf_op jit(solution)/shard_map/ppermute | solution.py:360
  128.1 34.3 %collective-permute-start.12 = (bf16[1,512,512]{2,1,0:T(8,128)(2,1)S(1)}, bf16[1,512,512]{2,1,0:T(8,128)(2,1)}, u32[]{:S(2)}, u32[]{:S(2)}) collective-permute-start(bf16[1,512,512]{2,1,0:T(8,128)(2,1)S(1)} %bitcast.355), channel_id=1, source_target_pairs={{0,16},{4,20},{8,24},{12,28},{16,0},{20,4},{24,8},{28,12},{1,17},{... | collective-permute-start | bytes 1572872 | tf_op jit(solution)/shard_map/ppermute | solution.py:360
  129.7 208.8 %reduce-scatter.5.cloned.1.call-start = ((), (), s32[]{:S(2)}) async-start(), calls=%async_computation.5 | async-start | bytes 5242880 | tf_op jit(solution)/shard_map/reduce_scatter | solution.py:1155
  171.0 31.1 %collective-permute-start.13 = (bf16[1,1024,512]{2,1,0:T(8,128)(2,1)S(1)}, bf16[1,1024,512]{2,1,0:T(8,128)(2,1)}, u32[]{:S(2)}, u32[]{:S(2)}) collective-permute-start(bf16[1,1024,512]{2,1,0:T(8,128)(2,1)S(1)} %bitcast.346), channel_id=1, source_target_pairs={{0,16},{4,20},{8,24},{12,28},{16,0},{20,4},{24,8},{28,12},{1,17},{... | collective-permute-start | bytes 3145736 | tf_op jit(solution)/shard_map/ppermute | solution.py:360
  171.6 30.4 %collective-permute-start.14 = (bf16[1,1024,512]{2,1,0:T(8,128)(2,1)}, bf16[1,1024,512]{2,1,0:T(8,128)(2,1)}, u32[]{:S(2)}, u32[]{:S(2)}) collective-permute-start(bf16[1,1024,512]{2,1,0:T(8,128)(2,1)} %bitcast.59.rest_3_), channel_id=1, source_target_pairs={{0,8},{4,12},{8,0},{12,4},{16,24},{20,28},{24,16},{28,20},{1,9},{5... | collective-permute-start | bytes 3145736 | tf_op jit(solution)/shard_map/ppermute | solution.py:360
  212.1 27.8 %collective-permute-start.22 = (bf16[128,1024]{1,0:T(8,128)(2,1)S(1)}, bf16[128,1024]{1,0:T(8,128)(2,1)S(1)}, u32[]{:S(2)}, u32[]{:S(2)}) collective-permute-start(bf16[128,1024]{1,0:T(8,128)(2,1)S(1)} %bitcast.372), channel_id=1, source_target_pairs={{0,1},{1,2},{2,3},{3,0},{4,5},{5,6},{6,7},{7,4},{8,9},{9,10},{10,1... | collective-permute-start | bytes 786440 | tf_op jit(solution)/shard_map/ppermute | solution.py:1087
  213.9 26.0 %collective-permute-start.23 = (bf16[128,1024]{1,0:T(8,128)(2,1)S(1)}, bf16[128,1024]{1,0:T(8,128)(2,1)}, u32[]{:S(2)}, u32[]{:S(2)}) collective-permute-start(bf16[128,1024]{1,0:T(8,128)(2,1)S(1)} %bitcast.370), channel_id=1, source_target_pairs={{0,2},{1,3},{2,0},{3,1},{4,6},{5,7},{6,4},{7,5},{8,10},{9,11},{10,... | collective-permute-start | bytes 786440 | tf_op jit(solution)/shard_map/ppermute | solution.py:1087
  215.1 24.8 %collective-permute-start.24 = (bf16[128,1024]{1,0:T(8,128)(2,1)S(1)}, bf16[128,1024]{1,0:T(8,128)(2,1)}, u32[]{:S(2)}, u32[]{:S(2)}) collective-permute-start(bf16[128,1024]{1,0:T(8,128)(2,1)S(1)} %bitcast.368), channel_id=1, source_target_pairs={{0,3},{1,0},{2,1},{3,2},{4,7},{5,4},{6,5},{7,6},{8,11},{9,8},{10,9... | collective-permute-start | bytes 786440 | tf_op jit(solution)/shard_map/ppermute | solution.py:1087
  256.3 110.4 %reduce-scatter.7.cloned.1.call-start = ((), (), s32[]{:S(2)}) async-start(), calls=%async_computation.6 | async-start | bytes 5242880 | tf_op jit(solution)/shard_map/reduce_scatter | solution.py:1155
  277.8 151.9 %reduce-scatter.9.cloned.1.call-start = ((), (), s32[]{:S(2)}) async-start(), calls=%async_computation.7 | async-start | bytes 1310720 | tf_op jit(solution)/shard_map/reduce_scatter | solution.py:1195
  302.6 61.0 %collective-permute-start.19 = (bf16[128,1024]{1,0:T(8,128)(2,1)S(1)}, bf16[128,1024]{1,0:T(8,128)(2,1)S(1)}, u32[]{:S(2)}, u32[]{:S(2)}) collective-permute-start(bf16[128,1024]{1,0:T(8,128)(2,1)S(1)} %get-tuple-element.320.rest_5_), channel_id=1, source_target_pairs={{0,1},{1,2},{2,3},{3,0},{4,5},{5,6},{6,7},{7,4},{8,9},{9,10},{10,1... | collective-permute-start | bytes 786440 | tf_op jit(solution)/shard_map/ppermute | solution.py:1087
  303.2 60.4 %collective-permute-start.20 = (bf16[128,1024]{1,0:T(8,128)(2,1)S(1)}, bf16[128,1024]{1,0:T(8,128)(2,1)}, u32[]{:S(2)}, u32[]{:S(2)}) collective-permute-start(bf16[128,1024]{1,0:T(8,128)(2,1)S(1)} %get-tuple-element.319.rest_6_), channel_id=1, source_target_pairs={{0,2},{1,3},{2,0},{3,1},{4,6},{5,7},{6,4},{7,5},{8,10},{9,11},{10,... | collective-permute-start | bytes 786440 | tf_op jit(solution)/shard_map/ppermute | solution.py:1087
  305.5 58.2 %collective-permute-start.21 = (bf16[128,1024]{1,0:T(8,128)(2,1)S(1)}, bf16[128,1024]{1,0:T(8,128)(2,1)}, u32[]{:S(2)}, u32[]{:S(2)}) collective-permute-start(bf16[128,1024]{1,0:T(8,128)(2,1)S(1)} %get-tuple-element.318.rest_7_), channel_id=1, source_target_pairs={{0,3},{1,0},{2,1},{3,2},{4,7},{5,4},{6,5},{7,6},{8,11},{9,8},{10,9... | collective-permute-start | bytes 786440 | tf_op jit(solution)/shard_map/ppermute | solution.py:1087
  339.0 103.1 %reduce-scatter.11.cloned.1.call-start = ((), (), s32[]{:S(2)}) async-start(), calls=%async_computation.8 | async-start | bytes 1310720 | tf_op jit(solution)/shard_map/reduce_scatter | solution.py:1200
  366.7 25.6 %collective-permute-start.27 = (bf16[6,512,512]{2,1,0:T(8,128)(2,1)}, bf16[6,512,512]{2,1,0:T(8,128)(2,1)}, u32[]{:S(2)}, u32[]{:S(2)}) collective-permute-start(bf16[6,512,512]{2,1,0:T(8,128)(2,1)} %get-tuple-element.196.rest_3_), channel_id=1, source_target_pairs={{0,4},{4,0},{8,12},{12,8},{16,20},{20,16},{24,28},{28,24},{1,5},{5... | collective-permute-start | bytes 9437192 | tf_op jit(solution)/shard_map/ppermute | solution.py:360
  366.8 178.0 %all-gather.6.cloned.1.call-start = ((), (), s32[]{:S(2)}) async-start(), calls=%async_computation.9 | async-start | bytes 2359296 | tf_op jit(solution)/shard_map/all_gather | solution.py:1207
  401.5 28.2 %collective-permute-start.28 = (bf16[3,256,512]{2,1,0:T(8,128)(2,1)}, bf16[3,256,512]{2,1,0:T(8,128)(2,1)}, u32[]{:S(2)}, u32[]{:S(2)}) collective-permute-start(bf16[3,256,512]{2,1,0:T(8,128)(2,1)} %bitcast.96.rest_5_), channel_id=1, source_target_pairs={{0,16},{4,20},{8,24},{12,28},{16,0},{20,4},{24,8},{28,12},{1,17},{... | collective-permute-start | bytes 2359304 | tf_op jit(solution)/shard_map/ppermute | solution.py:360
  403.0 26.8 %collective-permute-start.29 = (bf16[3,256,512]{2,1,0:T(8,128)(2,1)}, bf16[3,256,512]{2,1,0:T(8,128)(2,1)}, u32[]{:S(2)}, u32[]{:S(2)}) collective-permute-start(bf16[3,256,512]{2,1,0:T(8,128)(2,1)} %bitcast.98.rest_6_), channel_id=1, source_target_pairs={{0,8},{4,12},{8,0},{12,4},{16,24},{20,28},{24,16},{28,20},{1,9},{5... | collective-permute-start | bytes 2359304 | tf_op jit(solution)/shard_map/ppermute | solution.py:360
  439.5 132.2 %all-gather.8.cloned.1.call-start = ((), (), s32[]{:S(2)}) async-start(), calls=%async_computation.10 | async-start | bytes 2359296 | tf_op jit(solution)/shard_map/all_gather | solution.py:1277
  439.5 16.1 %collective-permute-start.35 = (bf16[4,512,512]{2,1,0:T(8,128)(2,1)}, bf16[4,512,512]{2,1,0:T(8,128)(2,1)}, u32[]{:S(2)}, u32[]{:S(2)}) collective-permute-start(bf16[4,512,512]{2,1,0:T(8,128)(2,1)} %get-tuple-element.232), channel_id=1, source_target_pairs={{0,4},{4,0},{8,12},{12,8},{16,20},{20,16},{24,28},{28,24},{1,5},{5... | collective-permute-start | bytes 6291464 | tf_op jit(solution)/shard_map/ppermute | solution.py:360
  439.6 14.5 %collective-permute-start.33 = (bf16[3,128,512]{2,1,0:T(8,128)(2,1)}, bf16[3,128,512]{2,1,0:T(8,128)(2,1)S(1)}, u32[]{:S(2)}, u32[]{:S(2)}) collective-permute-start(bf16[3,128,512]{2,1,0:T(8,128)(2,1)} %bitcast.445), channel_id=1, source_target_pairs={{0,8},{4,12},{8,0},{12,4},{16,24},{20,28},{24,16},{28,20},{1,9},{5... | collective-permute-start | bytes 1179656 | tf_op jit(solution)/shard_map/ppermute | solution.py:360
  440.2 14.7 %collective-permute-start.34 = (bf16[3,128,512]{2,1,0:T(8,128)(2,1)S(1)}, bf16[3,128,512]{2,1,0:T(8,128)(2,1)S(1)}, u32[]{:S(2)}, u32[]{:S(2)}) collective-permute-start(bf16[3,128,512]{2,1,0:T(8,128)(2,1)S(1)} %bitcast.443), channel_id=1, source_target_pairs={{0,16},{4,20},{8,24},{12,28},{16,0},{20,4},{24,8},{28,12},{1,17},{... | collective-permute-start | bytes 1179656 | tf_op jit(solution)/shard_map/ppermute | solution.py:360
  480.3 22.5 %collective-permute-start.39 = (bf16[1,1536,256]{2,1,0:T(8,128)(2,1)}, bf16[1,1536,256]{2,1,0:T(8,128)(2,1)}, u32[]{:S(2)}, u32[]{:S(2)}) collective-permute-start(bf16[1,1536,256]{2,1,0:T(8,128)(2,1)} %get-tuple-element.316), channel_id=1, source_target_pairs={{0,4},{4,0},{8,12},{12,8},{16,20},{20,16},{24,28},{28,24},{1,5},{5... | collective-permute-start | bytes 2359304 | tf_op jit(solution)/shard_map/ppermute | solution.py:360
  480.3 22.5 %collective-permute-start.37 = (bf16[2,256,512]{2,1,0:T(8,128)(2,1)}, bf16[2,256,512]{2,1,0:T(8,128)(2,1)}, u32[]{:S(2)}, u32[]{:S(2)}) collective-permute-start(bf16[2,256,512]{2,1,0:T(8,128)(2,1)} %bitcast.441), channel_id=1, source_target_pairs={{0,16},{4,20},{8,24},{12,28},{16,0},{20,4},{24,8},{28,12},{1,17},{... | collective-permute-start | bytes 1572872 | tf_op jit(solution)/shard_map/ppermute | solution.py:360
  480.9 21.9 %collective-permute-start.38 = (bf16[2,256,512]{2,1,0:T(8,128)(2,1)}, bf16[2,256,512]{2,1,0:T(8,128)(2,1)}, u32[]{:S(2)}, u32[]{:S(2)}) collective-permute-start(bf16[2,256,512]{2,1,0:T(8,128)(2,1)} %bitcast.119), channel_id=1, source_target_pairs={{0,8},{4,12},{8,0},{12,4},{16,24},{20,28},{24,16},{28,20},{1,9},{5... | collective-permute-start | bytes 1572872 | tf_op jit(solution)/shard_map/ppermute | solution.py:360
  485.5 28.1 %collective-permute-start.30 = (bf16[128,1024]{1,0:T(8,128)(2,1)}, bf16[128,1024]{1,0:T(8,128)(2,1)S(1)}, u32[]{:S(2)}, u32[]{:S(2)}) collective-permute-start(bf16[128,1024]{1,0:T(8,128)(2,1)} %get-tuple-element.224.refs_9_), channel_id=1, source_target_pairs={{0,1},{1,2},{2,3},{3,0},{4,5},{5,6},{6,7},{7,4},{8,9},{9,10},{10,1... | collective-permute-start | bytes 786440 | tf_op jit(solution)/shard_map/ppermute | solution.py:1087
  486.3 16.5 %collective-permute-start.36 = (bf16[6,64,512]{2,1,0:T(8,128)(2,1)}, bf16[6,64,512]{2,1,0:T(8,128)(2,1)S(1)}, u32[]{:S(2)}, u32[]{:S(2)}) collective-permute-start(bf16[6,64,512]{2,1,0:T(8,128)(2,1)} %bitcast.442), channel_id=1, source_target_pairs={{0,1},{1,0},{2,3},{3,2},{4,5},{5,4},{6,7},{7,6},{8,9},{9,8},{10,11... | collective-permute-start | bytes 1179656 | tf_op jit(solution)/shard_map/ppermute | solution.py:360
  508.1 15.5 %collective-permute-start.43 = (bf16[1,768,256]{2,1,0:T(8,128)(2,1)S(1)}, bf16[1,768,256]{2,1,0:T(8,128)(2,1)S(1)}, u32[]{:S(2)}, u32[]{:S(2)}) collective-permute-start(bf16[1,768,256]{2,1,0:T(8,128)(2,1)S(1)} %bitcast.444), channel_id=1, source_target_pairs={{0,16},{4,20},{8,24},{12,28},{16,0},{20,4},{24,8},{28,12},{1,17},{... | collective-permute-start | bytes 1179656 | tf_op jit(solution)/shard_map/ppermute | solution.py:360
  513.7 17.6 %collective-permute-start.47 = (f32[1,96,128]{2,1,0:T(8,128)S(1)}, f32[1,96,128]{2,1,0:T(8,128)S(1)}, u32[]{:S(2)}, u32[]{:S(2)}) collective-permute-start(f32[1,96,128]{2,1,0:T(8,128)S(1)} %bitcast.436), channel_id=1, source_target_pairs={{0,4},{4,0},{8,12},{12,8},{16,20},{20,16},{24,28},{28,24},{1,5},{5... | collective-permute-start | bytes 147464 | tf_op jit(solution)/shard_map/ppermute | solution.py:360
  551.2 24.8 %collective-permute-start.52 = (bf16[3,128,512]{2,1,0:T(8,128)(2,1)S(1)}, bf16[3,128,512]{2,1,0:T(8,128)(2,1)S(1)}, u32[]{:S(2)}, u32[]{:S(2)}) collective-permute-start(bf16[3,128,512]{2,1,0:T(8,128)(2,1)S(1)} %bitcast.392), channel_id=1, source_target_pairs={{0,8},{4,12},{8,0},{12,4},{16,24},{20,28},{24,16},{28,20},{1,9},{5... | collective-permute-start | bytes 1179656 | tf_op jit(solution)/shard_map/ppermute | solution.py:360
  552.3 24.4 %collective-permute-start.53 = (bf16[3,128,512]{2,1,0:T(8,128)(2,1)S(1)}, bf16[3,128,512]{2,1,0:T(8,128)(2,1)S(1)}, u32[]{:S(2)}, u32[]{:S(2)}) collective-permute-start(bf16[3,128,512]{2,1,0:T(8,128)(2,1)S(1)} %bitcast.394), channel_id=1, source_target_pairs={{0,16},{4,20},{8,24},{12,28},{16,0},{20,4},{24,8},{28,12},{1,17},{... | collective-permute-start | bytes 1179656 | tf_op jit(solution)/shard_map/ppermute | solution.py:360
  553.6 23.9 %collective-permute-start.55 = (bf16[1,768,256]{2,1,0:T(8,128)(2,1)S(1)}, bf16[1,768,256]{2,1,0:T(8,128)(2,1)S(1)}, u32[]{:S(2)}, u32[]{:S(2)}) collective-permute-start(bf16[1,768,256]{2,1,0:T(8,128)(2,1)S(1)} %bitcast.396), channel_id=1, source_target_pairs={{0,16},{4,20},{8,24},{12,28},{16,0},{20,4},{24,8},{28,12},{1,17},{... | collective-permute-start | bytes 1179656 | tf_op jit(solution)/shard_map/ppermute | solution.py:360
  554.3 16.3 %collective-permute-start.31 = (bf16[128,1024]{1,0:T(8,128)(2,1)S(1)}, bf16[128,1024]{1,0:T(8,128)(2,1)S(1)}, u32[]{:S(2)}, u32[]{:S(2)}) collective-permute-start(bf16[128,1024]{1,0:T(8,128)(2,1)S(1)} %copy-done.95), channel_id=1, source_target_pairs={{0,2},{1,3},{2,0},{3,1},{4,6},{5,7},{6,4},{7,5},{8,10},{9,11},{10,... | collective-permute-start | bytes 786440 | tf_op jit(solution)/shard_map/ppermute | solution.py:1087
  557.0 19.0 %collective-permute-start.54 = (bf16[4,32,512]{2,1,0:T(8,128)(2,1)S(1)}, bf16[4,32,512]{2,1,0:T(8,128)(2,1)S(1)}, u32[]{:S(2)}, u32[]{:S(2)}) collective-permute-start(bf16[4,32,512]{2,1,0:T(8,128)(2,1)S(1)} %get-tuple-element.268), channel_id=1, source_target_pairs={{0,2},{1,3},{2,0},{3,1},{4,6},{5,7},{6,4},{7,5},{8,10},{9,11},{10,... | collective-permute-start | bytes 393224 | tf_op jit(solution)/shard_map/ppermute | solution.py:360
  581.9 18.0 %collective-permute-start.57 = (bf16[3,256,512]{2,1,0:T(8,128)(2,1)S(1)}, bf16[3,256,512]{2,1,0:T(8,128)(2,1)S(1)}, u32[]{:S(2)}, u32[]{:S(2)}) collective-permute-start(bf16[3,256,512]{2,1,0:T(8,128)(2,1)S(1)} %bitcast.376), channel_id=1, source_target_pairs={{0,16},{4,20},{8,24},{12,28},{16,0},{20,4},{24,8},{28,12},{1,17},{... | collective-permute-start | bytes 2359304 | tf_op jit(solution)/shard_map/ppermute | solution.py:360
  582.9 17.1 %collective-permute-start.58 = (bf16[3,256,512]{2,1,0:T(8,128)(2,1)S(1)}, bf16[3,256,512]{2,1,0:T(8,128)(2,1)S(1)}, u32[]{:S(2)}, u32[]{:S(2)}) collective-permute-start(bf16[3,256,512]{2,1,0:T(8,128)(2,1)S(1)} %bitcast.377), channel_id=1, source_target_pairs={{0,8},{4,12},{8,0},{12,4},{16,24},{20,28},{24,16},{28,20},{1,9},{5... | collective-permute-start | bytes 2359304 | tf_op jit(solution)/shard_map/ppermute | solution.py:360
  584.5 15.4 %collective-permute-start.60 = (bf16[1,1536,256]{2,1,0:T(8,128)(2,1)S(1)}, bf16[1,1536,256]{2,1,0:T(8,128)(2,1)S(1)}, u32[]{:S(2)}, u32[]{:S(2)}) collective-permute-start(bf16[1,1536,256]{2,1,0:T(8,128)(2,1)S(1)} %bitcast.378), channel_id=1, source_target_pairs={{0,4},{4,0},{8,12},{12,8},{16,20},{20,16},{24,28},{28,24},{1,5},{5... | collective-permute-start | bytes 2359304 | tf_op jit(solution)/shard_map/ppermute | solution.py:360
  603.0 15.2 %collective-permute-start.67 = (bf16[6,512,512]{2,1,0:T(8,128)(2,1)}, bf16[6,512,512]{2,1,0:T(8,128)(2,1)}, u32[]{:S(2)}, u32[]{:S(2)}) collective-permute-start(bf16[6,512,512]{2,1,0:T(8,128)(2,1)} %bitcast.348), channel_id=1, source_target_pairs={{0,4},{4,0},{8,12},{12,8},{16,20},{20,16},{24,28},{28,24},{1,5},{5... | collective-permute-start | bytes 9437192 | tf_op jit(solution)/shard_map/ppermute | solution.py:360
  (169 other events, 1091.0 us)
Sparse Core Ops, SparseCore 0:
  129.7 77.8 all-gather.3
  256.4 51.9 reduce-scatter.4
  312.2 52.6 reduce-scatter.6
  367.1 27.1 reduce-scatter.8
  396.5 25.7 reduce-scatter.10
  439.6 27.1 all-gather.5
  468.7 33.5 all-gather.7

commit v4 on v3

--- a/solution.py
+++ b/solution.py
@@ -560,10 +560,9 @@
 
     @pl.when(head == 0)
     def _():
-        before = rest[:3] if with_sums else None
-        rows_ref[...] = own_rows + before[0][...] if with_sums else own_rows
-        along_ref[...] = own_along + before[1][...] if with_sums else own_along
-        shift_ref[...] = own_shift + before[2][...] if with_sums else own_shift
+        rows_ref[...] = own_rows + rest[0][...] if with_sums else own_rows
+        along_ref[...] = own_along
+        shift_ref[...] = own_shift
 
     @pl.when(head > 0)
     def _():
@@ -1011,6 +1010,58 @@
     )(rows)
 
 
+def compress_kernel(mem_ref, gc_ref, w_ref, bias_ref, new_ref, grad_ref, wide_ref, sum_ref):
+    stream = pl.program_id(0)
+    count = gc_ref.shape[1]
+    rows = mem_ref.shape[1]
+    blocks, depth, lanes = wide_ref.shape
+    for i in range(blocks):
+        wide_ref[i, :rows] = mem_ref[0, :, i * lanes : (i + 1) * lanes].astype(F32)
+        wide_ref[i, rows:] = jnp.zeros((depth - rows, lanes), F32)
+    made = jnp.zeros((count, gc_ref.shape[2]), F32) + bias_ref[...]
+    for tap in range(RATE):
+        taken = [wide_ref[i, pl.ds(tap, count, stride=RATE), :] for i in range(blocks)]
+        window = jnp.concatenate(taken, 1).astype(BF16)
+        made = made + jnp.dot(window, w_ref[tap], preferred_element_type=F32)
+        part = contract(window, gc_ref[0], 0, 0)
+        sum_ref[tap] = jnp.where(stream == 0, part, part + sum_ref[tap])
+    new_ref[0] = made.astype(BF16)
+
+    @pl.when(stream == pl.num_programs(0) - 1)
+    def _():
+        grad_ref[...] = sum_ref[...].astype(BF16)
+
+
+def compress_rows(memory, grad, weights, bias):
+    streams, rows, width = memory.shape
+    count, columns = grad.shape[1:]
+    return pl.pallas_call(
+        compress_kernel,
+        grid=(streams,),
+        in_specs=[
+            pl.BlockSpec((1, rows, width), lambda i: (i, 0, 0)),
+            pl.BlockSpec((1, count, columns), lambda i: (i, 0, 0)),
+            pl.BlockSpec(weights.shape, lambda i: (0, 0, 0)),
+            pl.BlockSpec((1, columns), lambda i: (0, 0)),
+        ],
+        out_specs=[
+            pl.BlockSpec((1, count, columns), lambda i: (i, 0, 0)),
+            pl.BlockSpec(weights.shape, lambda i: (0, 0, 0)),
+        ],
+        out_shape=[
+            jax.ShapeDtypeStruct((streams, count, columns), BF16),
+            jax.ShapeDtypeStruct(weights.shape, BF16),
+        ],
+        scratch_shapes=[
+            pltpu.VMEM((width // DH, RATE * count + 16, DH), F32),
+            pltpu.VMEM(weights.shape, F32),
+        ],
+        compiler_params=pltpu.CompilerParams(vmem_limit_bytes=48 * MIB),
+        cost_estimate=SHORT,
+        name="compress_rows",
+    )(memory, grad, weights, bias.reshape(1, -1))
+
+
 def own_streams_plan(
     inputs,
     memory,
@@ -1176,7 +1227,7 @@
     groups, biases, head_sums = [], [], []
     output_rows = send(output_parts)
 
-    first, start = [], 0
+    first, start, alongs, shifts = [], 0, [], []
     for call, heads in enumerate(CALLS):
         base = start // half_heads * half_heads
         group_heads = range(base, base + half_heads)
@@ -1206,7 +1257,9 @@
             down_sum, *passing = round_of(groups, bits, bit_names, [], [down_sum, *passing])
             down_sum = lax.all_gather(down_sum, "dp", tiled=True)
         *halves, d_rows, along, shift_part, bias_part = passing
-        head_sums = [d_rows, along, shift_part]
+        head_sums = [d_rows]
+        alongs.append(along)
+        shifts.append(shift_part)
         biases.append(bias_part)
         if start == group_heads.stop:
             groups.append(Chain(group_moves, [halves[0]], [halves[1]]))
@@ -1214,21 +1267,20 @@
     output = by_stream(output_rows)
 
     def compress(memory_all):
-        new_rows = memory_all.shape[1] // RATE
-        windows = memory_all[:, : new_rows * RATE].reshape(streams, new_rows, RATE, width)
-        made = jnp.einsum("srtd,tde->rse", windows, w_comp, preferred_element_type=F32)
-        grad = jnp.einsum("srtd,rse->tde", windows, grad_comp, preferred_element_type=F32)
-        grad = grad.astype(BF16).reshape(1, -1, grad.shape[2])
+        new_rows = grad_comp.shape[0]
+        padded = jnp.pad(by_stream(grad_comp), ((0, 0), (0, -new_rows % 16), (0, 0)))
+        made, grad = compress_rows(memory_all, padded, w_comp, comp_bias)
+        grad = grad.reshape(1, -1, grad.shape[2])
         moves = moves_of([core_cut] + wide_cuts, [core_cut] + wide_cuts)
-        return (made + comp_bias).astype(BF16), Chain(moves, *first_halves(grad, moves[0]))
+        return by_stream(made)[:new_rows], Chain(moves, *first_halves(grad, moves[0]))
 
     grad_comp_bias = jnp.sum(grad_comp.astype(F32), (0, 1))
     targets = jnp.stack([(me + shift) % seq_parts for shift in range(seq_parts)]).astype(jnp.int32)
     input_parts = input_grad(targets, d_rows, x_rows, d_hidden, gain_first, seq_parts)
     input_rows = send(input_parts)
 
-    grad_shift_first = jnp.sum(shift_part, 1)
-    grad_gain_first = (jnp.sum(along, 1) - shift_first * grad_shift_first) / gain_first
+    grad_shift_first = jnp.sum(sum(shifts), 1)
+    grad_gain_first = (jnp.sum(sum(alongs), 1) - shift_first * grad_shift_first) / gain_first
     vectors = jnp.concatenate(
         [
             jnp.concatenate(biases, 1).reshape(-1),
@@ -1256,30 +1308,29 @@
     pinned = {
         1: input_parts,
         2: [input_rows[1]],
-        5: [*input_rows[2:-1]],
         6: [input_rows[-1]],
+        7: [*input_rows[2:-1]],
     }
     comp = None
     while len(two.moves) > 1 or vector.moves:
-        active = [one, two] + [comp] * (turn > 0) + [vector] * (turn > 2)
+        active = [one, two] + [comp] * (turn > 1) + [vector] * (turn > 2)
         active = [c for c in active if len(c.moves) > (c in groups)]
         fence = pinned.get(turn, [])
-        if turn == 7:
-            grad_inputs = by_stream(place_rows(input_rows, owners))
-            fence = [grad_inputs]
         if turn == 8:
             results = finished(0, one, results)
             grad_w_comp = widen(comp.gives[0][0]).reshape(w_comp.shape)
-            fence = [*fence, *results, grad_w_comp]
+            grad_inputs = by_stream(place_rows(input_rows, owners))
+            fence = [*fence, *results, grad_w_comp, grad_inputs]
         through = [up_sum, memory_all] if turn == 0 else []
         through = round_of(active, bits, bit_names, fence, through)
         if turn == 0:
             up_sum = lax.all_gather(through[0], "dp", tiled=True)
             new_compressed, comp = compress(through[1])
-            pinned[3] = [new_compressed, output]
+            pinned[2] = [*pinned[2], new_compressed]
+            pinned[3] = [output]
             grad_w_down, grad_w_up = widen(down_sum), widen(up_sum, True)
             pinned[4] = [grad_w_down]
-            pinned[5] = [*pinned[5], grad_w_up]
+            pinned[5] = [grad_w_up]
         turn += 1
     vectors = vector.gives[0].reshape(-1)
 

time: 657 us -> 639 us (0.973)
  local copies, waits for them, and re-layouts: 117 us -> 95.8 us
  Pallas kernels: 204 us -> 211 us
    unnamed x298 -> x299, local copies, waits for them, and re-layouts: 79.8 us -> 67.3 us
  transfers between devices with their start and end apart: 76 -> 76, of which waited for: 21 -> 22; matrix products, arithmetic and copies ran while one was open for 23% -> 23% of each run, Pallas kernels for 30% -> 31%
where the time goes in v4:
time: 639 us; the launch traced here: 629 us
  Pallas kernels  211 us (33%)
  waiting for transfers between devices  118 us (18%)
  local copies, waits for them, and re-layouts  95.8 us (15%)
  matrix products  76 us (12%)
  starting transfers between devices  71.5 us (11%)
  other arithmetic  39.5 us (6%)
  between operations  17.5 us (3%)
    ppermute x57, waiting for transfers between devices, swap(): return lax.ppermute(rows, axis, [(i, i ^ distance) for i in range(count)])  102 us
    pallas_call x4, Pallas kernels, attend_back(): pl.pallas_call(functools.partial(attend_back_kernel, bool(sums)), grid=(c...  85.7 us
    unnamed x299, local copies, waits for them, and re-layouts  67.3 us
    ppermute x57, starting transfers between devices, swap(): return lax.ppermute(rows, axis, [(i, i ^ distance) for i in range(count)])  51.7 us
    dot_general x5, matrix products, contract(): lax.dot_general(left, right, (((left_dim,), (right_dim,)), ((), ())), pre...  46.5 us
    pallas_call x2, Pallas kernels, attend(): pl.pallas_call(attend_kernel, grid=(count, seg // block), in_specs=[pl.Bl...  41.9 us
    pallas_call x18, Pallas kernels, round_of(): pl.pallas_call(kernel, in_specs=[pl.BlockSpec(memory_space=pltpu.SMEM)] +...  37.1 us
    ppermute x12, starting transfers between devices, send(): lax.ppermute(part, 'seq', [(i, (i + shift) % seq_parts) for i in range(se...  19.2 us
  transfers between devices with their start and end apart: 76, of which 22 were waited for; matrix products, arithmetic and copies ran while one was open for 23% of the time, Pallas kernels for 31%

profile of v4, /device:TPU:0, one launch (start us, length us, event | category | flops | bytes accessed | tf_op | source)
XLA Modules:
  0.0 628.8 jit_solution(9639971263858977635)
XLA Ops:
  8.5 4.1 collective-permute-start.3
  15.1 3.5 copy_bitcast_fusion.2
  28.0 13.9 %multiply_sine_fusion = (f32[1536,512]{1,0:T(8,128)}, bf16[1536,512]{1,0:T(8,128)(2,1)}, bf16[1536,512]{1,0:T(8,128)(2,1)}, f32[1536,512]{1,0:T(8,128)}) fusion(f32[512]{0:T(512)S(1)} %multiply_exponential_fusion, f32[1536]{0:T(1024)S(1)} %iota_convert_fusion), kind=kLoop, calls=%fused_computation.11 | loop fusion | flops 2359296 | bytes 9445376 | tf_op jit(solution)/shard_map/sin | solution.py:33
  51.8 36.3 %collective-permute-done.4 = bf16[2,256,512]{2,1,0:T(8,128)(2,1)} collective-permute-done((bf16[2,256,512]{2,1,0:T(8,128)(2,1)}, bf16[2,256,512]{2,1,0:T(8,128)(2,1)}, u32[]{:S(2)}, u32[]{:S(2)}) %collective-permute-start.4) | collective-permute-done | bytes 524320 | tf_op jit(solution)/shard_map/ppermute | solution.py:360
  95.9 4.1 pad_maximum_fusion.1.refs_9_.table_ref
  103.1 5.6 norm_context.1
  112.7 5.2 convolution_convert_fusion.1.refs_2_.v_ref
  131.7 7.8 %convolution_convert_fusion.k_ref = bf16[1536,1024]{1,0:T(8,128)(2,1)} fusion(bf16[1536,1024]{1,0:T(8,128)(2,1)} %bitcast.316, bf16[1024,1024]{1,0:T(8,128)(2,1)} %wk_ref.7), kind=kOutput, calls=%fused_computation.13 | convolution fusion | flops 3222798336 | bytes 8388608 | tf_op jit(solution)/shard_map/dot_general | solution.py:1165
  143.4 20.9 %attend.2 = (bf16[8,512,1536]{2,1,0:T(8,128)(2,1)}, bf16[512,1024]{1,0:T(8,128)(2,1)}) custom-call(s32[1]{0:T(128)} %dynamic_slice.78.len_ref, bf16[512,1024]{1,0:T(8,128)(2,1)} %get-tuple-element.319.qc_ref, bf16[512,1024]{1,0:T(8,128)(2,1)} %get-tuple-element.318.qp_ref, bf16[1536,1024]{1,0:T(8,128)(2,1)} %convolution_convert_fusion.k_ref, ...), custom_call_target="tpu_custom_call" | custom-call | flops 1024 | bytes 1024 | tf_op jit(solution)/shard_map/attend/pallas_call | solution.py:451
  166.6 5.3 add_and_split.23
  177.2 3.6 collective-permute-done.15
  182.0 21.0 %attend.3 = (bf16[8,512,1536]{2,1,0:T(8,128)(2,1)}, bf16[512,1024]{1,0:T(8,128)(2,1)S(1)}) custom-call(s32[1]{0:T(128)} %dynamic_slice.78.len_ref, bf16[512,1024]{1,0:T(8,128)(2,1)} %get-tuple-element.319.qc_ref, bf16[512,1024]{1,0:T(8,128)(2,1)} %get-tuple-element.318.qp_ref, ...), custom_call_target="tpu_custom_call", output_to_operand_aliasing={{0}: (9, {}), {1}: (10, {})} | custom-call | flops 1024 | bytes 1024 | tf_op jit(solution)/shard_map/attend/pallas_call | solution.py:451
  206.4 4.2 add_and_split.24
  218.0 2.9 collective-permute-start.24
  223.8 2.7 copy-done.135
  226.5 17.8 %multiply_convert_fusion = (bf16[1024,2048]{1,0:T(8,128)(2,1)}, f32[1024,2048]{1,0:T(8,128)}) fusion(f32[2048]{0:T(1024)S(1)} %bitcast.460, bf16[1024,1024]{1,0:T(8,128)(2,1)S(1)} %bitcast.444, bf16[2048,1024]{1,0:T(8,128)(2,1)S(1)} %bitcast.470), kind=kOutput, calls=%fused_computation.10 | convolution fusion | flops 4315938816 | bytes 18882560 | tf_op jit(solution)/shard_map/dot_general | solution.py:349
  247.4 2.9 collective-permute-done.25
  254.6 6.2 convolution_convert_fusion.3
  260.9 14.0 %convert_reduce_fusion = (f32[2048]{0:T(1024)}, bf16[1024,2048]{1,0:T(8,128)(2,1)S(1)}) fusion(f32[1024,2048]{1,0:T(8,128)} %get-tuple-element.347, f32[2048]{0:T(1024)S(1)} %bitcast.461, bf16[1024,1024]{1,0:T(8,128)(2,1)} %bitcast.447, bf16[2048,1024]{1,0:T(8,128)(2,1)} %bitcast.471), kind=kOutput, calls=%fused_computation.9 | convolution fusion | flops 4343199744 | bytes 18890752 | tf_op jit(solution)/shard_map/dot_general | solution.py:349
  276.9 6.2 convolution_convert_fusion.2
  283.2 8.0 %fusion.25 = f32[2,512,1024]{2,1,0:T(8,128)S(1)} fusion(bf16[2,512,2048]{2,1,0:T(8,128)(2,1)} %bitcast.473, bf16[2048,1024,1]{1,0,2:T(8,128)(2,1)} %bitcast.469), kind=kOutput, calls=%fused_computation.122 | convolution fusion | flops 4294967296 | bytes 12582912 | tf_op jit(solution)/shard_map/dot_general | solution.py:1212
  292.5 4.5 fusion.24
  299.9 3.8 multiply_reduce_fusion
  303.7 3.9 fusion.21
  308.9 3.3 collective-permute-start.21
  316.2 2.8 out_grad.1
  320.7 20.8 %attend_back.4 = (bf16[6,512,512]{2,1,0:T(8,128)(2,1)}, bf16[6,512,512]{2,1,0:T(8,128)(2,1)}, f32[512,1024]{1,0:T(8,128)}, f32[1024,128]{1,0:T(8,128)S(1)}, f32[...) custom-call(s32[5]{0:T(128)S(1)} %stack.92.bits_ref.refs_0_, ...), custom_call_target="tpu_custom_call", output_to_operand_aliasing={{0}: (15, {}), {1}: (16, {})} | custom-call | flops 1024 | bytes 1024 | tf_op jit(solution)/shard_map/attend_back/pallas_call | solution.py:620
  343.7 21.8 %attend_back.5 = (bf16[6,512,512]{2,1,0:T(8,128)(2,1)}, bf16[6,512,512]{2,1,0:T(8,128)(2,1)}, f32[512,1024]{1,0:T(8,128)}, f32[1024,128]{1,0:T(8,128)S(1)}, f32[...) custom-call(s32[5]{0:T(128)S(1)} %stack.92.bits_ref.refs_0_, ...), custom_call_target="tpu_custom_call", output_to_operand_aliasing={{2}: (15, {}), {0}: (16, {}), {1}: (17, {})} | custom-call | flops 1024 | bytes 1024 | tf_op jit(solution)/shard_map/attend_back/pallas_call | solution.py:620
  369.3 21.4 %attend_back.6 = (bf16[4,512,512]{2,1,0:T(8,128)(2,1)}, bf16[4,512,512]{2,1,0:T(8,128)(2,1)}, f32[512,1024]{1,0:T(8,128)}, f32[1024,128]{1,0:T(8,128)S(1)}, f32[...) custom-call(s32[5]{0:T(128)S(1)} %stack.92.bits_ref.refs_0_, ...), custom_call_target="tpu_custom_call", output_to_operand_aliasing={{2}: (15, {})} | custom-call | flops 1024 | bytes 1024 | tf_op jit(solution)/shard_map/attend_back/pallas_call | solution.py:620
  390.8 4.7 add_and_split.25
  400.5 21.7 %attend_back.7 = (bf16[4,512,512]{2,1,0:T(8,128)(2,1)}, bf16[4,512,512]{2,1,0:T(8,128)(2,1)}, f32[512,1024]{1,0:T(8,128)}, f32[1024,128]{1,0:T(8,128)S(1)}, f32[...) custom-call(s32[5]{0:T(128)S(1)} %stack.92.bits_ref.refs_0_, ...), custom_call_target="tpu_custom_call", output_to_operand_aliasing={{2}: (15, {}), {0}: (16, {}), {1}: (17, {})} | custom-call | flops 1024 | bytes 1024 | tf_op jit(solution)/shard_map/attend_back/pallas_call | solution.py:620
  431.0 11.6 %collective-permute-done.33 = bf16[3,128,512]{2,1,0:T(8,128)(2,1)S(1)} collective-permute-done((bf16[3,128,512]{2,1,0:T(8,128)(2,1)}, bf16[3,128,512]{2,1,0:T(8,128)(2,1)S(1)}, u32[]{:S(2)}, u32[]{:S(2)}) %collective-permute-start.33) | collective-permute-done | bytes 393248 | tf_op jit(solution)/shard_map/ppermute | solution.py:360
  448.0 2.9 add_and_split.27
  466.0 3.1 input_grad.1
  475.9 6.1 compress_rows.1
  482.2 4.0 collective-permute-done.36
  486.3 4.9 collective-permute-done.37
  497.1 10.0 %collective-permute-done.39.refs_1_ = bf16[6,32,512]{2,1,0:T(8,128)(2,1)S(1)} collective-permute-done((bf16[6,32,512]{2,1,0:T(8,128)(2,1)S(1)}, bf16[6,32,512]{2,1,0:T(8,128)(2,1)S(1)}, u32[]{:S(2)}, u32[]{:S(2)}) %collective-permute-start.39) | collective-permute-done | bytes 196640 | tf_op jit(solution)/shard_map/ppermute | solution.py:360
  509.9 3.4 collective-permute-start.44
  514.5 4.1 collective-permute-done.43
  539.9 2.7 widen.4.refs_10_
  554.2 4.1 collective-permute-done.32.refs_3_.refs_10_
  559.2 3.2 collective-permute-done.60.refs_9_
  562.4 7.0 %collective-permute-done.59 = bf16[1,768,256]{2,1,0:T(8,128)(2,1)S(1)} collective-permute-done((bf16[1,768,256]{2,1,0:T(8,128)(2,1)S(1)}, bf16[1,768,256]{2,1,0:T(8,128)(2,1)S(1)}, u32[]{:S(2)}, u32[]{:S(2)}) %collective-permute-start.59) | collective-permute-done | bytes 393248 | tf_op jit(solution)/shard_map/ppermute | solution.py:360
  575.6 11.1 %collective-permute-done.31.refs_2_.refs_8_ = bf16[128,1024]{1,0:T(8,128)(2,1)S(1)} collective-permute-done((bf16[128,1024]{1,0:T(8,128)(2,1)S(1)}, bf16[128,1024]{1,0:T(8,128)(2,1)S(1)}, u32[]{:S(2)}, u32[]{:S(2)}) %collective-permute-start.31) | collective-permute-done | bytes 262176 | tf_op jit(solution)/shard_map/ppermute | solution.py:1138
  586.8 5.0 collective-permute-done.64.refs_7_
  601.6 7.0 %finish.2 = (f32[1024,1024]{1,0:T(8,128)}, f32[1024,1024]{1,0:T(8,128)}, f32[1024,1024]{1,0:T(8,128)}, f32[1024,1024]{1,0:T(8,128)}, f32[1024,1024]{1,0:T(8,128)}) custom-call(s32[5]{0:T(128)S(1)} %stack.92.bits_ref.refs_0_, bf16[6,512,512]{2,1,0:T(8,128)(2,1)S(1)} %bitcast.338, bf16[6,512,512]{2,1,0:T(8,128)(2,1)} %collective-permute-done.67.got_ref), custom_call_target="tpu_custom_call" | custom-call | flops 1024 | bytes 1024 | tf_op jit(solution)/shard_map/finish/pallas_call | solution.py:798
  616.1 5.3 finish.3
  (528 shorter events, 211.0 us)
Async XLA Ops:
  7.2 237.2 %all-gather.4.cloned.1.call-start = ((), (), s32[]{:S(2)}) async-start(), calls=%async_computation.4 | async-start | bytes 5242880 | tf_op jit(solution)/shard_map/all_gather | solution.py:1173
  8.5 17.6 %collective-permute-start.3 = (bf16[2,128,512]{2,1,0:T(8,128)(2,1)S(1)}, bf16[2,128,512]{2,1,0:T(8,128)(2,1)S(1)}, u32[]{:S(2)}, u32[]{:S(2)}) collective-permute-start(bf16[2,128,512]{2,1,0:T(8,128)(2,1)S(1)} %bitcast.364), channel_id=1, source_target_pairs={{0,2},{1,3},{2,0},{3,1},{4,6},{5,7},{6,4},{7,5},{8,10},{9,11},{10,... | collective-permute-start | bytes 786440 | tf_op jit(solution)/shard_map/ppermute | solution.py:360
  22.1 79.4 %collective-permute-start = (bf16[384,1024]{1,0:T(8,128)(2,1)}, bf16[384,1024]{1,0:T(8,128)(2,1)}, u32[]{:S(2)}, u32[]{:S(2)}) collective-permute-start(bf16[384,1024]{1,0:T(8,128)(2,1)} %get-tuple-element.311), channel_id=1, source_target_pairs={{0,1},{1,2},{2,3},{3,0},{4,5},{5,6},{6,7},{7,4},{8,9},{9,10},{10,1... | collective-permute-start | bytes 2359304 | tf_op jit(solution)/shard_map/ppermute | solution.py:1138
  23.7 79.4 %collective-permute-start.1 = (bf16[384,1024]{1,0:T(8,128)(2,1)}, bf16[384,1024]{1,0:T(8,128)(2,1)}, u32[]{:S(2)}, u32[]{:S(2)}) collective-permute-start(bf16[384,1024]{1,0:T(8,128)(2,1)} %get-tuple-element.310), channel_id=1, source_target_pairs={{0,2},{1,3},{2,0},{3,1},{4,6},{5,7},{6,4},{7,5},{8,10},{9,11},{10,... | collective-permute-start | bytes 2359304 | tf_op jit(solution)/shard_map/ppermute | solution.py:1138
  24.0 79.0 %collective-permute-start.2 = (bf16[384,1024]{1,0:T(8,128)(2,1)}, bf16[384,1024]{1,0:T(8,128)(2,1)}, u32[]{:S(2)}, u32[]{:S(2)}) collective-permute-start(bf16[384,1024]{1,0:T(8,128)(2,1)} %get-tuple-element.309), channel_id=1, source_target_pairs={{0,3},{1,0},{2,1},{3,2},{4,7},{5,4},{6,5},{7,6},{8,11},{9,8},{10,9... | collective-permute-start | bytes 2359304 | tf_op jit(solution)/shard_map/ppermute | solution.py:1138
  27.5 60.6 %collective-permute-start.4 = (bf16[2,256,512]{2,1,0:T(8,128)(2,1)}, bf16[2,256,512]{2,1,0:T(8,128)(2,1)}, u32[]{:S(2)}, u32[]{:S(2)}) collective-permute-start(bf16[2,256,512]{2,1,0:T(8,128)(2,1)} %bitcast.24), channel_id=1, source_target_pairs={{0,1},{1,0},{2,3},{3,2},{4,5},{5,4},{6,7},{7,6},{8,9},{9,8},{10,11... | collective-permute-start | bytes 1572872 | tf_op jit(solution)/shard_map/ppermute | solution.py:360
  100.0 18.0 %collective-permute-start.5 = (bf16[1,512,512]{2,1,0:T(8,128)(2,1)S(1)}, bf16[1,512,512]{2,1,0:T(8,128)(2,1)S(1)}, u32[]{:S(2)}, u32[]{:S(2)}) collective-permute-start(bf16[1,512,512]{2,1,0:T(8,128)(2,1)S(1)} %bitcast.350), channel_id=1, source_target_pairs={{0,8},{4,12},{8,0},{12,4},{16,24},{20,28},{24,16},{28,20},{1,9},{5... | collective-permute-start | bytes 1572872 | tf_op jit(solution)/shard_map/ppermute | solution.py:360
  101.5 16.5 %collective-permute-start.6 = (bf16[1,512,512]{2,1,0:T(8,128)(2,1)S(1)}, bf16[1,512,512]{2,1,0:T(8,128)(2,1)S(1)}, u32[]{:S(2)}, u32[]{:S(2)}) collective-permute-start(bf16[1,512,512]{2,1,0:T(8,128)(2,1)S(1)} %bitcast.353), channel_id=1, source_target_pairs={{0,16},{4,20},{8,24},{12,28},{16,0},{20,4},{24,8},{28,12},{1,17},{... | collective-permute-start | bytes 1572872 | tf_op jit(solution)/shard_map/ppermute | solution.py:360
  111.4 13.9 %collective-permute-start.10 = (bf16[2,256,512]{2,1,0:T(8,128)(2,1)S(1)}, bf16[2,256,512]{2,1,0:T(8,128)(2,1)S(1)}, u32[]{:S(2)}, u32[]{:S(2)}) collective-permute-start(bf16[2,256,512]{2,1,0:T(8,128)(2,1)S(1)} %bitcast.348), channel_id=1, source_target_pairs={{0,1},{1,0},{2,3},{3,2},{4,5},{5,4},{6,7},{7,6},{8,9},{9,8},{10,11... | collective-permute-start | bytes 1572872 | tf_op jit(solution)/shard_map/ppermute | solution.py:360
  120.3 44.0 %collective-permute-start.7 = (bf16[1,1024,512]{2,1,0:T(8,128)(2,1)}, bf16[1,1024,512]{2,1,0:T(8,128)(2,1)}, u32[]{:S(2)}, u32[]{:S(2)}) collective-permute-start(bf16[1,1024,512]{2,1,0:T(8,128)(2,1)} %bitcast.41), channel_id=1, source_target_pairs={{0,16},{4,20},{8,24},{12,28},{16,0},{20,4},{24,8},{28,12},{1,17},{... | collective-permute-start | bytes 3145736 | tf_op jit(solution)/shard_map/ppermute | solution.py:360
  121.9 42.5 %collective-permute-start.8 = (bf16[1,1024,512]{2,1,0:T(8,128)(2,1)}, bf16[1,1024,512]{2,1,0:T(8,128)(2,1)}, u32[]{:S(2)}, u32[]{:S(2)}) collective-permute-start(bf16[1,1024,512]{2,1,0:T(8,128)(2,1)} %bitcast.43), channel_id=1, source_target_pairs={{0,8},{4,12},{8,0},{12,4},{16,24},{20,28},{24,16},{28,20},{1,9},{5... | collective-permute-start | bytes 3145736 | tf_op jit(solution)/shard_map/ppermute | solution.py:360
  126.0 38.3 %collective-permute-start.11 = (bf16[1,512,512]{2,1,0:T(8,128)(2,1)S(1)}, bf16[1,512,512]{2,1,0:T(8,128)(2,1)}, u32[]{:S(2)}, u32[]{:S(2)}) collective-permute-start(bf16[1,512,512]{2,1,0:T(8,128)(2,1)S(1)} %bitcast.327), channel_id=1, source_target_pairs={{0,8},{4,12},{8,0},{12,4},{16,24},{20,28},{24,16},{28,20},{1,9},{5... | collective-permute-start | bytes 1572872 | tf_op jit(solution)/shard_map/ppermute | solution.py:360
  129.8 34.5 %collective-permute-start.12 = (bf16[1,512,512]{2,1,0:T(8,128)(2,1)S(1)}, bf16[1,512,512]{2,1,0:T(8,128)(2,1)}, u32[]{:S(2)}, u32[]{:S(2)}) collective-permute-start(bf16[1,512,512]{2,1,0:T(8,128)(2,1)S(1)} %bitcast.345), channel_id=1, source_target_pairs={{0,16},{4,20},{8,24},{12,28},{16,0},{20,4},{24,8},{28,12},{1,17},{... | collective-permute-start | bytes 1572872 | tf_op jit(solution)/shard_map/ppermute | solution.py:360
  131.4 211.6 %reduce-scatter.5.cloned.1.call-start = ((), (), s32[]{:S(2)}) async-start(), calls=%async_computation.5 | async-start | bytes 5242880 | tf_op jit(solution)/shard_map/reduce_scatter | solution.py:1206
  172.9 31.1 %collective-permute-start.13 = (bf16[1,1024,512]{2,1,0:T(8,128)(2,1)S(1)}, bf16[1,1024,512]{2,1,0:T(8,128)(2,1)}, u32[]{:S(2)}, u32[]{:S(2)}) collective-permute-start(bf16[1,1024,512]{2,1,0:T(8,128)(2,1)S(1)} %bitcast.335), channel_id=1, source_target_pairs={{0,16},{4,20},{8,24},{12,28},{16,0},{20,4},{24,8},{28,12},{1,17},{... | collective-permute-start | bytes 3145736 | tf_op jit(solution)/shard_map/ppermute | solution.py:360
  173.5 30.5 %collective-permute-start.14 = (bf16[1,1024,512]{2,1,0:T(8,128)(2,1)}, bf16[1,1024,512]{2,1,0:T(8,128)(2,1)}, u32[]{:S(2)}, u32[]{:S(2)}) collective-permute-start(bf16[1,1024,512]{2,1,0:T(8,128)(2,1)} %bitcast.59.rest_3_), channel_id=1, source_target_pairs={{0,8},{4,12},{8,0},{12,4},{16,24},{20,28},{24,16},{28,20},{1,9},{5... | collective-permute-start | bytes 3145736 | tf_op jit(solution)/shard_map/ppermute | solution.py:360
  214.0 30.3 %collective-permute-start.22 = (bf16[128,1024]{1,0:T(8,128)(2,1)S(1)}, bf16[128,1024]{1,0:T(8,128)(2,1)S(1)}, u32[]{:S(2)}, u32[]{:S(2)}) collective-permute-start(bf16[128,1024]{1,0:T(8,128)(2,1)S(1)} %bitcast.363), channel_id=1, source_target_pairs={{0,1},{1,2},{2,3},{3,0},{4,5},{5,6},{6,7},{7,4},{8,9},{9,10},{10,1... | collective-permute-start | bytes 786440 | tf_op jit(solution)/shard_map/ppermute | solution.py:1138
  215.9 28.5 %collective-permute-start.23 = (bf16[128,1024]{1,0:T(8,128)(2,1)S(1)}, bf16[128,1024]{1,0:T(8,128)(2,1)S(1)}, u32[]{:S(2)}, u32[]{:S(2)}) collective-permute-start(bf16[128,1024]{1,0:T(8,128)(2,1)S(1)} %bitcast.361), channel_id=1, source_target_pairs={{0,2},{1,3},{2,0},{3,1},{4,6},{5,7},{6,4},{7,5},{8,10},{9,11},{10,... | collective-permute-start | bytes 786440 | tf_op jit(solution)/shard_map/ppermute | solution.py:1138
  218.0 26.4 %collective-permute-start.24 = (bf16[128,1024]{1,0:T(8,128)(2,1)S(1)}, bf16[128,1024]{1,0:T(8,128)(2,1)}, u32[]{:S(2)}, u32[]{:S(2)}) collective-permute-start(bf16[128,1024]{1,0:T(8,128)(2,1)S(1)} %bitcast.359), channel_id=1, source_target_pairs={{0,3},{1,0},{2,1},{3,2},{4,7},{5,4},{6,5},{7,6},{8,11},{9,8},{10,9... | collective-permute-start | bytes 786440 | tf_op jit(solution)/shard_map/ppermute | solution.py:1138
  260.8 108.4 %reduce-scatter.7.cloned.1.call-start = ((), (), s32[]{:S(2)}) async-start(), calls=%async_computation.6 | async-start | bytes 5242880 | tf_op jit(solution)/shard_map/reduce_scatter | solution.py:1206
  283.1 139.1 %reduce-scatter.9.cloned.1.call-start = ((), (), s32[]{:S(2)}) async-start(), calls=%async_computation.7 | async-start | bytes 1310720 | tf_op jit(solution)/shard_map/reduce_scatter | solution.py:1246
  308.4 57.7 %collective-permute-start.19 = (bf16[128,1024]{1,0:T(8,128)(2,1)S(1)}, bf16[128,1024]{1,0:T(8,128)(2,1)S(1)}, u32[]{:S(2)}, u32[]{:S(2)}) collective-permute-start(bf16[128,1024]{1,0:T(8,128)(2,1)S(1)} %get-tuple-element.324.rest_3_), channel_id=1, source_target_pairs={{0,1},{1,2},{2,3},{3,0},{4,5},{5,6},{6,7},{7,4},{8,9},{9,10},{10,1... | collective-permute-start | bytes 786440 | tf_op jit(solution)/shard_map/ppermute | solution.py:1138
  308.4 57.7 %collective-permute-start.20 = (bf16[128,1024]{1,0:T(8,128)(2,1)S(1)}, bf16[128,1024]{1,0:T(8,128)(2,1)S(1)}, u32[]{:S(2)}, u32[]{:S(2)}) collective-permute-start(bf16[128,1024]{1,0:T(8,128)(2,1)S(1)} %get-tuple-element.323.rest_4_), channel_id=1, source_target_pairs={{0,2},{1,3},{2,0},{3,1},{4,6},{5,7},{6,4},{7,5},{8,10},{9,11},{10,... | collective-permute-start | bytes 786440 | tf_op jit(solution)/shard_map/ppermute | solution.py:1138
  308.9 57.2 %collective-permute-start.21 = (bf16[128,1024]{1,0:T(8,128)(2,1)S(1)}, bf16[128,1024]{1,0:T(8,128)(2,1)}, u32[]{:S(2)}, u32[]{:S(2)}) collective-permute-start(bf16[128,1024]{1,0:T(8,128)(2,1)S(1)} %get-tuple-element.322.rest_5_), channel_id=1, source_target_pairs={{0,3},{1,0},{2,1},{3,2},{4,7},{5,4},{6,5},{7,6},{8,11},{9,8},{10,9... | collective-permute-start | bytes 786440 | tf_op jit(solution)/shard_map/ppermute | solution.py:1138
  343.6 87.3 %reduce-scatter.11.cloned.1.call-start = ((), (), s32[]{:S(2)}) async-start(), calls=%async_computation.8 | async-start | bytes 1310720 | tf_op jit(solution)/shard_map/reduce_scatter | solution.py:1251
  369.2 21.6 %collective-permute-start.27 = (bf16[6,512,512]{2,1,0:T(8,128)(2,1)}, bf16[6,512,512]{2,1,0:T(8,128)(2,1)}, u32[]{:S(2)}, u32[]{:S(2)}) collective-permute-start(bf16[6,512,512]{2,1,0:T(8,128)(2,1)} %get-tuple-element.196.rest_1_), channel_id=1, source_target_pairs={{0,4},{4,0},{8,12},{12,8},{16,20},{20,16},{24,28},{28,24},{1,5},{5... | collective-permute-start | bytes 9437192 | tf_op jit(solution)/shard_map/ppermute | solution.py:360
  369.3 156.8 %all-gather.6.cloned.1.call-start = ((), (), s32[]{:S(2)}) async-start(), calls=%async_computation.9 | async-start | bytes 2359296 | tf_op jit(solution)/shard_map/all_gather | solution.py:1258
  398.9 23.3 %collective-permute-start.28 = (bf16[3,256,512]{2,1,0:T(8,128)(2,1)}, bf16[3,256,512]{2,1,0:T(8,128)(2,1)}, u32[]{:S(2)}, u32[]{:S(2)}) collective-permute-start(bf16[3,256,512]{2,1,0:T(8,128)(2,1)} %bitcast.96.rest_3_), channel_id=1, source_target_pairs={{0,16},{4,20},{8,24},{12,28},{16,0},{20,4},{24,8},{28,12},{1,17},{... | collective-permute-start | bytes 2359304 | tf_op jit(solution)/shard_map/ppermute | solution.py:360
  399.2 23.0 %collective-permute-start.29 = (bf16[3,256,512]{2,1,0:T(8,128)(2,1)}, bf16[3,256,512]{2,1,0:T(8,128)(2,1)}, u32[]{:S(2)}, u32[]{:S(2)}) collective-permute-start(bf16[3,256,512]{2,1,0:T(8,128)(2,1)} %bitcast.98.rest_4_), channel_id=1, source_target_pairs={{0,8},{4,12},{8,0},{12,4},{16,24},{20,28},{24,16},{28,20},{1,9},{5... | collective-permute-start | bytes 2359304 | tf_op jit(solution)/shard_map/ppermute | solution.py:360
  428.3 110.0 %all-gather.8.cloned.1.call-start = ((), (), s32[]{:S(2)}) async-start(), calls=%async_computation.10 | async-start | bytes 2359296 | tf_op jit(solution)/shard_map/all_gather | solution.py:1327
  428.3 15.8 %collective-permute-start.35 = (bf16[4,512,512]{2,1,0:T(8,128)(2,1)}, bf16[4,512,512]{2,1,0:T(8,128)(2,1)}, u32[]{:S(2)}, u32[]{:S(2)}) collective-permute-start(bf16[4,512,512]{2,1,0:T(8,128)(2,1)} %get-tuple-element.228), channel_id=1, source_target_pairs={{0,4},{4,0},{8,12},{12,8},{16,20},{20,16},{24,28},{28,24},{1,5},{5... | collective-permute-start | bytes 6291464 | tf_op jit(solution)/shard_map/ppermute | solution.py:360
  428.4 14.2 %collective-permute-start.33 = (bf16[3,128,512]{2,1,0:T(8,128)(2,1)}, bf16[3,128,512]{2,1,0:T(8,128)(2,1)S(1)}, u32[]{:S(2)}, u32[]{:S(2)}) collective-permute-start(bf16[3,128,512]{2,1,0:T(8,128)(2,1)} %bitcast.432), channel_id=1, source_target_pairs={{0,8},{4,12},{8,0},{12,4},{16,24},{20,28},{24,16},{28,20},{1,9},{5... | collective-permute-start | bytes 1179656 | tf_op jit(solution)/shard_map/ppermute | solution.py:360
  429.2 14.1 %collective-permute-start.34 = (bf16[3,128,512]{2,1,0:T(8,128)(2,1)S(1)}, bf16[3,128,512]{2,1,0:T(8,128)(2,1)S(1)}, u32[]{:S(2)}, u32[]{:S(2)}) collective-permute-start(bf16[3,128,512]{2,1,0:T(8,128)(2,1)S(1)} %bitcast.431), channel_id=1, source_target_pairs={{0,16},{4,20},{8,24},{12,28},{16,0},{20,4},{24,8},{28,12},{1,17},{... | collective-permute-start | bytes 1179656 | tf_op jit(solution)/shard_map/ppermute | solution.py:360
  469.2 27.8 %collective-permute-start.30 = (bf16[128,1024]{1,0:T(8,128)(2,1)S(1)}, bf16[128,1024]{1,0:T(8,128)(2,1)S(1)}, u32[]{:S(2)}, u32[]{:S(2)}) collective-permute-start(bf16[128,1024]{1,0:T(8,128)(2,1)S(1)} %get-tuple-element.220.refs_7_), channel_id=1, source_target_pairs={{0,1},{1,2},{2,3},{3,0},{4,5},{5,6},{6,7},{7,4},{8,9},{9,10},{10,1... | collective-permute-start | bytes 786440 | tf_op jit(solution)/shard_map/ppermute | solution.py:1138
  470.9 15.4 %collective-permute-start.36 = (bf16[6,64,512]{2,1,0:T(8,128)(2,1)S(1)}, bf16[6,64,512]{2,1,0:T(8,128)(2,1)S(1)}, u32[]{:S(2)}, u32[]{:S(2)}) collective-permute-start(bf16[6,64,512]{2,1,0:T(8,128)(2,1)S(1)} %bitcast.429), channel_id=1, source_target_pairs={{0,1},{1,0},{2,3},{3,2},{4,5},{5,4},{6,7},{7,6},{8,9},{9,8},{10,11... | collective-permute-start | bytes 1179656 | tf_op jit(solution)/shard_map/ppermute | solution.py:360
  472.8 18.3 %collective-permute-start.37 = (bf16[2,256,512]{2,1,0:T(8,128)(2,1)S(1)}, bf16[2,256,512]{2,1,0:T(8,128)(2,1)S(1)}, u32[]{:S(2)}, u32[]{:S(2)}) collective-permute-start(bf16[2,256,512]{2,1,0:T(8,128)(2,1)S(1)} %bitcast.428), channel_id=1, source_target_pairs={{0,16},{4,20},{8,24},{12,28},{16,0},{20,4},{24,8},{28,12},{1,17},{... | collective-permute-start | bytes 1572872 | tf_op jit(solution)/shard_map/ppermute | solution.py:360
  474.5 18.1 %collective-permute-start.38 = (bf16[2,256,512]{2,1,0:T(8,128)(2,1)S(1)}, bf16[2,256,512]{2,1,0:T(8,128)(2,1)S(1)}, u32[]{:S(2)}, u32[]{:S(2)}) collective-permute-start(bf16[2,256,512]{2,1,0:T(8,128)(2,1)S(1)} %bitcast.427), channel_id=1, source_target_pairs={{0,8},{4,12},{8,0},{12,4},{16,24},{20,28},{24,16},{28,20},{1,9},{5... | collective-permute-start | bytes 1572872 | tf_op jit(solution)/shard_map/ppermute | solution.py:360
  482.1 24.9 %collective-permute-start.42 = (bf16[1,1536,256]{2,1,0:T(8,128)(2,1)S(1)}, bf16[1,1536,256]{2,1,0:T(8,128)(2,1)S(1)}, u32[]{:S(2)}, u32[]{:S(2)}) collective-permute-start(bf16[1,1536,256]{2,1,0:T(8,128)(2,1)S(1)} %get-tuple-element.320), channel_id=1, source_target_pairs={{0,4},{4,0},{8,12},{12,8},{16,20},{20,16},{24,28},{28,24},{1,5},{5... | collective-permute-start | bytes 2359304 | tf_op jit(solution)/shard_map/ppermute | solution.py:360
  548.7 20.7 %collective-permute-start.56 = (bf16[3,256,512]{2,1,0:T(8,128)(2,1)S(1)}, bf16[3,256,512]{2,1,0:T(8,128)(2,1)S(1)}, u32[]{:S(2)}, u32[]{:S(2)}) collective-permute-start(bf16[3,256,512]{2,1,0:T(8,128)(2,1)S(1)} %bitcast.367), channel_id=1, source_target_pairs={{0,16},{4,20},{8,24},{12,28},{16,0},{20,4},{24,8},{28,12},{1,17},{... | collective-permute-start | bytes 2359304 | tf_op jit(solution)/shard_map/ppermute | solution.py:360
  549.1 20.2 %collective-permute-start.57 = (bf16[3,256,512]{2,1,0:T(8,128)(2,1)S(1)}, bf16[3,256,512]{2,1,0:T(8,128)(2,1)S(1)}, u32[]{:S(2)}, u32[]{:S(2)}) collective-permute-start(bf16[3,256,512]{2,1,0:T(8,128)(2,1)S(1)} %bitcast.368), channel_id=1, source_target_pairs={{0,8},{4,12},{8,0},{12,4},{16,24},{20,28},{24,16},{28,20},{1,9},{5... | collective-permute-start | bytes 2359304 | tf_op jit(solution)/shard_map/ppermute | solution.py:360
  550.4 18.9 %collective-permute-start.59 = (bf16[1,768,256]{2,1,0:T(8,128)(2,1)S(1)}, bf16[1,768,256]{2,1,0:T(8,128)(2,1)S(1)}, u32[]{:S(2)}, u32[]{:S(2)}) collective-permute-start(bf16[1,768,256]{2,1,0:T(8,128)(2,1)S(1)} %bitcast.386), channel_id=1, source_target_pairs={{0,16},{4,20},{8,24},{12,28},{16,0},{20,4},{24,8},{28,12},{1,17},{... | collective-permute-start | bytes 1179656 | tf_op jit(solution)/shard_map/ppermute | solution.py:360
  571.9 29.8 %collective-permute-start.67 = (bf16[6,512,512]{2,1,0:T(8,128)(2,1)}, bf16[6,512,512]{2,1,0:T(8,128)(2,1)}, u32[]{:S(2)}, u32[]{:S(2)}) collective-permute-start(bf16[6,512,512]{2,1,0:T(8,128)(2,1)} %bitcast.337), channel_id=1, source_target_pairs={{0,4},{4,0},{8,12},{12,8},{16,20},{20,16},{24,28},{28,24},{1,5},{5... | collective-permute-start | bytes 9437192 | tf_op jit(solution)/shard_map/ppermute | solution.py:360
  571.9 19.9 %collective-permute-start.63 = (bf16[1,1536,256]{2,1,0:T(8,128)(2,1)S(1)}, bf16[1,1536,256]{2,1,0:T(8,128)(2,1)S(1)}, u32[]{:S(2)}, u32[]{:S(2)}) collective-permute-start(bf16[1,1536,256]{2,1,0:T(8,128)(2,1)S(1)} %bitcast.372), channel_id=1, source_target_pairs={{0,4},{4,0},{8,12},{12,8},{16,20},{20,16},{24,28},{28,24},{1,5},{5... | collective-permute-start | bytes 2359304 | tf_op jit(solution)/shard_map/ppermute | solution.py:360
  572.4 14.4 %collective-permute-start.31 = (bf16[128,1024]{1,0:T(8,128)(2,1)S(1)}, bf16[128,1024]{1,0:T(8,128)(2,1)S(1)}, u32[]{:S(2)}, u32[]{:S(2)}) collective-permute-start(bf16[128,1024]{1,0:T(8,128)(2,1)S(1)} %copy-done.81), channel_id=1, source_target_pairs={{0,2},{1,3},{2,0},{3,1},{4,6},{5,7},{6,4},{7,5},{8,10},{9,11},{10,... | collective-permute-start | bytes 786440 | tf_op jit(solution)/shard_map/ppermute | solution.py:1138
  573.7 18.1 %collective-permute-start.61 = (bf16[2,128,512]{2,1,0:T(8,128)(2,1)S(1)}, bf16[2,128,512]{2,1,0:T(8,128)(2,1)S(1)}, u32[]{:S(2)}, u32[]{:S(2)}) collective-permute-start(bf16[2,128,512]{2,1,0:T(8,128)(2,1)S(1)} %bitcast.403), channel_id=1, source_target_pairs={{0,8},{4,12},{8,0},{12,4},{16,24},{20,28},{24,16},{28,20},{1,9},{5... | collective-permute-start | bytes 786440 | tf_op jit(solution)/shard_map/ppermute | solution.py:360
  575.3 16.4 %collective-permute-start.62 = (bf16[2,128,512]{2,1,0:T(8,128)(2,1)S(1)}, bf16[2,128,512]{2,1,0:T(8,128)(2,1)S(1)}, u32[]{:S(2)}, u32[]{:S(2)}) collective-permute-start(bf16[2,128,512]{2,1,0:T(8,128)(2,1)S(1)} %bitcast.405), channel_id=1, source_target_pairs={{0,16},{4,20},{8,24},{12,28},{16,0},{20,4},{24,8},{28,12},{1,17},{... | collective-permute-start | bytes 786440 | tf_op jit(solution)/shard_map/ppermute | solution.py:360
  593.3 15.4 %collective-permute-start.65 = (bf16[2,256,512]{2,1,0:T(8,128)(2,1)S(1)}, bf16[2,256,512]{2,1,0:T(8,128)(2,1)}, u32[]{:S(2)}, u32[]{:S(2)}) collective-permute-start(bf16[2,256,512]{2,1,0:T(8,128)(2,1)S(1)} %bitcast.375), channel_id=1, source_target_pairs={{0,16},{4,20},{8,24},{12,28},{16,0},{20,4},{24,8},{28,12},{1,17},{... | collective-permute-start | bytes 1572872 | tf_op jit(solution)/shard_map/ppermute | solution.py:360
  594.0 14.7 %collective-permute-start.66 = (bf16[2,256,512]{2,1,0:T(8,128)(2,1)}, bf16[2,256,512]{2,1,0:T(8,128)(2,1)}, u32[]{:S(2)}, u32[]{:S(2)}) collective-permute-start(bf16[2,256,512]{2,1,0:T(8,128)(2,1)} %bitcast.182), channel_id=1, source_target_pairs={{0,8},{4,12},{8,0},{12,4},{16,24},{20,28},{24,16},{28,20},{1,9},{5... | collective-permute-start | bytes 1572872 | tf_op jit(solution)/shard_map/ppermute | solution.py:360
  (169 other events, 1357.7 us)
Sparse Core Ops, SparseCore 0:
  131.5 77.7 all-gather.3
  260.9 49.4 reduce-scatter.4
  314.3 52.6 reduce-scatter.6
  369.1 27.1 reduce-scatter.8
  398.6 25.7 reduce-scatter.10
  428.4 28.9 all-gather.5
  459.2 33.0 all-gather.7

commit v5 on v4

--- a/solution.py
+++ b/solution.py
@@ -1313,7 +1313,7 @@
     }
     comp = None
     while len(two.moves) > 1 or vector.moves:
-        active = [one, two] + [comp] * (turn > 1) + [vector] * (turn > 2)
+        active = [one, two] + [comp] * (turn > 1) + [vector] * (turn > 1)
         active = [c for c in active if len(c.moves) > (c in groups)]
         fence = pinned.get(turn, [])
         if turn == 8:

time: 639 us -> 642 us (level)
    unnamed x299 -> x295, local copies, waits for them, and re-layouts: 67.3 us -> 65.8 us
  transfers between devices with their start and end apart: 76 -> 76, of which waited for: 22 -> 21; matrix products, arithmetic and copies ran while one was open for 23% -> 23% of each run, Pallas kernels for 31% -> 31%
where the time goes in v5:
time: 642 us; the launch traced here: 632 us
  Pallas kernels  211 us (33%)
  waiting for transfers between devices  120 us (19%)
  local copies, waits for them, and re-layouts  95 us (15%)
  matrix products  75.9 us (12%)
  starting transfers between devices  73.5 us (11%)
  other arithmetic  39.1 us (6%)
  between operations  17.6 us (3%)
    ppermute x57, waiting for transfers between devices, swap(): return lax.ppermute(rows, axis, [(i, i ^ distance) for i in range(count)])  103 us
    pallas_call x4, Pallas kernels, attend_back(): pl.pallas_call(functools.partial(attend_back_kernel, bool(sums)), grid=(c...  85.7 us
    unnamed x295, local copies, waits for them, and re-layouts  65.8 us
    ppermute x57, starting transfers between devices, swap(): return lax.ppermute(rows, axis, [(i, i ^ distance) for i in range(count)])  54.5 us
    dot_general x5, matrix products, contract(): lax.dot_general(left, right, (((left_dim,), (right_dim,)), ((), ())), pre...  46.5 us
    pallas_call x2, Pallas kernels, attend(): pl.pallas_call(attend_kernel, grid=(count, seg // block), in_specs=[pl.Bl...  41.9 us
    pallas_call x18, Pallas kernels, round_of(): pl.pallas_call(kernel, in_specs=[pl.BlockSpec(memory_space=pltpu.SMEM)] +...  37.1 us
    ppermute x12, starting transfers between devices, send(): lax.ppermute(part, 'seq', [(i, (i + shift) % seq_parts) for i in range(se...  18.5 us
  transfers between devices with their start and end apart: 76, of which 21 were waited for; matrix products, arithmetic and copies ran while one was open for 23% of the time, Pallas kernels for 31%

profile of v5, /device:TPU:0, one launch (start us, length us, event | category | flops | bytes accessed | tf_op | source)
XLA Modules:
  0.0 632.1 jit_solution(9910808571696899416)
XLA Ops:
  8.5 4.1 collective-permute-start.3
  15.1 3.5 copy_bitcast_fusion.2
  28.0 13.9 %multiply_sine_fusion = (f32[1536,512]{1,0:T(8,128)}, bf16[1536,512]{1,0:T(8,128)(2,1)}, bf16[1536,512]{1,0:T(8,128)(2,1)}, f32[1536,512]{1,0:T(8,128)}) fusion(f32[512]{0:T(512)S(1)} %multiply_exponential_fusion, f32[1536]{0:T(1024)S(1)} %iota_convert_fusion), kind=kLoop, calls=%fused_computation.11 | loop fusion | flops 2359296 | bytes 9445376 | tf_op jit(solution)/shard_map/sin | solution.py:33
  51.9 36.3 %collective-permute-done.4 = bf16[2,256,512]{2,1,0:T(8,128)(2,1)} collective-permute-done((bf16[2,256,512]{2,1,0:T(8,128)(2,1)}, bf16[2,256,512]{2,1,0:T(8,128)(2,1)}, u32[]{:S(2)}, u32[]{:S(2)}) %collective-permute-start.4) | collective-permute-done | bytes 524320 | tf_op jit(solution)/shard_map/ppermute | solution.py:360
  95.9 4.1 pad_maximum_fusion.1.refs_9_.table_ref
  103.1 5.6 norm_context.1
  112.7 5.2 convolution_convert_fusion.1.refs_2_.v_ref
  131.7 7.8 %convolution_convert_fusion.k_ref = bf16[1536,1024]{1,0:T(8,128)(2,1)} fusion(bf16[1536,1024]{1,0:T(8,128)(2,1)} %bitcast.316, bf16[1024,1024]{1,0:T(8,128)(2,1)} %wk_ref.7), kind=kOutput, calls=%fused_computation.13 | convolution fusion | flops 3222798336 | bytes 8388608 | tf_op jit(solution)/shard_map/dot_general | solution.py:1165
  143.4 20.9 %attend.2 = (bf16[8,512,1536]{2,1,0:T(8,128)(2,1)}, bf16[512,1024]{1,0:T(8,128)(2,1)}) custom-call(s32[1]{0:T(128)} %dynamic_slice.78.len_ref, bf16[512,1024]{1,0:T(8,128)(2,1)} %get-tuple-element.319.qc_ref, bf16[512,1024]{1,0:T(8,128)(2,1)} %get-tuple-element.318.qp_ref, bf16[1536,1024]{1,0:T(8,128)(2,1)} %convolution_convert_fusion.k_ref, ...), custom_call_target="tpu_custom_call" | custom-call | flops 1024 | bytes 1024 | tf_op jit(solution)/shard_map/attend/pallas_call | solution.py:451
  166.6 5.3 add_and_split.23
  177.2 3.5 collective-permute-done.15
  182.0 21.0 %attend.3 = (bf16[8,512,1536]{2,1,0:T(8,128)(2,1)}, bf16[512,1024]{1,0:T(8,128)(2,1)S(1)}) custom-call(s32[1]{0:T(128)} %dynamic_slice.78.len_ref, bf16[512,1024]{1,0:T(8,128)(2,1)} %get-tuple-element.319.qc_ref, bf16[512,1024]{1,0:T(8,128)(2,1)} %get-tuple-element.318.qp_ref, ...), custom_call_target="tpu_custom_call", output_to_operand_aliasing={{0}: (9, {}), {1}: (10, {})} | custom-call | flops 1024 | bytes 1024 | tf_op jit(solution)/shard_map/attend/pallas_call | solution.py:451
  206.4 4.2 add_and_split.24
  218.0 2.9 collective-permute-start.24
  223.8 2.7 copy-done.133
  226.5 17.8 %multiply_convert_fusion = (bf16[1024,2048]{1,0:T(8,128)(2,1)}, f32[1024,2048]{1,0:T(8,128)}) fusion(f32[2048]{0:T(1024)S(1)} %bitcast.460, bf16[1024,1024]{1,0:T(8,128)(2,1)S(1)} %bitcast.444, bf16[2048,1024]{1,0:T(8,128)(2,1)S(1)} %bitcast.470), kind=kOutput, calls=%fused_computation.10 | convolution fusion | flops 4315938816 | bytes 18882560 | tf_op jit(solution)/shard_map/dot_general | solution.py:349
  247.4 2.9 collective-permute-done.25
  254.6 6.2 convolution_convert_fusion.3
  260.9 14.0 %convert_reduce_fusion = (f32[2048]{0:T(1024)}, bf16[1024,2048]{1,0:T(8,128)(2,1)S(1)}) fusion(f32[1024,2048]{1,0:T(8,128)} %get-tuple-element.347, f32[2048]{0:T(1024)S(1)} %bitcast.461, bf16[1024,1024]{1,0:T(8,128)(2,1)} %bitcast.447, bf16[2048,1024]{1,0:T(8,128)(2,1)} %bitcast.471), kind=kOutput, calls=%fused_computation.9 | convolution fusion | flops 4343199744 | bytes 18890752 | tf_op jit(solution)/shard_map/dot_general | solution.py:349
  276.9 6.2 convolution_convert_fusion.2
  283.2 8.0 %fusion.25 = f32[2,512,1024]{2,1,0:T(8,128)S(1)} fusion(bf16[2,512,2048]{2,1,0:T(8,128)(2,1)} %bitcast.473, bf16[2048,1024,1]{1,0,2:T(8,128)(2,1)} %bitcast.469), kind=kOutput, calls=%fused_computation.122 | convolution fusion | flops 4294967296 | bytes 12582912 | tf_op jit(solution)/shard_map/dot_general | solution.py:1212
  292.5 4.5 fusion.24
  299.9 3.9 multiply_reduce_fusion
  303.8 3.9 fusion.21
  309.0 3.3 collective-permute-start.21
  316.2 2.8 out_grad.1
  320.7 20.8 %attend_back.4 = (bf16[6,512,512]{2,1,0:T(8,128)(2,1)}, bf16[6,512,512]{2,1,0:T(8,128)(2,1)}, f32[512,1024]{1,0:T(8,128)}, f32[1024,128]{1,0:T(8,128)S(1)}, f32[...) custom-call(s32[5]{0:T(128)S(1)} %stack.92.bits_ref.refs_0_, ...), custom_call_target="tpu_custom_call", output_to_operand_aliasing={{0}: (15, {}), {1}: (16, {})} | custom-call | flops 1024 | bytes 1024 | tf_op jit(solution)/shard_map/attend_back/pallas_call | solution.py:620
  343.7 21.8 %attend_back.5 = (bf16[6,512,512]{2,1,0:T(8,128)(2,1)}, bf16[6,512,512]{2,1,0:T(8,128)(2,1)}, f32[512,1024]{1,0:T(8,128)}, f32[1024,128]{1,0:T(8,128)S(1)}, f32[...) custom-call(s32[5]{0:T(128)S(1)} %stack.92.bits_ref.refs_0_, ...), custom_call_target="tpu_custom_call", output_to_operand_aliasing={{2}: (15, {}), {0}: (16, {}), {1}: (17, {})} | custom-call | flops 1024 | bytes 1024 | tf_op jit(solution)/shard_map/attend_back/pallas_call | solution.py:620
  369.4 21.4 %attend_back.6 = (bf16[4,512,512]{2,1,0:T(8,128)(2,1)}, bf16[4,512,512]{2,1,0:T(8,128)(2,1)}, f32[512,1024]{1,0:T(8,128)}, f32[1024,128]{1,0:T(8,128)S(1)}, f32[...) custom-call(s32[5]{0:T(128)S(1)} %stack.92.bits_ref.refs_0_, ...), custom_call_target="tpu_custom_call", output_to_operand_aliasing={{2}: (15, {})} | custom-call | flops 1024 | bytes 1024 | tf_op jit(solution)/shard_map/attend_back/pallas_call | solution.py:620
  390.8 4.7 add_and_split.25
  400.5 21.7 %attend_back.7 = (bf16[4,512,512]{2,1,0:T(8,128)(2,1)}, bf16[4,512,512]{2,1,0:T(8,128)(2,1)}, f32[512,1024]{1,0:T(8,128)}, f32[1024,128]{1,0:T(8,128)S(1)}, f32[...) custom-call(s32[5]{0:T(128)S(1)} %stack.92.bits_ref.refs_0_, ...), custom_call_target="tpu_custom_call", output_to_operand_aliasing={{2}: (15, {}), {0}: (16, {}), {1}: (17, {})} | custom-call | flops 1024 | bytes 1024 | tf_op jit(solution)/shard_map/attend_back/pallas_call | solution.py:620
  432.7 9.8 %collective-permute-done.33 = bf16[3,128,512]{2,1,0:T(8,128)(2,1)S(1)} collective-permute-done((bf16[3,128,512]{2,1,0:T(8,128)(2,1)}, bf16[3,128,512]{2,1,0:T(8,128)(2,1)S(1)}, u32[]{:S(2)}, u32[]{:S(2)}) %collective-permute-start.33) | collective-permute-done | bytes 393248 | tf_op jit(solution)/shard_map/ppermute | solution.py:360
  448.0 2.9 add_and_split.27
  463.0 3.1 input_grad.1
  472.9 6.0 compress_rows.1
  479.2 4.1 collective-permute-done.36
  492.8 10.0 %collective-permute-done.39.refs_1_ = bf16[6,32,512]{2,1,0:T(8,128)(2,1)S(1)} collective-permute-done((bf16[6,32,512]{2,1,0:T(8,128)(2,1)S(1)}, bf16[6,32,512]{2,1,0:T(8,128)(2,1)S(1)}, u32[]{:S(2)}, u32[]{:S(2)}) %collective-permute-start.39) | collective-permute-done | bytes 196640 | tf_op jit(solution)/shard_map/ppermute | solution.py:360
  509.8 5.8 collective-permute-done.47.refs_7_
  528.2 3.0 collective-permute-done.49.refs_3_
  537.5 2.8 collective-permute-start.54
  542.4 2.7 widen.4.refs_10_
  545.7 3.0 collective-permute-done.55
  557.0 6.0 collective-permute-done.32.refs_3_.refs_10_
  564.4 3.6 collective-permute-done.61.refs_9_
  568.0 9.8 %collective-permute-done.60 = bf16[1,768,256]{2,1,0:T(8,128)(2,1)S(1)} collective-permute-done((bf16[1,768,256]{2,1,0:T(8,128)(2,1)S(1)}, bf16[1,768,256]{2,1,0:T(8,128)(2,1)S(1)}, u32[]{:S(2)}, u32[]{:S(2)}) %collective-permute-start.60) | collective-permute-done | bytes 393248 | tf_op jit(solution)/shard_map/ppermute | solution.py:360
  584.2 11.3 %collective-permute-done.31.refs_2_.refs_6_ = bf16[128,1024]{1,0:T(8,128)(2,1)S(1)} collective-permute-done((bf16[128,1024]{1,0:T(8,128)(2,1)S(1)}, bf16[128,1024]{1,0:T(8,128)(2,1)S(1)}, u32[]{:S(2)}, u32[]{:S(2)}) %collective-permute-start.31) | collective-permute-done | bytes 262176 | tf_op jit(solution)/shard_map/ppermute | solution.py:1138
  604.9 7.0 %finish.2 = (f32[1024,1024]{1,0:T(8,128)}, f32[1024,1024]{1,0:T(8,128)}, f32[1024,1024]{1,0:T(8,128)}, f32[1024,1024]{1,0:T(8,128)}, f32[1024,1024]{1,0:T(8,128)}) custom-call(s32[5]{0:T(128)S(1)} %stack.92.bits_ref.refs_0_, bf16[6,512,512]{2,1,0:T(8,128)(2,1)S(1)} %bitcast.338, bf16[6,512,512]{2,1,0:T(8,128)(2,1)} %collective-permute-done.67.got_ref), custom_call_target="tpu_custom_call" | custom-call | flops 1024 | bytes 1024 | tf_op jit(solution)/shard_map/finish/pallas_call | solution.py:798
  619.4 5.3 finish.3
  (524 shorter events, 213.6 us)
Async XLA Ops:
  7.2 237.2 %all-gather.4.cloned.1.call-start = ((), (), s32[]{:S(2)}) async-start(), calls=%async_computation.4 | async-start | bytes 5242880 | tf_op jit(solution)/shard_map/all_gather | solution.py:1173
  8.5 17.6 %collective-permute-start.3 = (bf16[2,128,512]{2,1,0:T(8,128)(2,1)S(1)}, bf16[2,128,512]{2,1,0:T(8,128)(2,1)S(1)}, u32[]{:S(2)}, u32[]{:S(2)}) collective-permute-start(bf16[2,128,512]{2,1,0:T(8,128)(2,1)S(1)} %bitcast.364), channel_id=1, source_target_pairs={{0,2},{1,3},{2,0},{3,1},{4,6},{5,7},{6,4},{7,5},{8,10},{9,11},{10,... | collective-permute-start | bytes 786440 | tf_op jit(solution)/shard_map/ppermute | solution.py:360
  22.1 79.4 %collective-permute-start = (bf16[384,1024]{1,0:T(8,128)(2,1)}, bf16[384,1024]{1,0:T(8,128)(2,1)}, u32[]{:S(2)}, u32[]{:S(2)}) collective-permute-start(bf16[384,1024]{1,0:T(8,128)(2,1)} %get-tuple-element.311), channel_id=1, source_target_pairs={{0,1},{1,2},{2,3},{3,0},{4,5},{5,6},{6,7},{7,4},{8,9},{9,10},{10,1... | collective-permute-start | bytes 2359304 | tf_op jit(solution)/shard_map/ppermute | solution.py:1138
  23.7 79.4 %collective-permute-start.1 = (bf16[384,1024]{1,0:T(8,128)(2,1)}, bf16[384,1024]{1,0:T(8,128)(2,1)}, u32[]{:S(2)}, u32[]{:S(2)}) collective-permute-start(bf16[384,1024]{1,0:T(8,128)(2,1)} %get-tuple-element.310), channel_id=1, source_target_pairs={{0,2},{1,3},{2,0},{3,1},{4,6},{5,7},{6,4},{7,5},{8,10},{9,11},{10,... | collective-permute-start | bytes 2359304 | tf_op jit(solution)/shard_map/ppermute | solution.py:1138
  24.0 79.0 %collective-permute-start.2 = (bf16[384,1024]{1,0:T(8,128)(2,1)}, bf16[384,1024]{1,0:T(8,128)(2,1)}, u32[]{:S(2)}, u32[]{:S(2)}) collective-permute-start(bf16[384,1024]{1,0:T(8,128)(2,1)} %get-tuple-element.309), channel_id=1, source_target_pairs={{0,3},{1,0},{2,1},{3,2},{4,7},{5,4},{6,5},{7,6},{8,11},{9,8},{10,9... | collective-permute-start | bytes 2359304 | tf_op jit(solution)/shard_map/ppermute | solution.py:1138
  27.5 60.6 %collective-permute-start.4 = (bf16[2,256,512]{2,1,0:T(8,128)(2,1)}, bf16[2,256,512]{2,1,0:T(8,128)(2,1)}, u32[]{:S(2)}, u32[]{:S(2)}) collective-permute-start(bf16[2,256,512]{2,1,0:T(8,128)(2,1)} %bitcast.24), channel_id=1, source_target_pairs={{0,1},{1,0},{2,3},{3,2},{4,5},{5,4},{6,7},{7,6},{8,9},{9,8},{10,11... | collective-permute-start | bytes 1572872 | tf_op jit(solution)/shard_map/ppermute | solution.py:360
  100.0 18.0 %collective-permute-start.5 = (bf16[1,512,512]{2,1,0:T(8,128)(2,1)S(1)}, bf16[1,512,512]{2,1,0:T(8,128)(2,1)S(1)}, u32[]{:S(2)}, u32[]{:S(2)}) collective-permute-start(bf16[1,512,512]{2,1,0:T(8,128)(2,1)S(1)} %bitcast.350), channel_id=1, source_target_pairs={{0,8},{4,12},{8,0},{12,4},{16,24},{20,28},{24,16},{28,20},{1,9},{5... | collective-permute-start | bytes 1572872 | tf_op jit(solution)/shard_map/ppermute | solution.py:360
  101.5 16.5 %collective-permute-start.6 = (bf16[1,512,512]{2,1,0:T(8,128)(2,1)S(1)}, bf16[1,512,512]{2,1,0:T(8,128)(2,1)S(1)}, u32[]{:S(2)}, u32[]{:S(2)}) collective-permute-start(bf16[1,512,512]{2,1,0:T(8,128)(2,1)S(1)} %bitcast.353), channel_id=1, source_target_pairs={{0,16},{4,20},{8,24},{12,28},{16,0},{20,4},{24,8},{28,12},{1,17},{... | collective-permute-start | bytes 1572872 | tf_op jit(solution)/shard_map/ppermute | solution.py:360
  120.3 44.0 %collective-permute-start.7 = (bf16[1,1024,512]{2,1,0:T(8,128)(2,1)}, bf16[1,1024,512]{2,1,0:T(8,128)(2,1)}, u32[]{:S(2)}, u32[]{:S(2)}) collective-permute-start(bf16[1,1024,512]{2,1,0:T(8,128)(2,1)} %bitcast.41), channel_id=1, source_target_pairs={{0,16},{4,20},{8,24},{12,28},{16,0},{20,4},{24,8},{28,12},{1,17},{... | collective-permute-start | bytes 3145736 | tf_op jit(solution)/shard_map/ppermute | solution.py:360
  121.9 42.5 %collective-permute-start.8 = (bf16[1,1024,512]{2,1,0:T(8,128)(2,1)}, bf16[1,1024,512]{2,1,0:T(8,128)(2,1)}, u32[]{:S(2)}, u32[]{:S(2)}) collective-permute-start(bf16[1,1024,512]{2,1,0:T(8,128)(2,1)} %bitcast.43), channel_id=1, source_target_pairs={{0,8},{4,12},{8,0},{12,4},{16,24},{20,28},{24,16},{28,20},{1,9},{5... | collective-permute-start | bytes 3145736 | tf_op jit(solution)/shard_map/ppermute | solution.py:360
  126.0 38.3 %collective-permute-start.11 = (bf16[1,512,512]{2,1,0:T(8,128)(2,1)S(1)}, bf16[1,512,512]{2,1,0:T(8,128)(2,1)}, u32[]{:S(2)}, u32[]{:S(2)}) collective-permute-start(bf16[1,512,512]{2,1,0:T(8,128)(2,1)S(1)} %bitcast.327), channel_id=1, source_target_pairs={{0,8},{4,12},{8,0},{12,4},{16,24},{20,28},{24,16},{28,20},{1,9},{5... | collective-permute-start | bytes 1572872 | tf_op jit(solution)/shard_map/ppermute | solution.py:360
  129.8 34.5 %collective-permute-start.12 = (bf16[1,512,512]{2,1,0:T(8,128)(2,1)S(1)}, bf16[1,512,512]{2,1,0:T(8,128)(2,1)}, u32[]{:S(2)}, u32[]{:S(2)}) collective-permute-start(bf16[1,512,512]{2,1,0:T(8,128)(2,1)S(1)} %bitcast.345), channel_id=1, source_target_pairs={{0,16},{4,20},{8,24},{12,28},{16,0},{20,4},{24,8},{28,12},{1,17},{... | collective-permute-start | bytes 1572872 | tf_op jit(solution)/shard_map/ppermute | solution.py:360
  131.4 211.7 %reduce-scatter.5.cloned.1.call-start = ((), (), s32[]{:S(2)}) async-start(), calls=%async_computation.5 | async-start | bytes 5242880 | tf_op jit(solution)/shard_map/reduce_scatter | solution.py:1206
  172.9 31.1 %collective-permute-start.13 = (bf16[1,1024,512]{2,1,0:T(8,128)(2,1)S(1)}, bf16[1,1024,512]{2,1,0:T(8,128)(2,1)}, u32[]{:S(2)}, u32[]{:S(2)}) collective-permute-start(bf16[1,1024,512]{2,1,0:T(8,128)(2,1)S(1)} %bitcast.335), channel_id=1, source_target_pairs={{0,16},{4,20},{8,24},{12,28},{16,0},{20,4},{24,8},{28,12},{1,17},{... | collective-permute-start | bytes 3145736 | tf_op jit(solution)/shard_map/ppermute | solution.py:360
  173.5 30.5 %collective-permute-start.14 = (bf16[1,1024,512]{2,1,0:T(8,128)(2,1)}, bf16[1,1024,512]{2,1,0:T(8,128)(2,1)}, u32[]{:S(2)}, u32[]{:S(2)}) collective-permute-start(bf16[1,1024,512]{2,1,0:T(8,128)(2,1)} %bitcast.59.rest_3_), channel_id=1, source_target_pairs={{0,8},{4,12},{8,0},{12,4},{16,24},{20,28},{24,16},{28,20},{1,9},{5... | collective-permute-start | bytes 3145736 | tf_op jit(solution)/shard_map/ppermute | solution.py:360
  214.0 30.3 %collective-permute-start.22 = (bf16[128,1024]{1,0:T(8,128)(2,1)S(1)}, bf16[128,1024]{1,0:T(8,128)(2,1)S(1)}, u32[]{:S(2)}, u32[]{:S(2)}) collective-permute-start(bf16[128,1024]{1,0:T(8,128)(2,1)S(1)} %bitcast.363), channel_id=1, source_target_pairs={{0,1},{1,2},{2,3},{3,0},{4,5},{5,6},{6,7},{7,4},{8,9},{9,10},{10,1... | collective-permute-start | bytes 786440 | tf_op jit(solution)/shard_map/ppermute | solution.py:1138
  215.8 28.5 %collective-permute-start.23 = (bf16[128,1024]{1,0:T(8,128)(2,1)S(1)}, bf16[128,1024]{1,0:T(8,128)(2,1)S(1)}, u32[]{:S(2)}, u32[]{:S(2)}) collective-permute-start(bf16[128,1024]{1,0:T(8,128)(2,1)S(1)} %bitcast.361), channel_id=1, source_target_pairs={{0,2},{1,3},{2,0},{3,1},{4,6},{5,7},{6,4},{7,5},{8,10},{9,11},{10,... | collective-permute-start | bytes 786440 | tf_op jit(solution)/shard_map/ppermute | solution.py:1138
  218.0 26.4 %collective-permute-start.24 = (bf16[128,1024]{1,0:T(8,128)(2,1)S(1)}, bf16[128,1024]{1,0:T(8,128)(2,1)}, u32[]{:S(2)}, u32[]{:S(2)}) collective-permute-start(bf16[128,1024]{1,0:T(8,128)(2,1)S(1)} %bitcast.359), channel_id=1, source_target_pairs={{0,3},{1,0},{2,1},{3,2},{4,7},{5,4},{6,5},{7,6},{8,11},{9,8},{10,9... | collective-permute-start | bytes 786440 | tf_op jit(solution)/shard_map/ppermute | solution.py:1138
  260.8 108.4 %reduce-scatter.7.cloned.1.call-start = ((), (), s32[]{:S(2)}) async-start(), calls=%async_computation.6 | async-start | bytes 5242880 | tf_op jit(solution)/shard_map/reduce_scatter | solution.py:1206
  283.1 139.0 %reduce-scatter.9.cloned.1.call-start = ((), (), s32[]{:S(2)}) async-start(), calls=%async_computation.7 | async-start | bytes 1310720 | tf_op jit(solution)/shard_map/reduce_scatter | solution.py:1246
  308.5 57.7 %collective-permute-start.19 = (bf16[128,1024]{1,0:T(8,128)(2,1)S(1)}, bf16[128,1024]{1,0:T(8,128)(2,1)S(1)}, u32[]{:S(2)}, u32[]{:S(2)}) collective-permute-start(bf16[128,1024]{1,0:T(8,128)(2,1)S(1)} %get-tuple-element.324.rest_3_), channel_id=1, source_target_pairs={{0,1},{1,2},{2,3},{3,0},{4,5},{5,6},{6,7},{7,4},{8,9},{9,10},{10,1... | collective-permute-start | bytes 786440 | tf_op jit(solution)/shard_map/ppermute | solution.py:1138
  308.5 57.7 %collective-permute-start.20 = (bf16[128,1024]{1,0:T(8,128)(2,1)S(1)}, bf16[128,1024]{1,0:T(8,128)(2,1)S(1)}, u32[]{:S(2)}, u32[]{:S(2)}) collective-permute-start(bf16[128,1024]{1,0:T(8,128)(2,1)S(1)} %get-tuple-element.323.rest_4_), channel_id=1, source_target_pairs={{0,2},{1,3},{2,0},{3,1},{4,6},{5,7},{6,4},{7,5},{8,10},{9,11},{10,... | collective-permute-start | bytes 786440 | tf_op jit(solution)/shard_map/ppermute | solution.py:1138
  309.0 57.1 %collective-permute-start.21 = (bf16[128,1024]{1,0:T(8,128)(2,1)S(1)}, bf16[128,1024]{1,0:T(8,128)(2,1)}, u32[]{:S(2)}, u32[]{:S(2)}) collective-permute-start(bf16[128,1024]{1,0:T(8,128)(2,1)S(1)} %get-tuple-element.322.rest_5_), channel_id=1, source_target_pairs={{0,3},{1,0},{2,1},{3,2},{4,7},{5,4},{6,5},{7,6},{8,11},{9,8},{10,9... | collective-permute-start | bytes 786440 | tf_op jit(solution)/shard_map/ppermute | solution.py:1138
  343.7 89.0 %reduce-scatter.11.cloned.1.call-start = ((), (), s32[]{:S(2)}) async-start(), calls=%async_computation.8 | async-start | bytes 1310720 | tf_op jit(solution)/shard_map/reduce_scatter | solution.py:1251
  369.2 21.6 %collective-permute-start.27 = (bf16[6,512,512]{2,1,0:T(8,128)(2,1)}, bf16[6,512,512]{2,1,0:T(8,128)(2,1)}, u32[]{:S(2)}, u32[]{:S(2)}) collective-permute-start(bf16[6,512,512]{2,1,0:T(8,128)(2,1)} %get-tuple-element.196.rest_1_), channel_id=1, source_target_pairs={{0,4},{4,0},{8,12},{12,8},{16,20},{20,16},{24,28},{28,24},{1,5},{5... | collective-permute-start | bytes 9437192 | tf_op jit(solution)/shard_map/ppermute | solution.py:360
  369.3 154.9 %all-gather.6.cloned.1.call-start = ((), (), s32[]{:S(2)}) async-start(), calls=%async_computation.9 | async-start | bytes 2359296 | tf_op jit(solution)/shard_map/all_gather | solution.py:1258
  398.9 23.3 %collective-permute-start.28 = (bf16[3,256,512]{2,1,0:T(8,128)(2,1)}, bf16[3,256,512]{2,1,0:T(8,128)(2,1)}, u32[]{:S(2)}, u32[]{:S(2)}) collective-permute-start(bf16[3,256,512]{2,1,0:T(8,128)(2,1)} %bitcast.96.rest_3_), channel_id=1, source_target_pairs={{0,16},{4,20},{8,24},{12,28},{16,0},{20,4},{24,8},{28,12},{1,17},{... | collective-permute-start | bytes 2359304 | tf_op jit(solution)/shard_map/ppermute | solution.py:360
  399.1 23.0 %collective-permute-start.29 = (bf16[3,256,512]{2,1,0:T(8,128)(2,1)}, bf16[3,256,512]{2,1,0:T(8,128)(2,1)}, u32[]{:S(2)}, u32[]{:S(2)}) collective-permute-start(bf16[3,256,512]{2,1,0:T(8,128)(2,1)} %bitcast.98.rest_4_), channel_id=1, source_target_pairs={{0,8},{4,12},{8,0},{12,4},{16,24},{20,28},{24,16},{28,20},{1,9},{5... | collective-permute-start | bytes 2359304 | tf_op jit(solution)/shard_map/ppermute | solution.py:360
  428.3 112.5 %all-gather.8.cloned.1.call-start = ((), (), s32[]{:S(2)}) async-start(), calls=%async_computation.10 | async-start | bytes 2359296 | tf_op jit(solution)/shard_map/all_gather | solution.py:1327
  428.3 15.8 %collective-permute-start.35 = (bf16[4,512,512]{2,1,0:T(8,128)(2,1)}, bf16[4,512,512]{2,1,0:T(8,128)(2,1)}, u32[]{:S(2)}, u32[]{:S(2)}) collective-permute-start(bf16[4,512,512]{2,1,0:T(8,128)(2,1)} %get-tuple-element.228), channel_id=1, source_target_pairs={{0,4},{4,0},{8,12},{12,8},{16,20},{20,16},{24,28},{28,24},{1,5},{5... | collective-permute-start | bytes 6291464 | tf_op jit(solution)/shard_map/ppermute | solution.py:360
  428.4 14.2 %collective-permute-start.33 = (bf16[3,128,512]{2,1,0:T(8,128)(2,1)}, bf16[3,128,512]{2,1,0:T(8,128)(2,1)S(1)}, u32[]{:S(2)}, u32[]{:S(2)}) collective-permute-start(bf16[3,128,512]{2,1,0:T(8,128)(2,1)} %bitcast.431), channel_id=1, source_target_pairs={{0,8},{4,12},{8,0},{12,4},{16,24},{20,28},{24,16},{28,20},{1,9},{5... | collective-permute-start | bytes 1179656 | tf_op jit(solution)/shard_map/ppermute | solution.py:360
  429.2 14.2 %collective-permute-start.34 = (bf16[3,128,512]{2,1,0:T(8,128)(2,1)S(1)}, bf16[3,128,512]{2,1,0:T(8,128)(2,1)S(1)}, u32[]{:S(2)}, u32[]{:S(2)}) collective-permute-start(bf16[3,128,512]{2,1,0:T(8,128)(2,1)S(1)} %bitcast.430), channel_id=1, source_target_pairs={{0,16},{4,20},{8,24},{12,28},{16,0},{20,4},{24,8},{28,12},{1,17},{... | collective-permute-start | bytes 1179656 | tf_op jit(solution)/shard_map/ppermute | solution.py:360
  466.2 26.6 %collective-permute-start.30 = (bf16[128,1024]{1,0:T(8,128)(2,1)S(1)}, bf16[128,1024]{1,0:T(8,128)(2,1)S(1)}, u32[]{:S(2)}, u32[]{:S(2)}) collective-permute-start(bf16[128,1024]{1,0:T(8,128)(2,1)S(1)} %get-tuple-element.220.refs_7_), channel_id=1, source_target_pairs={{0,1},{1,2},{2,3},{3,0},{4,5},{5,6},{6,7},{7,4},{8,9},{9,10},{10,1... | collective-permute-start | bytes 786440 | tf_op jit(solution)/shard_map/ppermute | solution.py:1138
  468.0 15.2 %collective-permute-start.36 = (bf16[6,64,512]{2,1,0:T(8,128)(2,1)S(1)}, bf16[6,64,512]{2,1,0:T(8,128)(2,1)S(1)}, u32[]{:S(2)}, u32[]{:S(2)}) collective-permute-start(bf16[6,64,512]{2,1,0:T(8,128)(2,1)S(1)} %bitcast.429), channel_id=1, source_target_pairs={{0,1},{1,0},{2,3},{3,2},{4,5},{5,4},{6,7},{7,6},{8,9},{9,8},{10,11... | collective-permute-start | bytes 1179656 | tf_op jit(solution)/shard_map/ppermute | solution.py:360
  469.9 15.8 %collective-permute-start.37 = (bf16[2,256,512]{2,1,0:T(8,128)(2,1)S(1)}, bf16[2,256,512]{2,1,0:T(8,128)(2,1)S(1)}, u32[]{:S(2)}, u32[]{:S(2)}) collective-permute-start(bf16[2,256,512]{2,1,0:T(8,128)(2,1)S(1)} %bitcast.428), channel_id=1, source_target_pairs={{0,16},{4,20},{8,24},{12,28},{16,0},{20,4},{24,8},{28,12},{1,17},{... | collective-permute-start | bytes 1572872 | tf_op jit(solution)/shard_map/ppermute | solution.py:360
  471.6 14.3 %collective-permute-start.38 = (bf16[2,256,512]{2,1,0:T(8,128)(2,1)S(1)}, bf16[2,256,512]{2,1,0:T(8,128)(2,1)S(1)}, u32[]{:S(2)}, u32[]{:S(2)}) collective-permute-start(bf16[2,256,512]{2,1,0:T(8,128)(2,1)S(1)} %bitcast.427), channel_id=1, source_target_pairs={{0,8},{4,12},{8,0},{12,4},{16,24},{20,28},{24,16},{28,20},{1,9},{5... | collective-permute-start | bytes 1572872 | tf_op jit(solution)/shard_map/ppermute | solution.py:360
  479.0 23.7 %collective-permute-start.42 = (bf16[1,1536,256]{2,1,0:T(8,128)(2,1)S(1)}, bf16[1,1536,256]{2,1,0:T(8,128)(2,1)S(1)}, u32[]{:S(2)}, u32[]{:S(2)}) collective-permute-start(bf16[1,1536,256]{2,1,0:T(8,128)(2,1)S(1)} %get-tuple-element.320), channel_id=1, source_target_pairs={{0,4},{4,0},{8,12},{12,8},{16,20},{20,16},{24,28},{28,24},{1,5},{5... | collective-permute-start | bytes 2359304 | tf_op jit(solution)/shard_map/ppermute | solution.py:360
  486.8 15.9 %collective-permute-start.40 = (bf16[2,128,512]{2,1,0:T(8,128)(2,1)S(1)}, bf16[2,128,512]{2,1,0:T(8,128)(2,1)S(1)}, u32[]{:S(2)}, u32[]{:S(2)}) collective-permute-start(bf16[2,128,512]{2,1,0:T(8,128)(2,1)S(1)} %bitcast.434), channel_id=1, source_target_pairs={{0,8},{4,12},{8,0},{12,4},{16,24},{20,28},{24,16},{28,20},{1,9},{5... | collective-permute-start | bytes 786440 | tf_op jit(solution)/shard_map/ppermute | solution.py:360
  535.1 14.2 %collective-permute-start.52 = (bf16[3,128,512]{2,1,0:T(8,128)(2,1)S(1)}, bf16[3,128,512]{2,1,0:T(8,128)(2,1)S(1)}, u32[]{:S(2)}, u32[]{:S(2)}) collective-permute-start(bf16[3,128,512]{2,1,0:T(8,128)(2,1)S(1)} %bitcast.389), channel_id=1, source_target_pairs={{0,8},{4,12},{8,0},{12,4},{16,24},{20,28},{24,16},{28,20},{1,9},{5... | collective-permute-start | bytes 1179656 | tf_op jit(solution)/shard_map/ppermute | solution.py:360
  552.5 25.3 %collective-permute-start.57 = (bf16[3,256,512]{2,1,0:T(8,128)(2,1)S(1)}, bf16[3,256,512]{2,1,0:T(8,128)(2,1)S(1)}, u32[]{:S(2)}, u32[]{:S(2)}) collective-permute-start(bf16[3,256,512]{2,1,0:T(8,128)(2,1)S(1)} %bitcast.367), channel_id=1, source_target_pairs={{0,16},{4,20},{8,24},{12,28},{16,0},{20,4},{24,8},{28,12},{1,17},{... | collective-permute-start | bytes 2359304 | tf_op jit(solution)/shard_map/ppermute | solution.py:360
  552.6 25.2 %collective-permute-start.58 = (bf16[3,256,512]{2,1,0:T(8,128)(2,1)S(1)}, bf16[3,256,512]{2,1,0:T(8,128)(2,1)S(1)}, u32[]{:S(2)}, u32[]{:S(2)}) collective-permute-start(bf16[3,256,512]{2,1,0:T(8,128)(2,1)S(1)} %bitcast.368), channel_id=1, source_target_pairs={{0,8},{4,12},{8,0},{12,4},{16,24},{20,28},{24,16},{28,20},{1,9},{5... | collective-permute-start | bytes 2359304 | tf_op jit(solution)/shard_map/ppermute | solution.py:360
  554.1 23.6 %collective-permute-start.60 = (bf16[1,768,256]{2,1,0:T(8,128)(2,1)S(1)}, bf16[1,768,256]{2,1,0:T(8,128)(2,1)S(1)}, u32[]{:S(2)}, u32[]{:S(2)}) collective-permute-start(bf16[1,768,256]{2,1,0:T(8,128)(2,1)S(1)} %bitcast.386), channel_id=1, source_target_pairs={{0,16},{4,20},{8,24},{12,28},{16,0},{20,4},{24,8},{28,12},{1,17},{... | collective-permute-start | bytes 1179656 | tf_op jit(solution)/shard_map/ppermute | solution.py:360
  580.3 24.6 %collective-permute-start.67 = (bf16[6,512,512]{2,1,0:T(8,128)(2,1)}, bf16[6,512,512]{2,1,0:T(8,128)(2,1)}, u32[]{:S(2)}, u32[]{:S(2)}) collective-permute-start(bf16[6,512,512]{2,1,0:T(8,128)(2,1)} %bitcast.337), channel_id=1, source_target_pairs={{0,4},{4,0},{8,12},{12,8},{16,20},{20,16},{24,28},{28,24},{1,5},{5... | collective-permute-start | bytes 9437192 | tf_op jit(solution)/shard_map/ppermute | solution.py:360
  580.3 15.3 %collective-permute-start.64 = (bf16[1,1536,256]{2,1,0:T(8,128)(2,1)S(1)}, bf16[1,1536,256]{2,1,0:T(8,128)(2,1)S(1)}, u32[]{:S(2)}, u32[]{:S(2)}) collective-permute-start(bf16[1,1536,256]{2,1,0:T(8,128)(2,1)S(1)} %bitcast.372), channel_id=1, source_target_pairs={{0,4},{4,0},{8,12},{12,8},{16,20},{20,16},{24,28},{28,24},{1,5},{5... | collective-permute-start | bytes 2359304 | tf_op jit(solution)/shard_map/ppermute | solution.py:360
  580.8 14.7 %collective-permute-start.31 = (bf16[128,1024]{1,0:T(8,128)(2,1)S(1)}, bf16[128,1024]{1,0:T(8,128)(2,1)S(1)}, u32[]{:S(2)}, u32[]{:S(2)}) collective-permute-start(bf16[128,1024]{1,0:T(8,128)(2,1)S(1)} %copy-done.81), channel_id=1, source_target_pairs={{0,2},{1,3},{2,0},{3,1},{4,6},{5,7},{6,4},{7,5},{8,10},{9,11},{10,... | collective-permute-start | bytes 786440 | tf_op jit(solution)/shard_map/ppermute | solution.py:1138
  581.5 14.0 %collective-permute-start.62 = (bf16[2,128,512]{2,1,0:T(8,128)(2,1)S(1)}, bf16[2,128,512]{2,1,0:T(8,128)(2,1)S(1)}, u32[]{:S(2)}, u32[]{:S(2)}) collective-permute-start(bf16[2,128,512]{2,1,0:T(8,128)(2,1)S(1)} %bitcast.405), channel_id=1, source_target_pairs={{0,8},{4,12},{8,0},{12,4},{16,24},{20,28},{24,16},{28,20},{1,9},{5... | collective-permute-start | bytes 786440 | tf_op jit(solution)/shard_map/ppermute | solution.py:360
  597.1 14.9 %collective-permute-start.65 = (bf16[2,256,512]{2,1,0:T(8,128)(2,1)S(1)}, bf16[2,256,512]{2,1,0:T(8,128)(2,1)}, u32[]{:S(2)}, u32[]{:S(2)}) collective-permute-start(bf16[2,256,512]{2,1,0:T(8,128)(2,1)S(1)} %bitcast.375), channel_id=1, source_target_pairs={{0,16},{4,20},{8,24},{12,28},{16,0},{20,4},{24,8},{28,12},{1,17},{... | collective-permute-start | bytes 1572872 | tf_op jit(solution)/shard_map/ppermute | solution.py:360
  597.3 14.6 %collective-permute-start.66 = (bf16[2,256,512]{2,1,0:T(8,128)(2,1)}, bf16[2,256,512]{2,1,0:T(8,128)(2,1)}, u32[]{:S(2)}, u32[]{:S(2)}) collective-permute-start(bf16[2,256,512]{2,1,0:T(8,128)(2,1)} %bitcast.182), channel_id=1, source_target_pairs={{0,8},{4,12},{8,0},{12,4},{16,24},{20,28},{24,16},{28,20},{1,9},{5... | collective-permute-start | bytes 1572872 | tf_op jit(solution)/shard_map/ppermute | solution.py:360
  (167 other events, 1317.8 us)
Sparse Core Ops, SparseCore 0:
  131.5 77.7 all-gather.3
  260.9 49.4 reduce-scatter.4
  314.2 52.6 reduce-scatter.6
  369.1 27.1 reduce-scatter.8
  398.5 25.7 reduce-scatter.10
  428.4 28.9 all-gather.5
  459.8 32.7 all-gather.7
